TPU v7x, 128 devices: a whole 4x4x4 slice. The times are simulated.
128 devices in a mesh: query: 8 (over z, core), passage: 16 (over y, x).
Axes of the slice: x: 4, y: 4, z: 4, core: 2. Of those that a mesh axis runs over, the one named last changes fastest.
Arguments:
- queries: bfloat16 [32768, 4096], P(('query', 'passage')), may hold values from -24 to 24
- passages: bfloat16 [8192, 4096], P('passage', 'query'), may hold values from -24 to 24
- lists: int32 [256, 8], P(('query', 'passage')), may hold values from -1 to 31, as said below
- positive: int32 [32768], P(('query', 'passage')), may hold values from 0 to 8191, as said below
Outputs:
- loss: float32 [32768], P(('query', 'passage'))
Inputs may be any that keep to these rules, and one draw needn't show every extreme that they name: `lists`: each row holds distinct passage block ids in its first slots and -1 in the rest; at least 6 ids in every row, and row 0 fills all 8 slots; within each aligned group of 2 rows (the rows of one device) no two rows list blocks of the same owner, block id // 2. Query i's positive passage lies in block lists[i // 128, 0].
All inputs are finite; a program needn't handle non-finite values.
Results may differ from a plain program's by a relative error of at most 0.0003.
Values may be sent and summed in bfloat16 or wider, within the bound.
No kernel may reach another device: no remote copies, remote signals or barrier semaphores. Data moves between devices by JAX's collectives and lax.ppermute only.
A program may use at most 192 MiB of HBM per device.

v0:
```python
import jax
import jax.numpy as jnp
from jax import lax
from jax.sharding import PartitionSpec as P

QROWS = 128
PBLK = 256
PB_DEV = 2


def block_stats(scores, member, wanted, first_row):
    columns = jnp.repeat(member, PBLK, axis=1)
    masked = jnp.where(columns, scores, -jnp.inf)
    top = jnp.where(jnp.any(member, axis=1), jnp.max(masked, axis=1), -1e30)
    total = jnp.sum(jnp.where(columns, jnp.exp(scores - top[:, None]), 0.0), axis=1)
    index = first_row + jnp.arange(scores.shape[1], dtype=jnp.int32)
    chosen = jnp.sum(jnp.where(index[None, :] == wanted[:, None], scores, 0.0), axis=1)
    return (top, total, chosen)


def finish(top, total, chosen):
    peak = jnp.max(top, axis=0)
    summed = jnp.sum(total * jnp.exp(top - peak[None, :]), axis=0)
    return peak + jnp.log(summed) - jnp.sum(chosen, axis=0)


def body(queries, passages, lists, positive):
    full_pass = lax.all_gather(passages, "query", axis=1, tiled=True)
    scale = float(queries.shape[1]) ** (-0.5)
    owner = lax.axis_index("passage")
    first_block = owner * PB_DEV
    first_row = first_block * PBLK
    local_ids = first_block + jnp.arange(PB_DEV, dtype=jnp.int32)
    contract = (((1,), (1,)), ((), ()))
    blocks_here = lists.shape[0]
    all_rows, all_lists, all_wanted = (
        lax.all_gather(queries, "passage", axis=0, tiled=True),
        lax.all_gather(lists, "passage", axis=0, tiled=True),
        lax.all_gather(positive, "passage", axis=0, tiled=True),
    )
    member = jnp.any(all_lists[:, :, None] == local_ids[None, None, :], axis=1)
    count = lax.axis_size("passage")
    scores = (
        lax.dot_general(all_rows, full_pass, contract, preferred_element_type=jnp.float32) * scale
    )
    top, total, chosen = block_stats(
        scores, jnp.repeat(member, QROWS, axis=0), all_wanted, first_row
    )
    top = top.reshape(count, blocks_here * QROWS)
    total = total.reshape(count, blocks_here * QROWS)
    chosen = chosen.reshape(count, blocks_here * QROWS)
    top, total, chosen = (
        lax.all_to_all(top, "passage", split_axis=0, concat_axis=0, tiled=True),
        lax.all_to_all(total, "passage", split_axis=0, concat_axis=0, tiled=True),
        lax.all_to_all(chosen, "passage", split_axis=0, concat_axis=0, tiled=True),
    )
    return finish(top, total, chosen)


def solution(mesh):
    return jax.shard_map(
        body,
        mesh=mesh,
        in_specs=(
            P(("query", "passage"), None),
            P("passage", "query"),
            P(("query", "passage"), None),
            P(("query", "passage")),
        ),
        out_specs=P(("query", "passage")),
        check_vma=False,
    )
```

profile of v0, /device:TPU:0, one launch (start us, length us, event | category | flops | bytes accessed | tf_op | source)
XLA Modules:
  0.0 311.6 jit_solution(3864102794292578159)
XLA Ops:
  6.5 0.0 all-gather.7.cloned.1.call-start
  6.5 0.7 all-gather.7.cloned.1.call-update
  7.3 0.0 all-gather.5.cloned.1.call-start
  7.3 0.7 all-gather.5.cloned.1.call-update
  8.0 23.7 %all-gather = s32[16,2,8]{2,1,0:T(2,128)S(1)} all-gather(s32[1,2,8]{2,1,0:T(2,128)} %bitcast.38), channel_id=1, replica_groups=mesh['query'=8,'passage'=16] {'passage'}, dimensions={0}, use_global_device_ids=true | all-gather | bytes 1088 | tf_op jit(solution)/shard_map/all_gather | solution.py:38
  31.7 0.1 copy.8
  31.8 0.1 compare_reduce_fusion
  31.9 0.1 broadcast_bitcast_fusion
  32.0 0.1 reduce_or.29
  32.1 0.1 reduce_or.30
  32.2 22.6 %all-gather.1 = s32[16,1,256]{2,1,0:T(1,128)S(1)} all-gather(s32[1,1,256]{2,1,0:T(1,128)} %bitcast.39), channel_id=1, replica_groups=mesh['query'=8,'passage'=16] {'passage'}, dimensions={0}, use_global_device_ids=true | all-gather | bytes 17408 | tf_op jit(solution)/shard_map/all_gather | solution.py:39
  54.8 0.0 all-gather.7.cloned.1.call-done
  54.8 188.0 %all-gather.5.cloned.1.call-done = bf16[4096,4096]{1,0:T(8,128)(2,1)} async-done(((bf16[256,4096]{1,0:T(8,128)(2,1)}), bf16[4096,4096]{1,0:T(8,128)(2,1)}) %all-gather.5.cloned.1.call-update) | async-done | bytes 33554448 | tf_op jit(solution)/shard_map/all_gather | solution.py:37
  242.8 24.0 %fusion = (f32[4096]{0:T(1024)S(1)}, f32[4096,512]{0,1:T(8,128)}) fusion(pred[4096,2]{0,1:T(4,128)(4,1)S(1)} %bitcast.34, bf16[4096,4096]{1,0:T(8,128)(2,1)} %all-gather.5.cloned.1.call-done, bf16[512,4096]{1,0:T(8,128)(2,1)} %all-gather.7.cloned.1.call-done), kind=kOutput, calls=%fused_computation.2 | convolution fusion | flops 17186156544 | bytes 46161920 | tf_op jit(solution)/shard_map/dot_general | solution.py:44
  266.8 0.6 copy.9
  267.5 5.3 %all-to-all-start = ((f32[16,1,256]{2,1,0:T(1,128)}), f32[16,1,256]{2,1,0:T(1,128)S(1)}, u32[]{:S(2)}, u32[]{:S(2)}) async-start(f32[16,1,256]{2,1,0:T(1,128)} %copy.9), calls=%async_computation | async-start | bytes 32768 | tf_op jit(solution)/shard_map/all_to_all | solution.py:53
  272.8 0.1 bitcast_select_fusion.2
  272.8 5.5 %fusion.1 = (f32[4096]{0:T(1024)}, f32[4096]{0:T(1024)}) fusion(f32[4096,512]{0,1:T(8,128)} %get-tuple-element.10, f32[4096]{0:T(1024)S(1)} %bitcast_select_fusion.2, pred[4096,2]{0,1:T(4,128)(4,1)S(1)} %bitcast.35, s32[4096]{0:T(1024)S(1)} %bitcast.36, s32[512]{0:T(512)S(1)} %iota_add_fusion), kind=kLoop, calls=%fused_computation.3 | loop fusion | flops 14671872 | bytes 8464384 | tf_op jit(solution)/shard_map/reduce_sum | solution.py:15
  278.4 2.0 all-to-all-done
  280.3 5.2 %all-to-all-start.1 = ((f32[16,1,256]{2,1,0:T(1,128)}), f32[16,1,256]{2,1,0:T(1,128)S(1)}, u32[]{:S(2)}, u32[]{:S(2)}) async-start(f32[16,1,256]{2,1,0:T(1,128)} %bitcast.4), calls=%async_computation.1 | async-start | bytes 32768 | tf_op jit(solution)/shard_map/all_to_all | solution.py:54
  285.6 7.5 %all-to-all-done.1 = f32[16,1,256]{2,1,0:T(1,128)S(1)} async-done(((f32[16,1,256]{2,1,0:T(1,128)}), f32[16,1,256]{2,1,0:T(1,128)S(1)}, u32[]{:S(2)}, u32[]{:S(2)}) %all-to-all-start.1) | async-done | bytes 16416 | tf_op jit(solution)/shard_map/all_to_all | solution.py:54
  293.2 3.5 %all-to-all-start.2 = ((f32[16,1,256]{2,1,0:T(1,128)}), f32[16,1,256]{2,1,0:T(1,128)S(1)}, u32[]{:S(2)}, u32[]{:S(2)}) async-start(f32[16,1,256]{2,1,0:T(1,128)} %bitcast.7), calls=%async_computation.2 | async-start | bytes 32768 | tf_op jit(solution)/shard_map/all_to_all | solution.py:55
  296.7 7.5 %all-to-all-done.2 = f32[16,1,256]{2,1,0:T(1,128)S(1)} async-done(((f32[16,1,256]{2,1,0:T(1,128)}), f32[16,1,256]{2,1,0:T(1,128)S(1)}, u32[]{:S(2)}, u32[]{:S(2)}) %all-to-all-start.2) | async-done | bytes 16416 | tf_op jit(solution)/shard_map/all_to_all | solution.py:55
  304.2 0.6 add_subtract_fusion
  (9 shorter events, 0.2 us)
Async XLA Ops:
  6.5 48.3 %all-gather.7.cloned.1.call-start = ((), (), s32[]{:S(2)}) async-start(), calls=%async_computation.4 | async-start | bytes 4718592 | tf_op jit(solution)/shard_map/all_gather | solution.py:28
  7.3 235.5 %all-gather.5.cloned.1.call-start = ((), (), s32[]{:S(2)}) async-start(), calls=%async_computation.3 | async-start | bytes 35651584 | tf_op jit(solution)/shard_map/all_gather | solution.py:37
  267.5 12.9 %all-to-all-start = ((f32[16,1,256]{2,1,0:T(1,128)}), f32[16,1,256]{2,1,0:T(1,128)S(1)}, u32[]{:S(2)}, u32[]{:S(2)}) async-start(f32[16,1,256]{2,1,0:T(1,128)} %copy.9), calls=%async_computation | async-start | bytes 32768 | tf_op jit(solution)/shard_map/all_to_all | solution.py:53
  280.3 12.8 %all-to-all-start.1 = ((f32[16,1,256]{2,1,0:T(1,128)}), f32[16,1,256]{2,1,0:T(1,128)S(1)}, u32[]{:S(2)}, u32[]{:S(2)}) async-start(f32[16,1,256]{2,1,0:T(1,128)} %bitcast.4), calls=%async_computation.1 | async-start | bytes 32768 | tf_op jit(solution)/shard_map/all_to_all | solution.py:54
  293.2 11.0 %all-to-all-start.2 = ((f32[16,1,256]{2,1,0:T(1,128)}), f32[16,1,256]{2,1,0:T(1,128)S(1)}, u32[]{:S(2)}, u32[]{:S(2)}) async-start(f32[16,1,256]{2,1,0:T(1,128)} %bitcast.7), calls=%async_computation.2 | async-start | bytes 32768 | tf_op jit(solution)/shard_map/all_to_all | solution.py:55
Sparse Core Ops, SparseCore 0:
  9.0 34.7 all-gather.6
  46.0 196.7 all-gather.4
where the time goes:
time: 312 us
  waiting for transfers between devices  206 us (66%)
  blocking collectives  46.3 us (15%)
  matrix products  24 us (8%)
  starting transfers between devices  14 us (4%)
  between operations  13.5 us (4%)
  other arithmetic  6.38 us (2%)
    all_gather x1, waiting for transfers between devices, body(): lax.all_gather(queries, 'passage', axis=0, tiled=True)  188 us
    dot_general x1, matrix products, body(): lax.dot_general(all_rows, full_pass, contract, preferred_element_type=jnp...  24 us
    all_gather x1, blocking collectives, body(): lax.all_gather(lists, 'passage', axis=0, tiled=True)  23.7 us
    all_gather x1, blocking collectives, body(): lax.all_gather(positive, 'passage', axis=0, tiled=True)  22.6 us
    all_to_all x1, waiting for transfers between devices, body(): lax.all_to_all(total, 'passage', split_axis=0, concat_axis=0, tiled=True)  7.55 us
    all_to_all x1, waiting for transfers between devices, body(): lax.all_to_all(chosen, 'passage', split_axis=0, concat_axis=0, tiled=True)  7.49 us
  transfers between devices with their start and end apart: 5, of which 4 were waited for; matrix products, arithmetic and copies ran while one was open for 2% of the time, Pallas kernels for 0%

commit v1 on v0

v1 whole, which is shorter than its diff:
```python
import functools

import jax
import jax.numpy as jnp
from jax import lax
from jax.experimental import pallas as pl
from jax.experimental.pallas import tpu as pltpu
from jax.sharding import Mesh
from jax.sharding import PartitionSpec as P

QROWS = 128
PBLK = 256
RING = 4
AXES = ("z", "core", "y", "x")
REL = (0, -1, 1, 2)


def ring(axis, step):
    return [(i, (i + step) % RING) for i in range(RING)]


def shift(array, axis, step):
    return lax.ppermute(array, axis, ring(axis, step))


def device(z, core, y, x):
    return ((z * 2 + core) * RING + y) * RING + x


def shift_zy(array, first, step):
    pairs = []
    for z in range(RING):
        for core in range(2):
            for y in range(RING):
                for x in range(RING):
                    along_z = (core == 0) == first
                    to_z = (z + step) % RING if along_z else z
                    to_y = y if along_z else (y + step) % RING
                    pairs.append((device(z, core, y, x), device(to_z, core, to_y, x)))
    return lax.ppermute(array, AXES, pairs)


def swap(array):
    return lax.ppermute(array, "core", [(0, 1), (1, 0)])


def score_kernel(parts, groups, scale, has_init, info, *refs):
    refs = list(refs)
    meta = refs.pop(0)
    init = refs.pop(0) if has_init else None
    queries = [[refs.pop(0) for _ in rows] for rows in parts]
    pieces = [[refs.pop(0) for _ in range(5)] for _ in groups]
    out, q_buf, p_buf, q_sem, p_sem = refs
    me_z, me_core, me_y, me_x = (info[k] for k in range(4))
    feats = q_buf.shape[2] // 8

    def turn(value, step):
        return lax.rem(value + step + RING, RING)

    def load_queries(s):
        for n, (ref, rows) in enumerate(zip(queries[s], parts[s])):
            start, size = rows
            pltpu.make_async_copy(ref, q_buf.at[s, pl.ds(start, size)], q_sem.at[s]).start()

    def load_slot(g, k, source):
        for m in range(RING):
            i, j = (k, m) if source == 0 else (m, k)
            ref, at = (pieces[g][i], j) if i < 3 else (pieces[g][3 + j // 2], j % 2)
            zsrc = turn(me_z, REL[m])
            for c in range(2):
                column = pl.multiple_of((zsrc * 2 + (source ^ c)) * feats, feats)
                pltpu.make_async_copy(
                    ref.at[at, c],
                    p_buf.at[g * RING + k, :, pl.ds(column, feats)],
                    p_sem.at[g * RING + k],
                ).start()

    def load_group(g, ks):
        for source in range(2):
            @pl.when((me_core + groups[g]) % 2 == source)
            def _():
                for k in ks:
                    load_slot(g, k, source)

    load_queries(0)
    load_group(0, (0,))
    for s in range(1, len(parts)):
        load_queries(s)
    load_group(0, (1, 2, 3))
    for g in range(1, len(groups)):
        load_group(g, (0, 1, 2, 3))

    if has_init:
        out[...] = init[...]
    else:
        rows = lax.broadcasted_iota(jnp.int32, out.shape, 1)
        out[...] = jnp.where(rows == 0, -1e30, 0.0).astype(jnp.float32)

    def block(k, s):
        source = lax.rem(me_core + (groups[0] if len(groups) == 1 else k // RING), 2)
        rel = lax.rem(k, RING)
        offset = jnp.where(rel == 3, 2, jnp.where(rel == 1, -1, rel // 2))
        block_id = (turn(me_y, offset) * RING + me_x) * 2 + source
        scores = lax.dot_general(
            p_buf[k], q_buf[s], (((1,), (1,)), ((), ())), preferred_element_type=jnp.float32
        ) * scale
        listed = jnp.max((meta[s, 0:8, :] == block_id).astype(jnp.int32), axis=0, keepdims=True) > 0
        wanted = meta[s, 8:9, :] - block_id * PBLK
        top, total, chosen = out[s, 0:1, :], out[s, 1:2, :], out[s, 2:3, :]
        new_top = jnp.where(listed, jnp.maximum(top, jnp.max(scores, axis=0, keepdims=True)), top)
        here = jnp.sum(jnp.exp(scores - new_top), axis=0, keepdims=True)
        index = lax.broadcasted_iota(jnp.int32, scores.shape, 0)
        hit = jnp.sum(jnp.where(index == wanted, scores, 0.0), axis=0, keepdims=True)
        out[s, 0:1, :] = new_top
        out[s, 1:2, :] = total * jnp.exp(top - new_top) + jnp.where(listed, here, 0.0)
        out[s, 2:3, :] = chosen + hit

    def whole(ref, sem):
        pltpu.make_async_copy(ref, ref, sem).wait()

    @pl.loop(0, len(groups) * RING)
    def _(k):
        whole(p_buf.at[k], p_sem.at[k])

        @pl.loop(0, len(parts))
        def _(s):
            @pl.when(k == 0)
            def _():
                whole(q_buf.at[s], q_sem.at[s])

            block(k, s)


def score(info, meta, queries, pieces, groups, init=None):
    features = queries[0][0].shape[1]
    parts = []
    for arrays in queries:
        start, rows = 0, []
        for a in arrays:
            rows.append((start, a.shape[0]))
            start += a.shape[0]
        parts.append(tuple(rows))
    count, blocks = len(parts), len(groups) * RING
    size = 2 * QROWS
    flat = [a for arrays in queries for a in arrays] + [a for arrays in pieces for a in arrays]
    vmem = pl.BlockSpec(memory_space=pltpu.VMEM)
    shape = (count, 3, size)
    head = [meta] + ([init] if init is not None else [])
    kernel = functools.partial(
        score_kernel, tuple(parts), groups, float(features) ** -0.5, init is not None
    )
    return pl.pallas_call(
        kernel,
        out_shape=jax.ShapeDtypeStruct(shape, jnp.float32),
        in_specs=[pl.BlockSpec(memory_space=pltpu.SMEM)]
        + [vmem] * len(head)
        + [pl.BlockSpec(memory_space=pl.ANY)] * len(flat),
        out_specs=vmem,
        scratch_shapes=[
            pltpu.VMEM((count, size, features), jnp.bfloat16),
            pltpu.VMEM((blocks, PBLK, features), jnp.bfloat16),
            pltpu.SemaphoreType.DMA((count,)),
            pltpu.SemaphoreType.DMA((blocks,)),
        ],
        compiler_params=pltpu.CompilerParams(vmem_limit_bytes=32 * 1024 * 1024),
        cost_estimate=pl.CostEstimate(
            flops=2 * count * size * blocks * PBLK * features,
            bytes_accessed=(count * size + blocks * PBLK) * features * 2,
            transcendentals=count * size * blocks * PBLK,
        ),
    )(info, *head, *flat)


def finish(stats):
    top, total, chosen = stats[:, 0], stats[:, 1], stats[:, 2]
    peak = jnp.max(top, axis=0)
    summed = jnp.sum(total * jnp.exp(top - peak[None, :]), axis=0)
    return peak + jnp.log(summed) - jnp.sum(chosen, axis=0)


def body(queries, passages, lists, positive):
    info = jnp.stack([lax.axis_index(a) for a in AXES]).astype(jnp.int32)
    core = lax.axis_index("core")
    half = QROWS

    meta = jnp.concatenate([jnp.repeat(lists.T, QROWS, axis=1), positive[None, :]], axis=0)
    top, bottom = queries[:half], queries[half:]
    r0, l1 = shift(top, "x", 1), shift(bottom, "x", -1)
    r1, l0 = shift(bottom, "x", 1), shift(top, "x", -1)
    f0, f1 = shift(r0, "x", 1), shift(l1, "x", -1)
    meta_r, meta_l, meta_f = shift(meta, "x", 1), shift(meta, "x", -1), shift(meta, "x", 2)

    blocks = passages.reshape(2, PBLK, passages.shape[1])
    mine = lax.dynamic_index_in_dim(blocks, core, 0, keepdims=False)
    other = lax.dynamic_index_in_dim(blocks, 1 - core, 0, keepdims=False)
    piece = jnp.stack([mine, swap(other)])
    s = jnp.stack(
        [piece, shift_zy(piece, True, 1), shift_zy(piece, True, -1), shift_zy(piece, True, 2)]
    )
    pr, pl_ = shift_zy(s, False, 1), shift_zy(s, False, -1)
    fr, fl = shift_zy(pr[:2], False, 1), shift_zy(pl_[2:], False, -1)
    own = [s, pr, pl_, fr, fl]
    theirs = [swap(a) for a in own]

    near = [[queries], [r0, r1], [l0, l1]]
    metas = jnp.stack([meta, meta_r, meta_l])
    stats = score(info, metas, near, [own], (0,))
    stats = score(info, metas, near, [theirs], (1,), stats)
    far = score(info, meta_f[None], [[f0, f1]], [own, theirs], (0, 1))
    back = [
        stats[0],
        shift(stats[1], "x", -1),
        shift(stats[2], "x", 1),
        shift(far[0], "x", 2),
    ]
    return finish(jnp.stack(back))


def solution(mesh):
    fine = Mesh(mesh.devices.reshape(RING, 2, RING, RING), AXES)
    everywhere = ("z", "core", "y", "x")
    return jax.shard_map(
        body,
        mesh=fine,
        in_specs=(
            P(everywhere, None),
            P(("y", "x"), ("z", "core")),
            P(everywhere, None),
            P(everywhere),
        ),
        out_specs=P(everywhere),
        check_vma=False,
    )
```

time: 312 us -> 154 us (0.49)
  waiting for transfers between devices: 206 us -> 74.8 us
  blocking collectives: 46.3 us -> 0 us
  Pallas kernels: 0 us -> 31.5 us
  matrix products: 24 us -> 0 us
  starting transfers between devices: 14 us -> 32.3 us
  between operations: 13.5 us -> 0.25 us
  local copies, waits for them, and re-layouts: 1 us -> 12.4 us
  other arithmetic: 6.38 us -> 1.05 us
    all_gather x2 -> x0, waiting for transfers between devices: 188 us -> none  [the longest x1 188 us: body(): lax.all_gather(queries, 'passage', axis=0, tiled=True)]
    ppermute x0 -> x25, waiting for transfers between devices: none -> 74.8 us  [the longest x12 55.1 us: shift(): return lax.ppermute(array, axis, ring(axis, step))]
    all_gather x2 -> x0, blocking collectives: 46.3 us -> none  [the longest x1 23.7 us: body(): lax.all_gather(lists, 'passage', axis=0, tiled=True)]
    ppermute x0 -> x25, starting transfers between devices: none -> 32.3 us  [the longest x12 18.5 us: shift(): return lax.ppermute(array, axis, ring(axis, step))]
    pallas_call x0 -> x3, Pallas kernels: none -> 31.5 us  [score(): pl.pallas_call(kernel, out_shape=jax.ShapeDtypeStruct(shape, jnp.float32)...]
    dot_general x1 -> x0, matrix products: 24 us -> none  [body(): lax.dot_general(all_rows, full_pass, contract, preferred_element_type=jnp...]
    all_to_all x3 -> x0, waiting for transfers between devices: 17 us -> none  [the longest x1 7.55 us: body(): lax.all_to_all(total, 'passage', split_axis=0, concat_axis=0, tiled=True)]
    all_to_all x3 -> x0, starting transfers between devices: 14 us -> none  [the longest x1 5.29 us: body(): lax.all_to_all(top, 'passage', split_axis=0, concat_axis=0, tiled=True)]
  transfers between devices with their start and end apart: 5 -> 25, of which waited for: 4 -> 9; matrix products, arithmetic and copies ran while one was open for 2% -> 2% of each run, Pallas kernels for 0% -> 21%
where the time goes in v1:
time: 154 us; the launch traced here: 152 us
  waiting for transfers between devices  74.8 us (49%)
  starting transfers between devices  32.3 us (21%)
  Pallas kernels  31.5 us (20%)
  local copies, waits for them, and re-layouts  12.4 us (8%)
    ppermute x12, waiting for transfers between devices, shift(): return lax.ppermute(array, axis, ring(axis, step))  55.1 us
    pallas_call x3, Pallas kernels, score(): pl.pallas_call(kernel, out_shape=jax.ShapeDtypeStruct(shape, jnp.float32)...  31.5 us
    ppermute x12, starting transfers between devices, shift(): return lax.ppermute(array, axis, ring(axis, step))  18.5 us
    ppermute x7, starting transfers between devices, shift_zy(): return lax.ppermute(array, AXES, pairs)  13 us
    ppermute x7, waiting for transfers between devices, shift_zy(): return lax.ppermute(array, AXES, pairs)  12.4 us
    unnamed x34, local copies, waits for them, and re-layouts  8.48 us
    ppermute x6, waiting for transfers between devices, swap(): return lax.ppermute(array, 'core', [(0, 1), (1, 0)])  7.38 us
  transfers between devices with their start and end apart: 25, of which 9 were waited for; matrix products, arithmetic and copies ran while one was open for 2% of the time, Pallas kernels for 21%

profile of v1, /device:TPU:0, one launch (start us, length us, event | category | flops | bytes accessed | tf_op | source)
XLA Modules:
  0.0 152.3 jit_solution(10193744089161649563)
XLA Ops:
  1.2 1.5 collective-permute-done.6
  2.8 2.1 %collective-permute-start.7 = (bf16[2,256,512]{2,1,0:T(8,128)(2,1)S(1)}, bf16[2,256,512]{2,1,0:T(8,128)(2,1)S(1)}, u32[]{:S(2)}, u32[]{:S(2)}) collective-permute-start(bf16[2,256,512]{2,1,0:T(8,128)(2,1)S(1)} %get-tuple-element.10), channel_id=1, source_target_pairs={{0,32},{1,33},{2,34},{3,35},{4,36},{5,37},{6,38},{7,39},{8,40},{9,... | collective-permute-start | bytes 1572872 | tf_op jit(solution)/shard_map/ppermute | solution.py:40
  4.8 2.2 %collective-permute-start.8 = (bf16[2,256,512]{2,1,0:T(8,128)(2,1)S(1)}, bf16[2,256,512]{2,1,0:T(8,128)(2,1)S(1)}, u32[]{:S(2)}, u32[]{:S(2)}) collective-permute-start(bf16[2,256,512]{2,1,0:T(8,128)(2,1)S(1)} %get-tuple-element.10), channel_id=1, source_target_pairs={{0,96},{1,97},{2,98},{3,99},{4,100},{5,101},{6,102},{7,103},{8,104... | collective-permute-start | bytes 1572872 | tf_op jit(solution)/shard_map/ppermute | solution.py:40
  7.0 1.8 %collective-permute-start.9 = (bf16[2,256,512]{2,1,0:T(8,128)(2,1)S(1)}, bf16[2,256,512]{2,1,0:T(8,128)(2,1)S(1)}, u32[]{:S(2)}, u32[]{:S(2)}) collective-permute-start(bf16[2,256,512]{2,1,0:T(8,128)(2,1)S(1)} %get-tuple-element.10), channel_id=1, source_target_pairs={{0,64},{1,65},{2,66},{3,67},{4,68},{5,69},{6,70},{7,71},{8,72},{9,... | collective-permute-start | bytes 1572872 | tf_op jit(solution)/shard_map/ppermute | solution.py:40
  8.8 5.3 %collective-permute-done.7 = bf16[2,256,512]{2,1,0:T(8,128)(2,1)S(1)} collective-permute-done((bf16[2,256,512]{2,1,0:T(8,128)(2,1)S(1)}, bf16[2,256,512]{2,1,0:T(8,128)(2,1)S(1)}, u32[]{:S(2)}, u32[]{:S(2)}) %collective-permute-start.7) | collective-permute-done | bytes 524320 | tf_op jit(solution)/shard_map/ppermute | solution.py:40
  14.1 5.3 %collective-permute-done.8 = bf16[2,256,512]{2,1,0:T(8,128)(2,1)S(1)} collective-permute-done((bf16[2,256,512]{2,1,0:T(8,128)(2,1)S(1)}, bf16[2,256,512]{2,1,0:T(8,128)(2,1)S(1)}, u32[]{:S(2)}, u32[]{:S(2)}) %collective-permute-start.8) | collective-permute-done | bytes 524320 | tf_op jit(solution)/shard_map/ppermute | solution.py:40
  19.4 1.8 %collective-permute-done.9 = bf16[2,256,512]{2,1,0:T(8,128)(2,1)S(1)} collective-permute-done((bf16[2,256,512]{2,1,0:T(8,128)(2,1)S(1)}, bf16[2,256,512]{2,1,0:T(8,128)(2,1)S(1)}, u32[]{:S(2)}, u32[]{:S(2)}) %collective-permute-start.9) | collective-permute-done | bytes 524320 | tf_op jit(solution)/shard_map/ppermute | solution.py:40
  21.5 1.6 %collective-permute-start.10 = (bf16[4,2,256,512]{3,2,1,0:T(8,128)(2,1)S(1)}, bf16[4,2,256,512]{3,2,1,0:T(8,128)(2,1)}, u32[]{:S(2)}, u32[]{:S(2)}) collective-permute-start(bf16[4,2,256,512]{3,2,1,0:T(8,128)(2,1)S(1)} %pad_maximum_fusion.refs_6_.refs_3_), channel_id=1, source_target_pairs={{0,4},{1,5},{2,6},{3,7},{4,8},{5,9},{6,10},{7,11},{8,12},{9,13},{1... | collective-permute-start | bytes 6291464 | tf_op jit(solution)/shard_map/ppermute | solution.py:40
  23.1 1.7 %collective-permute-start.11 = (bf16[4,2,256,512]{3,2,1,0:T(8,128)(2,1)S(1)}, bf16[4,2,256,512]{3,2,1,0:T(8,128)(2,1)}, u32[]{:S(2)}, u32[]{:S(2)}) collective-permute-start(bf16[4,2,256,512]{3,2,1,0:T(8,128)(2,1)S(1)} %pad_maximum_fusion.refs_6_.refs_3_), channel_id=1, source_target_pairs={{0,12},{1,13},{2,14},{3,15},{4,0},{5,1},{6,2},{7,3},{8,4},{9,5},{1... | collective-permute-start | bytes 6291464 | tf_op jit(solution)/shard_map/ppermute | solution.py:40
  25.0 1.6 %collective-permute-start.2 = (bf16[128,4096]{1,0:T(8,128)(2,1)S(1)}, bf16[128,4096]{1,0:T(8,128)(2,1)S(1)}, u32[]{:S(2)}, u32[]{:S(2)}) collective-permute-start(bf16[128,4096]{1,0:T(8,128)(2,1)S(1)} %get-tuple-element.8), channel_id=1, source_target_pairs={{0,1},{1,2},{2,3},{3,0},{4,5},{5,6},{6,7},{7,4},{8,9},{9,10},{10,1... | collective-permute-start | bytes 3145736 | tf_op jit(solution)/shard_map/ppermute | solution.py:23
  26.6 1.6 %collective-permute-start = (s32[9,256]{1,0:T(8,128)S(1)}, s32[9,256]{1,0:T(8,128)S(1)}, u32[]{:S(2)}, u32[]{:S(2)}) collective-permute-start(s32[9,256]{1,0:T(8,128)S(1)} %get-tuple-element.19), channel_id=1, source_target_pairs={{0,1},{1,2},{2,3},{3,0},{4,5},{5,6},{6,7},{7,4},{8,9},{9,10},{10,1... | collective-permute-start | bytes 27656 | tf_op jit(solution)/shard_map/ppermute | solution.py:23
  28.2 1.7 %collective-permute-start.1 = (s32[9,256]{1,0:T(8,128)S(1)}, s32[9,256]{1,0:T(8,128)S(1)}, u32[]{:S(2)}, u32[]{:S(2)}) collective-permute-start(s32[9,256]{1,0:T(8,128)S(1)} %get-tuple-element.19), channel_id=1, source_target_pairs={{0,3},{1,0},{2,1},{3,2},{4,7},{5,4},{6,5},{7,6},{8,11},{9,8},{10,9... | collective-permute-start | bytes 27656 | tf_op jit(solution)/shard_map/ppermute | solution.py:23
  30.0 20.3 %collective-permute-done = s32[9,256]{1,0:T(8,128)S(1)} collective-permute-done((s32[9,256]{1,0:T(8,128)S(1)}, s32[9,256]{1,0:T(8,128)S(1)}, u32[]{:S(2)}, u32[]{:S(2)}) %collective-permute-start) | collective-permute-done | bytes 9248 | tf_op jit(solution)/shard_map/ppermute | solution.py:23
  50.3 1.5 %collective-permute-start.5 = (bf16[128,4096]{1,0:T(8,128)(2,1)S(1)}, bf16[128,4096]{1,0:T(8,128)(2,1)S(1)}, u32[]{:S(2)}, u32[]{:S(2)}) collective-permute-start(bf16[128,4096]{1,0:T(8,128)(2,1)S(1)} %get-tuple-element.7), channel_id=1, source_target_pairs={{0,3},{1,0},{2,1},{3,2},{4,7},{5,4},{6,5},{7,6},{8,11},{9,8},{10,9... | collective-permute-start | bytes 3145736 | tf_op jit(solution)/shard_map/ppermute | solution.py:23
  52.3 2.8 %collective-permute-start.4 = (bf16[128,4096]{1,0:T(8,128)(2,1)S(1)}, bf16[128,4096]{1,0:T(8,128)(2,1)S(1)}, u32[]{:S(2)}, u32[]{:S(2)}) collective-permute-start(bf16[128,4096]{1,0:T(8,128)(2,1)S(1)} %get-tuple-element.8), channel_id=1, source_target_pairs={{0,3},{1,0},{2,1},{3,2},{4,7},{5,4},{6,5},{7,6},{8,11},{9,8},{10,9... | collective-permute-start | bytes 3145736 | tf_op jit(solution)/shard_map/ppermute | solution.py:23
  55.1 1.3 slice.40
  56.5 1.5 collective-permute-start.12
  58.0 1.3 slice.41
  59.3 17.1 %collective-permute-done.5.refs_5_.refs_6_ = bf16[128,4096]{1,0:T(8,128)(2,1)S(1)} collective-permute-done((bf16[128,4096]{1,0:T(8,128)(2,1)S(1)}, bf16[128,4096]{1,0:T(8,128)(2,1)S(1)}, u32[]{:S(2)}, u32[]{:S(2)}) %collective-permute-start.5) | collective-permute-done | bytes 1048608 | tf_op jit(solution)/shard_map/ppermute | solution.py:23
  76.4 2.2 %collective-permute-start.13 = (bf16[2,2,256,512]{3,2,1,0:T(8,128)(2,1)S(1)}, bf16[2,2,256,512]{3,2,1,0:T(8,128)(2,1)}, u32[]{:S(2)}, u32[]{:S(2)}) collective-permute-start(bf16[2,2,256,512]{3,2,1,0:T(8,128)(2,1)S(1)} %slice.41), channel_id=1, source_target_pairs={{0,12},{1,13},{2,14},{3,15},{4,0},{5,1},{6,2},{7,3},{8,4},{9,5},{1... | collective-permute-start | bytes 3145736 | tf_op jit(solution)/shard_map/ppermute | solution.py:40
  79.5 16.1 %collective-permute-done.4.refs_4_.refs_5_ = bf16[128,4096]{1,0:T(8,128)(2,1)S(1)} collective-permute-done((bf16[128,4096]{1,0:T(8,128)(2,1)S(1)}, bf16[128,4096]{1,0:T(8,128)(2,1)S(1)}, u32[]{:S(2)}, u32[]{:S(2)}) %collective-permute-start.4) | collective-permute-done | bytes 1048608 | tf_op jit(solution)/shard_map/ppermute | solution.py:23
  97.6 5.9 %collective-permute-done.17.refs_10_.refs_11_ = bf16[2,2,256,512]{3,2,1,0:T(8,128)(2,1)} collective-permute-done((bf16[2,2,256,512]{3,2,1,0:T(8,128)(2,1)S(1)}, bf16[2,2,256,512]{3,2,1,0:T(8,128)(2,1)}, u32[]{:S(2)}, u32[]{:S(2)}) %collective-permute-start.17) | collective-permute-done | bytes 1048608 | tf_op jit(solution)/shard_map/ppermute | solution.py:44
  103.5 2.8 %collective-permute-start.23 = (bf16[128,4096]{1,0:T(8,128)(2,1)}, bf16[128,4096]{1,0:T(8,128)(2,1)S(1)}, u32[]{:S(2)}, u32[]{:S(2)}) collective-permute-start(bf16[128,4096]{1,0:T(8,128)(2,1)} %copy-done.7), channel_id=1, source_target_pairs={{0,3},{1,0},{2,1},{3,2},{4,7},{5,4},{6,5},{7,6},{8,11},{9,8},{10,9... | collective-permute-start | bytes 3145736 | tf_op jit(solution)/shard_map/ppermute | solution.py:23
  106.2 1.6 %copy-done.2 = bf16[256,4096]{1,0:T(8,128)(2,1)S(1)} copy-done((bf16[256,4096]{1,0:T(8,128)(2,1)S(1)}, bf16[256,4096]{1,0:T(8,128)(2,1)}, u32[]{:S(2)}) %copy-start.2) | copy-done | bytes 2097176
  109.0 1.2 copy-done.8
  110.3 1.2 copy-done.11
  112.7 11.2 %shard_map.46.refs_1_ = f32[3,3,256]{2,1,0:T(4,128)S(1)} custom-call(s32[4]{0:T(128)S(1)} %pad_add_fusion.2.info, s32[3,9,256]{2,1,0:T(8,128)S(1)} %pad_add_fusion.refs_0_, bf16[256,4096]{1,0:T(8,128)(2,1)S(1)} %copy-done.2, bf16[128,4096]{1,0:T(8,128)(2,1)S(1)} %copy-done.5, bf16[128,4096]{1,0:T(8,128)(2,1)S(1)} %copy-done.11, ...), custom_call_target="tpu_custom_call" | custom-call | flops 6442450944 | bytes 14680064 | tf_op jit(solution)/shard_map/pallas_call | solution.py:152
  124.1 12.1 %shard_map.47 = f32[3,3,256]{2,1,0:T(4,128)S(1)} custom-call(s32[4]{0:T(128)S(1)} %pad_add_fusion.2.info, s32[3,9,256]{2,1,0:T(8,128)S(1)} %pad_add_fusion.refs_0_, f32[3,3,256]{2,1,0:T(4,128)S(1)} %shard_map.46.refs_1_, bf16[256,4096]{1,0:T(8,128)(2,1)S(1)} %copy-done.3, bf16[128,4096]{1,0:T(8,128)(2,1)S(1)} %copy-done.6, bf16[128,4096]{1,0:T(8,128)(2,1)S(1)} %copy-done.12, ...), custom_call_target="tpu_custom_call" | custom-call | flops 6442450944 | bytes 14680064 | tf_op jit(solution)/shard_map/pallas_call | solution.py:152
  136.2 2.0 %collective-permute-start.19 = (f32[3,256]{1,0:T(4,128)S(1)}, f32[3,256]{1,0:T(4,128)S(1)}, u32[]{:S(2)}, u32[]{:S(2)}) collective-permute-start(f32[3,256]{1,0:T(4,128)S(1)} %get-tuple-element.17), channel_id=1, source_target_pairs={{0,3},{1,0},{2,1},{3,2},{4,7},{5,4},{6,5},{7,6},{8,11},{9,8},{10,9... | collective-permute-start | bytes 9224 | tf_op jit(solution)/shard_map/ppermute | solution.py:23
  138.3 8.2 %shard_map.48 = f32[1,3,256]{2,1,0:T(4,128)S(1)} custom-call(s32[4]{0:T(128)S(1)} %pad_add_fusion.2.info, s32[1,9,256]{2,1,0:T(8,128)S(1)} %bitcast.43, bf16[128,4096]{1,0:T(8,128)(2,1)S(1)} %collective-permute-done.22.refs_1_, bf16[128,4096]{1,0:T(8,128)(2,1)S(1)} %collective-permute-done.23.refs_2_, ...), custom_call_target="tpu_custom_call" | custom-call | flops 4294967296 | bytes 18874368 | tf_op jit(solution)/shard_map/pallas_call | solution.py:152
  146.5 3.6 %collective-permute-start.24 = (f32[3,256]{1,0:T(4,128)S(1)}, f32[3,256]{1,0:T(4,128)S(1)}, u32[]{:S(2)}, u32[]{:S(2)}) collective-permute-start(f32[3,256]{1,0:T(4,128)S(1)} %bitcast.44), channel_id=1, source_target_pairs={{0,2},{1,3},{2,0},{3,1},{4,6},{5,7},{6,4},{7,5},{8,10},{9,11},{10,... | collective-permute-start | bytes 9224 | tf_op jit(solution)/shard_map/ppermute | solution.py:23
  150.1 1.6 %collective-permute-done.24 = f32[3,256]{1,0:T(4,128)S(1)} collective-permute-done((f32[3,256]{1,0:T(4,128)S(1)}, f32[3,256]{1,0:T(4,128)S(1)}, u32[]{:S(2)}, u32[]{:S(2)}) %collective-permute-start.24) | collective-permute-done | bytes 3104 | tf_op jit(solution)/shard_map/ppermute | solution.py:23
  (69 shorter events, 8.7 us)
Async XLA Ops:
  0.0 26.6 %copy-start = (s32[2,8]{1,0:T(2,128)S(1)}, s32[2,8]{1,0:T(2,128)}, u32[]{:S(2)}) copy-start(s32[2,8]{1,0:T(2,128)} %param.6) | copy-start | bytes 196
  1.1 1.6 %collective-permute-start.6 = (bf16[256,512]{1,0:T(8,128)(2,1)S(1)}, bf16[256,512]{1,0:T(8,128)(2,1)S(1)}, u32[]{:S(2)}, u32[]{:S(2)}) collective-permute-start(bf16[256,512]{1,0:T(8,128)(2,1)S(1)} %get-tuple-element.12), channel_id=1, source_target_pairs={{0,16},{16,0},{1,17},{17,1},{2,18},{18,2},{3,19},{19,3},{4,20},{20... | collective-permute-start | bytes 786440 | tf_op jit(solution)/shard_map/ppermute | solution.py:44
  2.8 11.3 %collective-permute-start.7 = (bf16[2,256,512]{2,1,0:T(8,128)(2,1)S(1)}, bf16[2,256,512]{2,1,0:T(8,128)(2,1)S(1)}, u32[]{:S(2)}, u32[]{:S(2)}) collective-permute-start(bf16[2,256,512]{2,1,0:T(8,128)(2,1)S(1)} %get-tuple-element.10), channel_id=1, source_target_pairs={{0,32},{1,33},{2,34},{3,35},{4,36},{5,37},{6,38},{7,39},{8,40},{9,... | collective-permute-start | bytes 1572872 | tf_op jit(solution)/shard_map/ppermute | solution.py:40
  4.8 14.6 %collective-permute-start.8 = (bf16[2,256,512]{2,1,0:T(8,128)(2,1)S(1)}, bf16[2,256,512]{2,1,0:T(8,128)(2,1)S(1)}, u32[]{:S(2)}, u32[]{:S(2)}) collective-permute-start(bf16[2,256,512]{2,1,0:T(8,128)(2,1)S(1)} %get-tuple-element.10), channel_id=1, source_target_pairs={{0,96},{1,97},{2,98},{3,99},{4,100},{5,101},{6,102},{7,103},{8,104... | collective-permute-start | bytes 1572872 | tf_op jit(solution)/shard_map/ppermute | solution.py:40
  7.0 14.2 %collective-permute-start.9 = (bf16[2,256,512]{2,1,0:T(8,128)(2,1)S(1)}, bf16[2,256,512]{2,1,0:T(8,128)(2,1)S(1)}, u32[]{:S(2)}, u32[]{:S(2)}) collective-permute-start(bf16[2,256,512]{2,1,0:T(8,128)(2,1)S(1)} %get-tuple-element.10), channel_id=1, source_target_pairs={{0,64},{1,65},{2,66},{3,67},{4,68},{5,69},{6,70},{7,71},{8,72},{9,... | collective-permute-start | bytes 1572872 | tf_op jit(solution)/shard_map/ppermute | solution.py:40
  21.5 30.8 %collective-permute-start.10 = (bf16[4,2,256,512]{3,2,1,0:T(8,128)(2,1)S(1)}, bf16[4,2,256,512]{3,2,1,0:T(8,128)(2,1)}, u32[]{:S(2)}, u32[]{:S(2)}) collective-permute-start(bf16[4,2,256,512]{3,2,1,0:T(8,128)(2,1)S(1)} %pad_maximum_fusion.refs_6_.refs_3_), channel_id=1, source_target_pairs={{0,4},{1,5},{2,6},{3,7},{4,8},{5,9},{6,10},{7,11},{8,12},{9,13},{1... | collective-permute-start | bytes 6291464 | tf_op jit(solution)/shard_map/ppermute | solution.py:40
  23.1 33.3 %collective-permute-start.11 = (bf16[4,2,256,512]{3,2,1,0:T(8,128)(2,1)S(1)}, bf16[4,2,256,512]{3,2,1,0:T(8,128)(2,1)}, u32[]{:S(2)}, u32[]{:S(2)}) collective-permute-start(bf16[4,2,256,512]{3,2,1,0:T(8,128)(2,1)S(1)} %pad_maximum_fusion.refs_6_.refs_3_), channel_id=1, source_target_pairs={{0,12},{1,13},{2,14},{3,15},{4,0},{5,1},{6,2},{7,3},{8,4},{9,5},{1... | collective-permute-start | bytes 6291464 | tf_op jit(solution)/shard_map/ppermute | solution.py:40
  25.0 31.4 %collective-permute-start.2 = (bf16[128,4096]{1,0:T(8,128)(2,1)S(1)}, bf16[128,4096]{1,0:T(8,128)(2,1)S(1)}, u32[]{:S(2)}, u32[]{:S(2)}) collective-permute-start(bf16[128,4096]{1,0:T(8,128)(2,1)S(1)} %get-tuple-element.8), channel_id=1, source_target_pairs={{0,1},{1,2},{2,3},{3,0},{4,5},{5,6},{6,7},{7,4},{8,9},{9,10},{10,1... | collective-permute-start | bytes 3145736 | tf_op jit(solution)/shard_map/ppermute | solution.py:23
  26.6 23.6 %collective-permute-start = (s32[9,256]{1,0:T(8,128)S(1)}, s32[9,256]{1,0:T(8,128)S(1)}, u32[]{:S(2)}, u32[]{:S(2)}) collective-permute-start(s32[9,256]{1,0:T(8,128)S(1)} %get-tuple-element.19), channel_id=1, source_target_pairs={{0,1},{1,2},{2,3},{3,0},{4,5},{5,6},{6,7},{7,4},{8,9},{9,10},{10,1... | collective-permute-start | bytes 27656 | tf_op jit(solution)/shard_map/ppermute | solution.py:23
  28.2 23.6 %collective-permute-start.1 = (s32[9,256]{1,0:T(8,128)S(1)}, s32[9,256]{1,0:T(8,128)S(1)}, u32[]{:S(2)}, u32[]{:S(2)}) collective-permute-start(s32[9,256]{1,0:T(8,128)S(1)} %get-tuple-element.19), channel_id=1, source_target_pairs={{0,3},{1,0},{2,1},{3,2},{4,7},{5,4},{6,5},{7,6},{8,11},{9,8},{10,9... | collective-permute-start | bytes 27656 | tf_op jit(solution)/shard_map/ppermute | solution.py:23
  50.3 26.1 %collective-permute-start.5 = (bf16[128,4096]{1,0:T(8,128)(2,1)S(1)}, bf16[128,4096]{1,0:T(8,128)(2,1)S(1)}, u32[]{:S(2)}, u32[]{:S(2)}) collective-permute-start(bf16[128,4096]{1,0:T(8,128)(2,1)S(1)} %get-tuple-element.7), channel_id=1, source_target_pairs={{0,3},{1,0},{2,1},{3,2},{4,7},{5,4},{6,5},{7,6},{8,11},{9,8},{10,9... | collective-permute-start | bytes 3145736 | tf_op jit(solution)/shard_map/ppermute | solution.py:23
  51.8 26.7 %collective-permute-start.3 = (bf16[128,4096]{1,0:T(8,128)(2,1)S(1)}, bf16[128,4096]{1,0:T(8,128)(2,1)S(1)}, u32[]{:S(2)}, u32[]{:S(2)}) collective-permute-start(bf16[128,4096]{1,0:T(8,128)(2,1)S(1)} %get-tuple-element.7), channel_id=1, source_target_pairs={{0,1},{1,2},{2,3},{3,0},{4,5},{5,6},{6,7},{7,4},{8,9},{9,10},{10,1... | collective-permute-start | bytes 3145736 | tf_op jit(solution)/shard_map/ppermute | solution.py:23
  52.3 43.3 %collective-permute-start.4 = (bf16[128,4096]{1,0:T(8,128)(2,1)S(1)}, bf16[128,4096]{1,0:T(8,128)(2,1)S(1)}, u32[]{:S(2)}, u32[]{:S(2)}) collective-permute-start(bf16[128,4096]{1,0:T(8,128)(2,1)S(1)} %get-tuple-element.8), channel_id=1, source_target_pairs={{0,3},{1,0},{2,1},{3,2},{4,7},{5,4},{6,5},{7,6},{8,11},{9,8},{10,9... | collective-permute-start | bytes 3145736 | tf_op jit(solution)/shard_map/ppermute | solution.py:23
  56.4 40.2 %copy-start.4 = (bf16[128,4096]{1,0:T(8,128)(2,1)}, bf16[128,4096]{1,0:T(8,128)(2,1)S(1)}, u32[]{:S(2)}) copy-start(bf16[128,4096]{1,0:T(8,128)(2,1)S(1)} %collective-permute-done.2.refs_2_.refs_3_) | copy-start | bytes 3145732
  56.4 40.9 %collective-permute-start.14 = (bf16[4,2,256,512]{3,2,1,0:T(8,128)(2,1)S(1)}, bf16[4,2,256,512]{3,2,1,0:T(8,128)(2,1)}, u32[]{:S(2)}, u32[]{:S(2)}) collective-permute-start(bf16[4,2,256,512]{3,2,1,0:T(8,128)(2,1)S(1)} %pad_maximum_fusion.refs_6_.refs_3_), channel_id=1, source_target_pairs={{0,16},{16,0},{1,17},{17,1},{2,18},{18,2},{3,19},{19,3},{4,20},{20... | collective-permute-start | bytes 6291464 | tf_op jit(solution)/shard_map/ppermute | solution.py:44
  56.5 40.1 %collective-permute-start.12 = (bf16[2,2,256,512]{3,2,1,0:T(8,128)(2,1)S(1)}, bf16[2,2,256,512]{3,2,1,0:T(8,128)(2,1)S(1)}, u32[]{:S(2)}, u32[]{:S(2)}) collective-permute-start(bf16[2,2,256,512]{3,2,1,0:T(8,128)(2,1)S(1)} %slice.40), channel_id=1, source_target_pairs={{0,4},{1,5},{2,6},{3,7},{4,8},{5,9},{6,10},{7,11},{8,12},{9,13},{1... | collective-permute-start | bytes 3145736 | tf_op jit(solution)/shard_map/ppermute | solution.py:40
  76.4 20.7 %copy-start.7 = (bf16[128,4096]{1,0:T(8,128)(2,1)}, bf16[128,4096]{1,0:T(8,128)(2,1)S(1)}, u32[]{:S(2)}) copy-start(bf16[128,4096]{1,0:T(8,128)(2,1)S(1)} %collective-permute-done.5.refs_5_.refs_6_) | copy-start | bytes 3145732
  76.4 20.7 %collective-permute-start.13 = (bf16[2,2,256,512]{3,2,1,0:T(8,128)(2,1)S(1)}, bf16[2,2,256,512]{3,2,1,0:T(8,128)(2,1)}, u32[]{:S(2)}, u32[]{:S(2)}) collective-permute-start(bf16[2,2,256,512]{3,2,1,0:T(8,128)(2,1)S(1)} %slice.41), channel_id=1, source_target_pairs={{0,12},{1,13},{2,14},{3,15},{4,0},{5,1},{6,2},{7,3},{8,4},{9,5},{1... | collective-permute-start | bytes 3145736 | tf_op jit(solution)/shard_map/ppermute | solution.py:40
  79.5 44.5 %collective-permute-start.15 = (bf16[4,2,256,512]{3,2,1,0:T(8,128)(2,1)}, bf16[4,2,256,512]{3,2,1,0:T(8,128)(2,1)}, u32[]{:S(2)}, u32[]{:S(2)}) collective-permute-start(bf16[4,2,256,512]{3,2,1,0:T(8,128)(2,1)} %collective-permute-done.10.refs_7_.refs_4_), channel_id=1, source_target_pairs={{0,16},{16,0},{1,17},{17,1},{2,18},{18,2},{3,19},{19,3},{4,20},{20... | collective-permute-start | bytes 6291464 | tf_op jit(solution)/shard_map/ppermute | solution.py:44
  96.5 27.5 %collective-permute-start.16 = (bf16[4,2,256,512]{3,2,1,0:T(8,128)(2,1)}, bf16[4,2,256,512]{3,2,1,0:T(8,128)(2,1)}, u32[]{:S(2)}, u32[]{:S(2)}) collective-permute-start(bf16[4,2,256,512]{3,2,1,0:T(8,128)(2,1)} %collective-permute-done.11.refs_8_.refs_5_), channel_id=1, source_target_pairs={{0,16},{16,0},{1,17},{17,1},{2,18},{18,2},{3,19},{19,3},{4,20},{20... | collective-permute-start | bytes 6291464 | tf_op jit(solution)/shard_map/ppermute | solution.py:44
  96.5 6.9 %collective-permute-start.17 = (bf16[2,2,256,512]{3,2,1,0:T(8,128)(2,1)S(1)}, bf16[2,2,256,512]{3,2,1,0:T(8,128)(2,1)}, u32[]{:S(2)}, u32[]{:S(2)}) collective-permute-start(bf16[2,2,256,512]{3,2,1,0:T(8,128)(2,1)S(1)} %collective-permute-done.12.refs_9_.refs_6_), channel_id=1, source_target_pairs={{0,16},{16,0},{1,17},{17,1},{2,18},{18,2},{3,19},{19,3},{4,20},{20... | collective-permute-start | bytes 3145736 | tf_op jit(solution)/shard_map/ppermute | solution.py:44
  97.1 26.9 %collective-permute-start.18 = (bf16[2,2,256,512]{3,2,1,0:T(8,128)(2,1)}, bf16[2,2,256,512]{3,2,1,0:T(8,128)(2,1)}, u32[]{:S(2)}, u32[]{:S(2)}) collective-permute-start(bf16[2,2,256,512]{3,2,1,0:T(8,128)(2,1)} %collective-permute-done.13.refs_10_.refs_7_), channel_id=1, source_target_pairs={{0,16},{16,0},{1,17},{17,1},{2,18},{18,2},{3,19},{19,3},{4,20},{20... | collective-permute-start | bytes 3145736 | tf_op jit(solution)/shard_map/ppermute | solution.py:44
  97.3 41.0 %collective-permute-start.22 = (bf16[128,4096]{1,0:T(8,128)(2,1)}, bf16[128,4096]{1,0:T(8,128)(2,1)S(1)}, u32[]{:S(2)}, u32[]{:S(2)}) collective-permute-start(bf16[128,4096]{1,0:T(8,128)(2,1)} %copy-done.4), channel_id=1, source_target_pairs={{0,1},{1,2},{2,3},{3,0},{4,5},{5,6},{6,7},{7,4},{8,9},{9,10},{10,1... | collective-permute-start | bytes 3145736 | tf_op jit(solution)/shard_map/ppermute | solution.py:23
  103.5 34.8 %collective-permute-start.23 = (bf16[128,4096]{1,0:T(8,128)(2,1)}, bf16[128,4096]{1,0:T(8,128)(2,1)S(1)}, u32[]{:S(2)}, u32[]{:S(2)}) collective-permute-start(bf16[128,4096]{1,0:T(8,128)(2,1)} %copy-done.7), channel_id=1, source_target_pairs={{0,3},{1,0},{2,1},{3,2},{4,7},{5,4},{6,5},{7,6},{8,11},{9,8},{10,9... | collective-permute-start | bytes 3145736 | tf_op jit(solution)/shard_map/ppermute | solution.py:23
  112.7 11.3 %copy-start.6 = (bf16[128,4096]{1,0:T(8,128)(2,1)S(1)}, bf16[128,4096]{1,0:T(8,128)(2,1)}, u32[]{:S(2)}) copy-start(bf16[128,4096]{1,0:T(8,128)(2,1)} %copy-done.4) | copy-start | bytes 3145732
  112.7 11.3 %copy-start.9 = (bf16[128,4096]{1,0:T(8,128)(2,1)S(1)}, bf16[128,4096]{1,0:T(8,128)(2,1)}, u32[]{:S(2)}) copy-start(bf16[128,4096]{1,0:T(8,128)(2,1)} %copy-done.7) | copy-start | bytes 3145732
  112.7 11.3 %copy-start.12 = (bf16[128,4096]{1,0:T(8,128)(2,1)S(1)}, bf16[128,4096]{1,0:T(8,128)(2,1)}, u32[]{:S(2)}) copy-start(bf16[128,4096]{1,0:T(8,128)(2,1)} %copy-done.10) | copy-start | bytes 3145732
  112.7 11.3 %copy-start.15 = (bf16[128,4096]{1,0:T(8,128)(2,1)S(1)}, bf16[128,4096]{1,0:T(8,128)(2,1)}, u32[]{:S(2)}) copy-start(bf16[128,4096]{1,0:T(8,128)(2,1)} %copy-done.13) | copy-start | bytes 3145732
  123.9 14.3 %collective-permute-start.21 = (s32[9,256]{1,0:T(8,128)S(1)}, s32[9,256]{1,0:T(8,128)S(1)}, u32[]{:S(2)}, u32[]{:S(2)}) collective-permute-start(s32[9,256]{1,0:T(8,128)S(1)} %get-tuple-element.19), channel_id=1, source_target_pairs={{0,2},{1,3},{2,0},{3,1},{4,6},{5,7},{6,4},{7,5},{8,10},{9,11},{10,... | collective-permute-start | bytes 27656 | tf_op jit(solution)/shard_map/ppermute | solution.py:23
  136.2 13.9 %collective-permute-start.19 = (f32[3,256]{1,0:T(4,128)S(1)}, f32[3,256]{1,0:T(4,128)S(1)}, u32[]{:S(2)}, u32[]{:S(2)}) collective-permute-start(f32[3,256]{1,0:T(4,128)S(1)} %get-tuple-element.17), channel_id=1, source_target_pairs={{0,3},{1,0},{2,1},{3,2},{4,7},{5,4},{6,5},{7,6},{8,11},{9,8},{10,9... | collective-permute-start | bytes 9224 | tf_op jit(solution)/shard_map/ppermute | solution.py:23
  138.1 12.0 %collective-permute-start.20 = (f32[3,256]{1,0:T(4,128)S(1)}, f32[3,256]{1,0:T(4,128)S(1)}, u32[]{:S(2)}, u32[]{:S(2)}) collective-permute-start(f32[3,256]{1,0:T(4,128)S(1)} %get-tuple-element.16), channel_id=1, source_target_pairs={{0,1},{1,2},{2,3},{3,0},{4,5},{5,6},{6,7},{7,4},{8,9},{9,10},{10,1... | collective-permute-start | bytes 9224 | tf_op jit(solution)/shard_map/ppermute | solution.py:23
  146.5 5.2 %collective-permute-start.24 = (f32[3,256]{1,0:T(4,128)S(1)}, f32[3,256]{1,0:T(4,128)S(1)}, u32[]{:S(2)}, u32[]{:S(2)}) collective-permute-start(f32[3,256]{1,0:T(4,128)S(1)} %bitcast.44), channel_id=1, source_target_pairs={{0,2},{1,3},{2,0},{3,1},{4,6},{5,7},{6,4},{7,5},{8,10},{9,11},{10,... | collective-permute-start | bytes 9224 | tf_op jit(solution)/shard_map/ppermute | solution.py:23
  (10 other events, 28.5 us)

commit v2 on v0

v2 whole, which is shorter than its diff:
```python
import functools

import jax
import jax.numpy as jnp
from jax import lax
from jax.experimental import pallas as pl
from jax.experimental.pallas import tpu as pltpu
from jax.sharding import Mesh
from jax.sharding import PartitionSpec as P

QROWS = 128
PBLK = 256
LISTED = 8
PIECES = 8
RING = 4
PACE_M, PACE_A, PACE_B = 4, 10, 5
AXES = ("z", "core", "y", "x")
VMEM = 60 * 1024 * 1024
REL = (0, -1, 1, 2)


def ring(axis, step):
    return [(i, (i + step) % RING) for i in range(RING)]


def shift(array, axis, step):
    return lax.ppermute(array, axis, ring(axis, step))


def device(z, core, y, x):
    return ((z * 2 + core) * RING + y) * RING + x


def shift_zy(array, first, step):
    pairs = []
    for z in range(RING):
        for core in range(2):
            for y in range(RING):
                for x in range(RING):
                    along_z = (core == 0) == first
                    to_z = (z + step) % RING if along_z else z
                    to_y = y if along_z else (y + step) % RING
                    pairs.append((device(z, core, y, x), device(to_z, core, to_y, x)))
    return lax.ppermute(array, AXES, pairs)


def shift_x(array, step):
    pairs = []
    for core in range(2):
        for x in range(RING):
            pairs.append((core * RING + x, core * RING + (x + (1 - 2 * core) * step) % RING))
    return lax.ppermute(array, ("core", "x"), pairs)


def both(array):
    return array, swap(array)


def swap(array):
    return lax.ppermute(array, "core", [(0, 1), (1, 0)])


def token(arrays, us):
    def kernel(*refs):
        refs[-1][...] = jnp.zeros_like(refs[-1])

    return pl.pallas_call(
        kernel,
        out_shape=jax.ShapeDtypeStruct((8, 128), jnp.float32),
        in_specs=[pl.BlockSpec(memory_space=pl.ANY)] * len(arrays),
        out_specs=pl.BlockSpec(memory_space=pltpu.VMEM),
        compiler_params=pltpu.CompilerParams(vmem_limit_bytes=VMEM),
        cost_estimate=pl.CostEstimate(
            flops=int(us * 1.15e9), bytes_accessed=0, transcendentals=0
        ),
    )(*arrays)


def after(array, tokens):
    def kernel(*refs):
        pass

    anywhere = pl.BlockSpec(memory_space=pl.ANY)
    return pl.pallas_call(
        kernel,
        out_shape=jax.ShapeDtypeStruct(array.shape, array.dtype),
        in_specs=[anywhere] * (1 + len(tokens)),
        out_specs=anywhere,
        input_output_aliases={0: 0},
        compiler_params=pltpu.CompilerParams(vmem_limit_bytes=VMEM),
        cost_estimate=pl.CostEstimate(flops=1000, bytes_accessed=0, transcendentals=0),
    )(array, *tokens)


def score_kernel(first, extra, scale, info, lists, positive, *refs):
    refs = list(refs)
    queries = [refs.pop(0) for _ in range(2)]
    pieces = [[refs.pop(0) for _ in range(PIECES)] for _ in range(2)] if first else refs.pop(0)
    del refs[:extra]
    outs = [refs.pop(0) for _ in range(2)]
    whole = refs.pop(0) if first else None
    q_all, p_buf, a_sem, p_sem, w_sem = refs
    me_z, me_core, me_y, me_x = (info[k] for k in range(4))
    feats = p_buf.shape[2] // 8

    def turn(value, step):
        return lax.rem(value + step + RING, RING)

    def any_of(s, block, test):
        found = test(lists[s, block * LISTED])
        for n in range(1, LISTED):
            found = jnp.logical_or(found, test(lists[s, block * LISTED + n]))
        return found

    def load_passages(k, source):
        g = lax.rem(me_core + source, 2)
        for which in range(2):
            @pl.when(g == which)
            def _():
                for m in range(RING):
                    i, j = (k, m) if source == 0 else (m, k)
                    column = pl.multiple_of((turn(me_z, REL[m]) * 2 + source) * feats, feats)
                    pltpu.make_async_copy(
                        pieces[which][i * 2 + j // 2].at[j % 2],
                        p_buf.at[k, :, pl.ds(column, feats)],
                        p_sem.at[k],
                    ).start()

    def load_whole(k):
        pltpu.make_async_copy(pieces.at[k], p_buf.at[k], p_sem.at[k]).start()

    for s in range(2):
        pltpu.make_async_copy(queries[s], q_all.at[s], a_sem.at[s]).start()
    for k in range(RING):
        if first:
            for source in range(2):
                load_passages(k, source)
        elif k < 2:
            load_whole(k)

    def owner_of(k):
        return turn(me_y, jnp.where(k == 3, 2, jnp.where(k == 2, 1, -k))) * RING + me_x

    def choose(k, s):
        owner = owner_of(k)
        block = any_of(s, 1, lambda b: lax.shift_right_arithmetic(b, 1) == owner)
        block = block.astype(jnp.int32)
        return block, pl.ds(pl.multiple_of(block * QROWS, QROWS), QROWS)

    for out in outs:
        rows = lax.broadcasted_iota(jnp.int32, out.shape, 0)
        out[...] = jnp.where(rows == 0, -1e30, 0.0).astype(jnp.float32)
    for s in range(2):
        pltpu.make_async_copy(q_all.at[s], q_all.at[s], a_sem.at[s]).wait()

    @pl.loop(0, RING)
    def _(k):
        index = lax.broadcasted_iota(jnp.int32, (PBLK, 2 * QROWS), 0)
        left = lax.broadcasted_iota(jnp.int32, (1, 2 * QROWS), 1) < QROWS
        owner = owner_of(k)
        chosen, lanes = zip(*[choose(k, s) for s in range(2)])
        listed = []
        for b in range(2):
            sides = [
                any_of(s, chosen[s], lambda v: v == owner * 2 + b).astype(jnp.int32)
                for s in range(2)
            ]
            listed.append(jnp.where(left, sides[0], sides[1]) > 0)
        pltpu.make_async_copy(p_buf.at[k], p_buf.at[k], p_sem.at[k]).wait()
        if first:
            pltpu.make_async_copy(p_buf.at[k], whole.at[k], w_sem.at[k]).start()
        else:
            @pl.when(k + 2 < RING)
            def _():
                load_whole(k + 2)
        rows = jnp.concatenate([q_all[s, lanes[s], :] for s in range(2)], axis=0)
        scores = lax.dot_general(
            p_buf[k], rows, (((1,), (1,)), ((), ())), preferred_element_type=jnp.float32
        ) * scale

        def get(row):
            return jnp.concatenate([outs[s][row : row + 1, lanes[s]] for s in range(2)], axis=1)

        wanted = jnp.concatenate([positive[s : s + 1, lanes[s]] for s in range(2)], axis=1)
        old = get(0)
        halves = [scores[:PBLK], scores[PBLK:]]
        top = old
        for b in range(2):
            peak = jnp.max(halves[b], axis=0, keepdims=True)
            top = jnp.where(listed[b], jnp.maximum(top, peak), top)
        total = get(1) * jnp.exp(old - top)
        hits = get(2)
        for b in range(2):
            here = jnp.sum(jnp.exp(halves[b] - top), axis=0, keepdims=True)
            total = total + jnp.where(listed[b], here, 0.0)
            place = wanted - (owner * 2 + b) * PBLK
            hits = hits + jnp.sum(jnp.where(index == place, halves[b], 0.0), axis=0, keepdims=True)
        for s in range(2):
            part = slice(s * QROWS, (s + 1) * QROWS)
            outs[s][0:1, lanes[s]] = top[:, part]
            outs[s][1:2, lanes[s]] = total[:, part]
            outs[s][2:3, lanes[s]] = hits[:, part]

    if first:
        for k in range(RING):
            pltpu.make_async_copy(p_buf.at[k], whole.at[k], w_sem.at[k]).wait()


def score(info, lists, positive, queries, pieces, extra=()):
    first = isinstance(pieces, list)
    rows, features = queries[0].shape
    flat = list(queries) + ([a for arrays in pieces for a in arrays] if first else [pieces])
    flat += list(extra)
    smem, vmem = pl.BlockSpec(memory_space=pltpu.SMEM), pl.BlockSpec(memory_space=pltpu.VMEM)
    anywhere = pl.BlockSpec(memory_space=pl.ANY)
    stats = [jax.ShapeDtypeStruct((3, rows), jnp.float32)] * 2
    whole = jax.ShapeDtypeStruct((RING, 2 * PBLK, features), jnp.bfloat16)
    return pl.pallas_call(
        functools.partial(score_kernel, first, len(extra), float(features) ** -0.5),
        out_shape=stats + [whole] * first,
        in_specs=[smem, smem, vmem] + [anywhere] * len(flat),
        out_specs=[vmem, vmem] + [anywhere] * first,
        scratch_shapes=[
            pltpu.VMEM((2, rows, features), jnp.bfloat16),
            pltpu.VMEM((RING, 2 * PBLK, features), jnp.bfloat16),
            pltpu.SemaphoreType.DMA((2,)),
            pltpu.SemaphoreType.DMA((RING,)),
            pltpu.SemaphoreType.DMA((RING,)),
        ],
        compiler_params=pltpu.CompilerParams(vmem_limit_bytes=VMEM),
        cost_estimate=pl.CostEstimate(flops=1000000, bytes_accessed=0, transcendentals=0),
    )(info, lists, positive, *flat)


def finish(stats):
    top, total, chosen = stats[:, 0], stats[:, 1], stats[:, 2]
    peak = jnp.max(top, axis=0)
    summed = jnp.sum(total * jnp.exp(top - peak[None, :]), axis=0)
    return peak + jnp.log(summed) - jnp.sum(chosen, axis=0)


def body(queries, passages, lists, positive):
    info = jnp.stack([lax.axis_index(a) for a in AXES]).astype(jnp.int32)

    meta = jnp.concatenate([positive, lists.reshape(-1)])
    ahead, behind = shift_x(queries, 1), shift_x(queries, -1)
    far = shift_x(ahead, 1)
    meta_a, meta_b, meta_f = shift_x(meta, 1), shift_x(meta, -1), shift_x(meta, 2)

    s01 = jnp.stack([passages, shift_zy(passages, True, 1)])
    s23 = jnp.stack([shift_zy(passages, True, -1), shift_zy(passages, True, 2)])
    r01, l01 = shift_zy(s01, False, 1), shift_zy(s01, False, -1)
    l23, r23 = shift_zy(s23, False, -1), shift_zy(s23, False, 1)
    gate = token([ahead, token([meta_a, meta_b, meta_f], PACE_M)], PACE_A)
    fr = shift_zy(after(r01, [gate]), False, 1)
    fl = shift_zy(l23, False, -1)
    gate = token([behind], PACE_B)
    fr, fl = after(fr, [gate]), after(fl, [gate])
    pieces = [both(a) for a in (s01, s23, r01, r23, l01, l23, fr, fl)]
    pieces = [[a for a, _ in pieces], [b for _, b in pieces]]

    size = positive.shape[0]

    def pair(metas, sources, passages, extra=()):
        wanted = jnp.stack([m[:size] for m in metas])
        ids = jnp.stack([m[size:] for m in metas])
        return score(info, ids, wanted, sources, passages, extra)

    stats_a, stats_b, whole = pair([meta_a, meta_b], [ahead, behind], pieces)
    back = [shift_x(stats_a, -1), shift_x(stats_b, 1)]
    stats_o, stats_f = pair([meta, meta_f], [queries, far], whole, back)
    return finish(jnp.stack(back + [stats_o, shift_x(stats_f, 2)]))


def solution(mesh):
    fine = Mesh(mesh.devices.reshape(RING, 2, RING, RING), AXES)
    everywhere = ("z", "core", "y", "x")
    return jax.shard_map(
        body,
        mesh=fine,
        in_specs=(
            P(everywhere, None),
            P(("y", "x"), ("z", "core")),
            P(everywhere, None),
            P(everywhere),
        ),
        out_specs=P(everywhere),
        check_vma=False,
    )
```

time: 312 us -> 116 us (0.37)
  waiting for transfers between devices: 206 us -> 43.3 us
  blocking collectives: 46.3 us -> 0 us
  Pallas kernels: 0 us -> 28.4 us
  matrix products: 24 us -> 0 us
  starting transfers between devices: 14 us -> 34.3 us
  between operations: 13.5 us -> 0.19 us
    all_gather x2 -> x0, waiting for transfers between devices: 188 us -> none  [the longest x1 188 us: body(): lax.all_gather(queries, 'passage', axis=0, tiled=True)]
    all_gather x2 -> x0, blocking collectives: 46.3 us -> none  [the longest x1 23.7 us: body(): lax.all_gather(lists, 'passage', axis=0, tiled=True)]
    ppermute x0 -> x26, waiting for transfers between devices: none -> 43.3 us  [the longest x9 23.5 us: shift_zy(): return lax.ppermute(array, AXES, pairs)]
    ppermute x0 -> x26, starting transfers between devices: none -> 34.3 us  [the longest x9 17.2 us: shift_zy(): return lax.ppermute(array, AXES, pairs)]
    pallas_call x0 -> x8, Pallas kernels: none -> 28.4 us  [the longest x2 26.7 us: score(): pl.pallas_call(functools.partial(score_kernel, first, len(extra), float(f...]
    dot_general x1 -> x0, matrix products: 24 us -> none  [body(): lax.dot_general(all_rows, full_pass, contract, preferred_element_type=jnp...]
    all_to_all x3 -> x0, waiting for transfers between devices: 17 us -> none  [the longest x1 7.55 us: body(): lax.all_to_all(total, 'passage', split_axis=0, concat_axis=0, tiled=True)]
    all_to_all x3 -> x0, starting transfers between devices: 14 us -> none  [the longest x1 5.29 us: body(): lax.all_to_all(top, 'passage', split_axis=0, concat_axis=0, tiled=True)]
  transfers between devices with their start and end apart: 5 -> 26, of which waited for: 4 -> 15; matrix products, arithmetic and copies ran while one was open for 2% -> 5% of each run, Pallas kernels for 0% -> 15%
where the time goes in v2:
time: 116 us; the launch traced here: 115 us
  waiting for transfers between devices  43.3 us (37%)
  starting transfers between devices  34.3 us (30%)
  Pallas kernels  28.4 us (24%)
  other arithmetic  5.67 us (5%)
  local copies, waits for them, and re-layouts  3.43 us (3%)
    pallas_call x2, Pallas kernels, score(): pl.pallas_call(functools.partial(score_kernel, first, len(extra), float(f...  26.7 us
    ppermute x9, waiting for transfers between devices, shift_zy(): return lax.ppermute(array, AXES, pairs)  23.5 us
    ppermute x9, starting transfers between devices, shift_zy(): return lax.ppermute(array, AXES, pairs)  17.2 us
    ppermute x9, waiting for transfers between devices, shift_x(): return lax.ppermute(array, ('core', 'x'), pairs)  16 us
    ppermute x9, starting transfers between devices, shift_x(): return lax.ppermute(array, ('core', 'x'), pairs)  15.6 us
    ppermute x8, waiting for transfers between devices, swap(): return lax.ppermute(array, 'core', [(0, 1), (1, 0)])  3.8 us
    unnamed x34, local copies, waits for them, and re-layouts  3.22 us
  transfers between devices with their start and end apart: 26, of which 15 were waited for; matrix products, arithmetic and copies ran while one was open for 5% of the time, Pallas kernels for 15%

profile of v2, /device:TPU:0, one launch (start us, length us, event | category | flops | bytes accessed | tf_op | source)
XLA Modules:
  0.0 115.3 jit_solution(894027589983273264)
XLA Ops:
  0.0 1.6 %collective-permute-start.2 = (bf16[256,4096]{1,0:T(8,128)(2,1)}, bf16[256,4096]{1,0:T(8,128)(2,1)}, u32[]{:S(2)}, u32[]{:S(2)}) collective-permute-start(bf16[256,4096]{1,0:T(8,128)(2,1)} %refs_0_.1), channel_id=1, source_target_pairs={{0,1},{1,2},{2,3},{3,0},{16,19},{17,16},{18,17},{19,18},{4,5},{5,6... | collective-permute-start | bytes 6291464 | tf_op jit(solution)/shard_map/ppermute | solution.py:52
  1.6 1.9 %collective-permute-start.4 = (bf16[512,512]{1,0:T(8,128)(2,1)}, bf16[512,512]{1,0:T(8,128)(2,1)S(1)}, u32[]{:S(2)}, u32[]{:S(2)}) collective-permute-start(bf16[512,512]{1,0:T(8,128)(2,1)} %param.5), channel_id=1, source_target_pairs={{0,32},{1,33},{2,34},{3,35},{4,36},{5,37},{6,38},{7,39},{8,40},{9,... | collective-permute-start | bytes 1572872 | tf_op jit(solution)/shard_map/ppermute | solution.py:44
  3.5 2.1 %collective-permute-start.5 = (bf16[512,512]{1,0:T(8,128)(2,1)}, bf16[512,512]{1,0:T(8,128)(2,1)S(1)}, u32[]{:S(2)}, u32[]{:S(2)}) collective-permute-start(bf16[512,512]{1,0:T(8,128)(2,1)} %param.5), channel_id=1, source_target_pairs={{0,96},{1,97},{2,98},{3,99},{4,100},{5,101},{6,102},{7,103},{8,104... | collective-permute-start | bytes 1572872 | tf_op jit(solution)/shard_map/ppermute | solution.py:44
  5.6 1.9 %collective-permute-start.6 = (bf16[512,512]{1,0:T(8,128)(2,1)}, bf16[512,512]{1,0:T(8,128)(2,1)S(1)}, u32[]{:S(2)}, u32[]{:S(2)}) collective-permute-start(bf16[512,512]{1,0:T(8,128)(2,1)} %param.5), channel_id=1, source_target_pairs={{0,64},{1,65},{2,66},{3,67},{4,68},{5,69},{6,70},{7,71},{8,72},{9,... | collective-permute-start | bytes 1572872 | tf_op jit(solution)/shard_map/ppermute | solution.py:44
  7.5 5.5 %collective-permute-done.4 = bf16[512,512]{1,0:T(8,128)(2,1)S(1)} collective-permute-done((bf16[512,512]{1,0:T(8,128)(2,1)}, bf16[512,512]{1,0:T(8,128)(2,1)S(1)}, u32[]{:S(2)}, u32[]{:S(2)}) %collective-permute-start.4) | collective-permute-done | bytes 524320 | tf_op jit(solution)/shard_map/ppermute | solution.py:44
  13.0 1.2 %pad_maximum_fusion.refs_2_ = bf16[2,512,512]{2,1,0:T(8,128)(2,1)S(1)} fusion(bf16[1,512,512]{2,1,0:T(8,128)(2,1)S(1)} %bitcast.37, bf16[1,512,512]{2,1,0:T(8,128)(2,1)} %bitcast.34), kind=kLoop, calls=%fused_computation | loop fusion | flops 524288 | bytes 2097152 | tf_op jit(solution)/shard_map/stack | solution.py:250
  14.2 1.6 %collective-permute-start.7 = (bf16[2,512,512]{2,1,0:T(8,128)(2,1)S(1)}, bf16[2,512,512]{2,1,0:T(8,128)(2,1)S(1)}, u32[]{:S(2)}, u32[]{:S(2)}) collective-permute-start(bf16[2,512,512]{2,1,0:T(8,128)(2,1)S(1)} %pad_maximum_fusion.refs_2_), channel_id=1, source_target_pairs={{0,4},{1,5},{2,6},{3,7},{4,8},{5,9},{6,10},{7,11},{8,12},{9,13},{1... | collective-permute-start | bytes 3145736 | tf_op jit(solution)/shard_map/ppermute | solution.py:44
  15.8 2.5 %collective-permute-done.5 = bf16[512,512]{1,0:T(8,128)(2,1)S(1)} collective-permute-done((bf16[512,512]{1,0:T(8,128)(2,1)}, bf16[512,512]{1,0:T(8,128)(2,1)S(1)}, u32[]{:S(2)}, u32[]{:S(2)}) %collective-permute-start.5) | collective-permute-done | bytes 524320 | tf_op jit(solution)/shard_map/ppermute | solution.py:44
  18.3 2.1 %collective-permute-done.6 = bf16[512,512]{1,0:T(8,128)(2,1)S(1)} collective-permute-done((bf16[512,512]{1,0:T(8,128)(2,1)}, bf16[512,512]{1,0:T(8,128)(2,1)S(1)}, u32[]{:S(2)}, u32[]{:S(2)}) %collective-permute-start.6) | collective-permute-done | bytes 524320 | tf_op jit(solution)/shard_map/ppermute | solution.py:44
  20.5 4.3 %collective-permute-start.10 = (bf16[2,512,512]{2,1,0:T(8,128)(2,1)S(1)}, bf16[2,512,512]{2,1,0:T(8,128)(2,1)}, u32[]{:S(2)}, u32[]{:S(2)}) collective-permute-start(bf16[2,512,512]{2,1,0:T(8,128)(2,1)S(1)} %pad_maximum_fusion.1.refs_3_), channel_id=1, source_target_pairs={{0,12},{1,13},{2,14},{3,15},{4,0},{5,1},{6,2},{7,3},{8,4},{9,5},{1... | collective-permute-start | bytes 3145736 | tf_op jit(solution)/shard_map/ppermute | solution.py:44
  25.0 3.8 %collective-permute-start = (s32[272]{0:T(512)S(1)}, s32[272]{0:T(512)S(1)}, u32[]{:S(2)}, u32[]{:S(2)}) collective-permute-start(s32[272]{0:T(512)S(1)} %constant_dynamic-update-slice_fusion), channel_id=1, source_target_pairs={{0,1},{1,2},{2,3},{3,0},{16,19},{17,16},{18,17},{19,18},{4,5},{5,6... | collective-permute-start | bytes 3272 | tf_op jit(solution)/shard_map/ppermute | solution.py:52
  28.8 1.3 %collective-permute-done.refs_0_ = s32[272]{0:T(512)S(1)} collective-permute-done((s32[272]{0:T(512)S(1)}, s32[272]{0:T(512)S(1)}, u32[]{:S(2)}, u32[]{:S(2)}) %collective-permute-start) | collective-permute-done | bytes 1120 | tf_op jit(solution)/shard_map/ppermute | solution.py:52
  30.1 3.2 %collective-permute-start.11 = (s32[272]{0:T(512)S(1)}, s32[272]{0:T(512)S(1)}, u32[]{:S(2)}, u32[]{:S(2)}) collective-permute-start(s32[272]{0:T(512)S(1)} %constant_dynamic-update-slice_fusion), channel_id=1, source_target_pairs={{0,2},{1,3},{2,0},{3,1},{16,18},{17,19},{18,16},{19,17},{4,6},{5,7... | collective-permute-start | bytes 3272 | tf_op jit(solution)/shard_map/ppermute | solution.py:52
  33.3 1.7 %collective-permute-start.3 = (bf16[256,4096]{1,0:T(8,128)(2,1)}, bf16[256,4096]{1,0:T(8,128)(2,1)}, u32[]{:S(2)}, u32[]{:S(2)}) collective-permute-start(bf16[256,4096]{1,0:T(8,128)(2,1)} %refs_0_.1), channel_id=1, source_target_pairs={{0,3},{1,0},{2,1},{3,2},{16,17},{17,18},{18,19},{19,16},{4,7},{5,4... | collective-permute-start | bytes 6291464 | tf_op jit(solution)/shard_map/ppermute | solution.py:52
  36.5 3.2 %collective-permute-start.9 = (bf16[2,512,512]{2,1,0:T(8,128)(2,1)S(1)}, bf16[2,512,512]{2,1,0:T(8,128)(2,1)}, u32[]{:S(2)}, u32[]{:S(2)}) collective-permute-start(bf16[2,512,512]{2,1,0:T(8,128)(2,1)S(1)} %pad_maximum_fusion.refs_2_), channel_id=1, source_target_pairs={{0,12},{1,13},{2,14},{3,15},{4,0},{5,1},{6,2},{7,3},{8,4},{9,5},{1... | collective-permute-start | bytes 3145736 | tf_op jit(solution)/shard_map/ppermute | solution.py:44
  39.7 1.0 copy.24.refs_0_
  41.6 1.7 %collective-permute-start.12 = (bf16[2,512,512]{2,1,0:T(8,128)(2,1)}, bf16[2,512,512]{2,1,0:T(8,128)(2,1)}, u32[]{:S(2)}, u32[]{:S(2)}) collective-permute-start(bf16[2,512,512]{2,1,0:T(8,128)(2,1)} %shard_map.48), channel_id=1, source_target_pairs={{0,4},{1,5},{2,6},{3,7},{4,8},{5,9},{6,10},{7,11},{8,12},{9,13},{1... | collective-permute-start | bytes 3145736 | tf_op jit(solution)/shard_map/ppermute | solution.py:44
  43.3 9.2 %collective-permute-done.8.refs_5_ = bf16[2,512,512]{2,1,0:T(8,128)(2,1)} collective-permute-done((bf16[2,512,512]{2,1,0:T(8,128)(2,1)S(1)}, bf16[2,512,512]{2,1,0:T(8,128)(2,1)}, u32[]{:S(2)}, u32[]{:S(2)}) %collective-permute-start.8) | collective-permute-done | bytes 1048608 | tf_op jit(solution)/shard_map/ppermute | solution.py:44
  53.1 6.6 %collective-permute-done.3.refs_0_.refs_1_ = bf16[256,4096]{1,0:T(8,128)(2,1)} collective-permute-done((bf16[256,4096]{1,0:T(8,128)(2,1)}, bf16[256,4096]{1,0:T(8,128)(2,1)}, u32[]{:S(2)}, u32[]{:S(2)}) %collective-permute-start.3) | collective-permute-done | bytes 2097184 | tf_op jit(solution)/shard_map/ppermute | solution.py:52
  59.7 3.7 %collective-permute-done.13.refs_0_ = bf16[2,512,512]{2,1,0:T(8,128)(2,1)} collective-permute-done((bf16[2,512,512]{2,1,0:T(8,128)(2,1)}, bf16[2,512,512]{2,1,0:T(8,128)(2,1)}, u32[]{:S(2)}, u32[]{:S(2)}) %collective-permute-start.13) | collective-permute-done | bytes 1048608 | tf_op jit(solution)/shard_map/ppermute | solution.py:44
  63.8 2.3 %collective-permute-start.24 = (bf16[256,4096]{1,0:T(8,128)(2,1)}, bf16[256,4096]{1,0:T(8,128)(2,1)}, u32[]{:S(2)}, u32[]{:S(2)}) collective-permute-start(bf16[256,4096]{1,0:T(8,128)(2,1)} %collective-permute-done.2.refs_0_), channel_id=1, source_target_pairs={{0,1},{1,2},{2,3},{3,0},{16,19},{17,16},{18,17},{19,18},{4,5},{5,6... | collective-permute-start | bytes 6291464 | tf_op jit(solution)/shard_map/ppermute | solution.py:52
  70.4 2.3 %collective-permute-done.18.refs_14_ = bf16[2,512,512]{2,1,0:T(8,128)(2,1)S(1)} collective-permute-done((bf16[2,512,512]{2,1,0:T(8,128)(2,1)}, bf16[2,512,512]{2,1,0:T(8,128)(2,1)S(1)}, u32[]{:S(2)}, u32[]{:S(2)}) %collective-permute-start.18) | collective-permute-done | bytes 1048608 | tf_op jit(solution)/shard_map/ppermute | solution.py:60
  72.8 1.4 %collective-permute-done.20.refs_16_ = bf16[2,512,512]{2,1,0:T(8,128)(2,1)S(1)} collective-permute-done((bf16[2,512,512]{2,1,0:T(8,128)(2,1)}, bf16[2,512,512]{2,1,0:T(8,128)(2,1)S(1)}, u32[]{:S(2)}, u32[]{:S(2)}) %collective-permute-start.20) | collective-permute-done | bytes 1048608 | tf_op jit(solution)/shard_map/ppermute | solution.py:60
  74.2 1.0 copy-done.5
  75.2 15.9 %shard_map.52 = (f32[3,256]{1,0:T(4,128)}, f32[3,256]{1,0:T(4,128)}, bf16[4,512,4096]{2,1,0:T(8,128)(2,1)}) custom-call(s32[4]{0:T(128)} %pad_add_fusion.4.info, s32[2,16]{1,0:T(2,128)} %pad_add_fusion.2.lists, s32[2,256]{1,0:T(2,128)} %pad_add_fusion.positive, bf16[256,4096]{1,0:T(8,128)(2,1)} %collective-permute-done.2.refs_0_, ...), custom_call_target="tpu_custom_call" | custom-call | flops 1000000 | tf_op jit(solution)/shard_map/pallas_call | solution.py:218
  91.1 1.0 collective-permute-start.22
  92.1 1.1 collective-permute-start.23
  93.8 1.2 %collective-permute-done.22.refs_3_ = f32[3,256]{1,0:T(4,128)S(1)} collective-permute-done((f32[3,256]{1,0:T(4,128)}, f32[3,256]{1,0:T(4,128)S(1)}, u32[]{:S(2)}, u32[]{:S(2)}) %collective-permute-start.22) | collective-permute-done | bytes 3104 | tf_op jit(solution)/shard_map/ppermute | solution.py:52
  95.0 2.1 %collective-permute-done.23.refs_4_ = f32[3,256]{1,0:T(4,128)S(1)} collective-permute-done((f32[3,256]{1,0:T(4,128)}, f32[3,256]{1,0:T(4,128)S(1)}, u32[]{:S(2)}, u32[]{:S(2)}) %collective-permute-start.23) | collective-permute-done | bytes 3104 | tf_op jit(solution)/shard_map/ppermute | solution.py:52
  97.7 10.8 %shard_map.53 = (f32[3,256]{1,0:T(4,128)}, f32[3,256]{1,0:T(4,128)}) custom-call(s32[4]{0:T(128)} %pad_add_fusion.4.info, s32[2,16]{1,0:T(2,128)} %pad_add_fusion.3.lists, s32[2,256]{1,0:T(2,128)} %pad_add_fusion.1.positive, bf16[256,4096]{1,0:T(8,128)(2,1)} %refs_0_.1, bf16[256,4096]{1,0:T(8,128)(2,1)} %collective-permute-done.24.refs_1_, ...), custom_call_target="tpu_custom_call" | custom-call | flops 1000000 | tf_op jit(solution)/shard_map/pallas_call | solution.py:218
  108.5 0.9 collective-permute-start.25
  109.4 4.5 %collective-permute-done.25 = f32[3,256]{1,0:T(4,128)S(1)} collective-permute-done((f32[3,256]{1,0:T(4,128)}, f32[3,256]{1,0:T(4,128)S(1)}, u32[]{:S(2)}, u32[]{:S(2)}) %collective-permute-start.25) | collective-permute-done | bytes 3104 | tf_op jit(solution)/shard_map/ppermute | solution.py:52
  (85 shorter events, 10.4 us)
Async XLA Ops:
  0.0 41.0 %collective-permute-start.2 = (bf16[256,4096]{1,0:T(8,128)(2,1)}, bf16[256,4096]{1,0:T(8,128)(2,1)}, u32[]{:S(2)}, u32[]{:S(2)}) collective-permute-start(bf16[256,4096]{1,0:T(8,128)(2,1)} %refs_0_.1), channel_id=1, source_target_pairs={{0,1},{1,2},{2,3},{3,0},{16,19},{17,16},{18,17},{19,18},{4,5},{5,6... | collective-permute-start | bytes 6291464 | tf_op jit(solution)/shard_map/ppermute | solution.py:52
  1.6 11.4 %collective-permute-start.4 = (bf16[512,512]{1,0:T(8,128)(2,1)}, bf16[512,512]{1,0:T(8,128)(2,1)S(1)}, u32[]{:S(2)}, u32[]{:S(2)}) collective-permute-start(bf16[512,512]{1,0:T(8,128)(2,1)} %param.5), channel_id=1, source_target_pairs={{0,32},{1,33},{2,34},{3,35},{4,36},{5,37},{6,38},{7,39},{8,40},{9,... | collective-permute-start | bytes 1572872 | tf_op jit(solution)/shard_map/ppermute | solution.py:44
  3.5 14.8 %collective-permute-start.5 = (bf16[512,512]{1,0:T(8,128)(2,1)}, bf16[512,512]{1,0:T(8,128)(2,1)S(1)}, u32[]{:S(2)}, u32[]{:S(2)}) collective-permute-start(bf16[512,512]{1,0:T(8,128)(2,1)} %param.5), channel_id=1, source_target_pairs={{0,96},{1,97},{2,98},{3,99},{4,100},{5,101},{6,102},{7,103},{8,104... | collective-permute-start | bytes 1572872 | tf_op jit(solution)/shard_map/ppermute | solution.py:44
  5.6 14.8 %collective-permute-start.6 = (bf16[512,512]{1,0:T(8,128)(2,1)}, bf16[512,512]{1,0:T(8,128)(2,1)S(1)}, u32[]{:S(2)}, u32[]{:S(2)}) collective-permute-start(bf16[512,512]{1,0:T(8,128)(2,1)} %param.5), channel_id=1, source_target_pairs={{0,64},{1,65},{2,66},{3,67},{4,68},{5,69},{6,70},{7,71},{8,72},{9,... | collective-permute-start | bytes 1572872 | tf_op jit(solution)/shard_map/ppermute | solution.py:44
  13.0 11.9 %copy-start.15 = (s32[2,8]{1,0:T(2,128)S(1)}, s32[2,8]{1,0:T(2,128)}, u32[]{:S(2)}) copy-start(s32[2,8]{1,0:T(2,128)} %param.6) | copy-start | bytes 196
  13.0 12.0 %copy-start.8 = (s32[256]{0:T(256)S(1)}, s32[256]{0:T(256)}, u32[]{:S(2)}) copy-start(s32[256]{0:T(256)} %param.7) | copy-start | bytes 3076
  14.2 38.4 %copy-start = (bf16[2,512,512]{2,1,0:T(8,128)(2,1)}, bf16[2,512,512]{2,1,0:T(8,128)(2,1)S(1)}, u32[]{:S(2)}) copy-start(bf16[2,512,512]{2,1,0:T(8,128)(2,1)S(1)} %pad_maximum_fusion.refs_2_) | copy-start | bytes 3145732
  14.2 22.3 %collective-permute-start.7 = (bf16[2,512,512]{2,1,0:T(8,128)(2,1)S(1)}, bf16[2,512,512]{2,1,0:T(8,128)(2,1)S(1)}, u32[]{:S(2)}, u32[]{:S(2)}) collective-permute-start(bf16[2,512,512]{2,1,0:T(8,128)(2,1)S(1)} %pad_maximum_fusion.refs_2_), channel_id=1, source_target_pairs={{0,4},{1,5},{2,6},{3,7},{4,8},{5,9},{6,10},{7,11},{8,12},{9,13},{1... | collective-permute-start | bytes 3145736 | tf_op jit(solution)/shard_map/ppermute | solution.py:44
  20.5 32.0 %copy-start.2 = (bf16[2,512,512]{2,1,0:T(8,128)(2,1)}, bf16[2,512,512]{2,1,0:T(8,128)(2,1)S(1)}, u32[]{:S(2)}) copy-start(bf16[2,512,512]{2,1,0:T(8,128)(2,1)S(1)} %pad_maximum_fusion.1.refs_3_) | copy-start | bytes 3145732
  20.5 20.2 %collective-permute-start.10 = (bf16[2,512,512]{2,1,0:T(8,128)(2,1)S(1)}, bf16[2,512,512]{2,1,0:T(8,128)(2,1)}, u32[]{:S(2)}, u32[]{:S(2)}) collective-permute-start(bf16[2,512,512]{2,1,0:T(8,128)(2,1)S(1)} %pad_maximum_fusion.1.refs_3_), channel_id=1, source_target_pairs={{0,12},{1,13},{2,14},{3,15},{4,0},{5,1},{6,2},{7,3},{8,4},{9,5},{1... | collective-permute-start | bytes 3145736 | tf_op jit(solution)/shard_map/ppermute | solution.py:44
  25.0 5.1 %collective-permute-start = (s32[272]{0:T(512)S(1)}, s32[272]{0:T(512)S(1)}, u32[]{:S(2)}, u32[]{:S(2)}) collective-permute-start(s32[272]{0:T(512)S(1)} %constant_dynamic-update-slice_fusion), channel_id=1, source_target_pairs={{0,1},{1,2},{2,3},{3,0},{16,19},{17,16},{18,17},{19,18},{4,5},{5,6... | collective-permute-start | bytes 3272 | tf_op jit(solution)/shard_map/ppermute | solution.py:52
  28.8 4.6 %collective-permute-start.1 = (s32[272]{0:T(512)S(1)}, s32[272]{0:T(512)S(1)}, u32[]{:S(2)}, u32[]{:S(2)}) collective-permute-start(s32[272]{0:T(512)S(1)} %constant_dynamic-update-slice_fusion), channel_id=1, source_target_pairs={{0,3},{1,0},{2,1},{3,2},{16,17},{17,18},{18,19},{19,16},{4,7},{5,4... | collective-permute-start | bytes 3272 | tf_op jit(solution)/shard_map/ppermute | solution.py:52
  30.1 5.2 %copy-start.11 = (s32[272]{0:T(512)}, s32[272]{0:T(512)S(1)}, u32[]{:S(2)}) copy-start(s32[272]{0:T(512)S(1)} %collective-permute-done.refs_0_) | copy-start | bytes 3268
  30.1 5.2 %collective-permute-start.11 = (s32[272]{0:T(512)S(1)}, s32[272]{0:T(512)S(1)}, u32[]{:S(2)}, u32[]{:S(2)}) collective-permute-start(s32[272]{0:T(512)S(1)} %constant_dynamic-update-slice_fusion), channel_id=1, source_target_pairs={{0,2},{1,3},{2,0},{3,1},{16,18},{17,19},{18,16},{19,17},{4,6},{5,7... | collective-permute-start | bytes 3272 | tf_op jit(solution)/shard_map/ppermute | solution.py:52
  33.3 26.4 %collective-permute-start.3 = (bf16[256,4096]{1,0:T(8,128)(2,1)}, bf16[256,4096]{1,0:T(8,128)(2,1)}, u32[]{:S(2)}, u32[]{:S(2)}) collective-permute-start(bf16[256,4096]{1,0:T(8,128)(2,1)} %refs_0_.1), channel_id=1, source_target_pairs={{0,3},{1,0},{2,1},{3,2},{16,17},{17,18},{18,19},{19,16},{4,7},{5,4... | collective-permute-start | bytes 6291464 | tf_op jit(solution)/shard_map/ppermute | solution.py:52
  36.4 16.1 %collective-permute-start.8 = (bf16[2,512,512]{2,1,0:T(8,128)(2,1)S(1)}, bf16[2,512,512]{2,1,0:T(8,128)(2,1)}, u32[]{:S(2)}, u32[]{:S(2)}) collective-permute-start(bf16[2,512,512]{2,1,0:T(8,128)(2,1)S(1)} %pad_maximum_fusion.1.refs_3_), channel_id=1, source_target_pairs={{0,4},{1,5},{2,6},{3,7},{4,8},{5,9},{6,10},{7,11},{8,12},{9,13},{1... | collective-permute-start | bytes 3145736 | tf_op jit(solution)/shard_map/ppermute | solution.py:44
  36.5 26.9 %copy-start.1 = (bf16[2,512,512]{2,1,0:T(8,128)(2,1)}, bf16[2,512,512]{2,1,0:T(8,128)(2,1)S(1)}, u32[]{:S(2)}) copy-start(bf16[2,512,512]{2,1,0:T(8,128)(2,1)S(1)} %collective-permute-done.7.refs_4_) | copy-start | bytes 3145732
  36.5 16.1 %collective-permute-start.9 = (bf16[2,512,512]{2,1,0:T(8,128)(2,1)S(1)}, bf16[2,512,512]{2,1,0:T(8,128)(2,1)}, u32[]{:S(2)}, u32[]{:S(2)}) collective-permute-start(bf16[2,512,512]{2,1,0:T(8,128)(2,1)S(1)} %pad_maximum_fusion.refs_2_), channel_id=1, source_target_pairs={{0,12},{1,13},{2,14},{3,15},{4,0},{5,1},{6,2},{7,3},{8,4},{9,5},{1... | collective-permute-start | bytes 3145736 | tf_op jit(solution)/shard_map/ppermute | solution.py:44
  40.7 22.7 %collective-permute-start.13 = (bf16[2,512,512]{2,1,0:T(8,128)(2,1)}, bf16[2,512,512]{2,1,0:T(8,128)(2,1)}, u32[]{:S(2)}, u32[]{:S(2)}) collective-permute-start(bf16[2,512,512]{2,1,0:T(8,128)(2,1)} %collective-permute-done.10.refs_7_), channel_id=1, source_target_pairs={{0,12},{1,13},{2,14},{3,15},{4,0},{5,1},{6,2},{7,3},{8,4},{9,5},{1... | collective-permute-start | bytes 3145736 | tf_op jit(solution)/shard_map/ppermute | solution.py:44
  41.6 22.2 %collective-permute-start.12 = (bf16[2,512,512]{2,1,0:T(8,128)(2,1)}, bf16[2,512,512]{2,1,0:T(8,128)(2,1)}, u32[]{:S(2)}, u32[]{:S(2)}) collective-permute-start(bf16[2,512,512]{2,1,0:T(8,128)(2,1)} %shard_map.48), channel_id=1, source_target_pairs={{0,4},{1,5},{2,6},{3,7},{4,8},{5,9},{6,10},{7,11},{8,12},{9,13},{1... | collective-permute-start | bytes 3145736 | tf_op jit(solution)/shard_map/ppermute | solution.py:44
  52.6 14.2 %collective-permute-start.15 = (bf16[2,512,512]{2,1,0:T(8,128)(2,1)S(1)}, bf16[2,512,512]{2,1,0:T(8,128)(2,1)}, u32[]{:S(2)}, u32[]{:S(2)}) collective-permute-start(bf16[2,512,512]{2,1,0:T(8,128)(2,1)S(1)} %pad_maximum_fusion.1.refs_3_), channel_id=1, source_target_pairs={{0,16},{16,0},{1,17},{17,1},{2,18},{18,2},{3,19},{19,3},{4,20},{20... | collective-permute-start | bytes 3145736 | tf_op jit(solution)/shard_map/ppermute | solution.py:60
  52.6 14.3 %collective-permute-start.14 = (bf16[2,512,512]{2,1,0:T(8,128)(2,1)S(1)}, bf16[2,512,512]{2,1,0:T(8,128)(2,1)}, u32[]{:S(2)}, u32[]{:S(2)}) collective-permute-start(bf16[2,512,512]{2,1,0:T(8,128)(2,1)S(1)} %pad_maximum_fusion.refs_2_), channel_id=1, source_target_pairs={{0,16},{16,0},{1,17},{17,1},{2,18},{18,2},{3,19},{19,3},{4,20},{20... | collective-permute-start | bytes 3145736 | tf_op jit(solution)/shard_map/ppermute | solution.py:60
  59.7 7.7 %collective-permute-start.19 = (bf16[2,512,512]{2,1,0:T(8,128)(2,1)}, bf16[2,512,512]{2,1,0:T(8,128)(2,1)}, u32[]{:S(2)}, u32[]{:S(2)}) collective-permute-start(bf16[2,512,512]{2,1,0:T(8,128)(2,1)} %collective-permute-done.10.refs_7_), channel_id=1, source_target_pairs={{0,16},{16,0},{1,17},{17,1},{2,18},{18,2},{3,19},{19,3},{4,20},{20... | collective-permute-start | bytes 3145736 | tf_op jit(solution)/shard_map/ppermute | solution.py:60
  63.4 4.1 %collective-permute-start.16 = (bf16[2,512,512]{2,1,0:T(8,128)(2,1)S(1)}, bf16[2,512,512]{2,1,0:T(8,128)(2,1)}, u32[]{:S(2)}, u32[]{:S(2)}) collective-permute-start(bf16[2,512,512]{2,1,0:T(8,128)(2,1)S(1)} %collective-permute-done.7.refs_4_), channel_id=1, source_target_pairs={{0,16},{16,0},{1,17},{17,1},{2,18},{18,2},{3,19},{19,3},{4,20},{20... | collective-permute-start | bytes 3145736 | tf_op jit(solution)/shard_map/ppermute | solution.py:60
  63.8 30.0 %collective-permute-start.24 = (bf16[256,4096]{1,0:T(8,128)(2,1)}, bf16[256,4096]{1,0:T(8,128)(2,1)}, u32[]{:S(2)}, u32[]{:S(2)}) collective-permute-start(bf16[256,4096]{1,0:T(8,128)(2,1)} %collective-permute-done.2.refs_0_), channel_id=1, source_target_pairs={{0,1},{1,2},{2,3},{3,0},{16,19},{17,16},{18,17},{19,18},{4,5},{5,6... | collective-permute-start | bytes 6291464 | tf_op jit(solution)/shard_map/ppermute | solution.py:52
  66.7 3.6 %collective-permute-start.17 = (bf16[2,512,512]{2,1,0:T(8,128)(2,1)}, bf16[2,512,512]{2,1,0:T(8,128)(2,1)S(1)}, u32[]{:S(2)}, u32[]{:S(2)}) collective-permute-start(bf16[2,512,512]{2,1,0:T(8,128)(2,1)} %collective-permute-done.8.refs_5_), channel_id=1, source_target_pairs={{0,16},{16,0},{1,17},{17,1},{2,18},{18,2},{3,19},{19,3},{4,20},{20... | collective-permute-start | bytes 3145736 | tf_op jit(solution)/shard_map/ppermute | solution.py:60
  66.8 5.8 %collective-permute-start.18 = (bf16[2,512,512]{2,1,0:T(8,128)(2,1)}, bf16[2,512,512]{2,1,0:T(8,128)(2,1)S(1)}, u32[]{:S(2)}, u32[]{:S(2)}) collective-permute-start(bf16[2,512,512]{2,1,0:T(8,128)(2,1)} %collective-permute-done.9.refs_6_), channel_id=1, source_target_pairs={{0,16},{16,0},{1,17},{17,1},{2,18},{18,2},{3,19},{19,3},{4,20},{20... | collective-permute-start | bytes 3145736 | tf_op jit(solution)/shard_map/ppermute | solution.py:60
  67.3 5.5 %collective-permute-start.21 = (bf16[2,512,512]{2,1,0:T(8,128)(2,1)}, bf16[2,512,512]{2,1,0:T(8,128)(2,1)}, u32[]{:S(2)}, u32[]{:S(2)}) collective-permute-start(bf16[2,512,512]{2,1,0:T(8,128)(2,1)} %shard_map.51.refs_9_), channel_id=1, source_target_pairs={{0,16},{16,0},{1,17},{17,1},{2,18},{18,2},{3,19},{19,3},{4,20},{20... | collective-permute-start | bytes 3145736 | tf_op jit(solution)/shard_map/ppermute | solution.py:60
  67.4 6.7 %collective-permute-start.20 = (bf16[2,512,512]{2,1,0:T(8,128)(2,1)}, bf16[2,512,512]{2,1,0:T(8,128)(2,1)S(1)}, u32[]{:S(2)}, u32[]{:S(2)}) collective-permute-start(bf16[2,512,512]{2,1,0:T(8,128)(2,1)} %shard_map.50.refs_8_), channel_id=1, source_target_pairs={{0,16},{16,0},{1,17},{17,1},{2,18},{18,2},{3,19},{19,3},{4,20},{20... | collective-permute-start | bytes 3145736 | tf_op jit(solution)/shard_map/ppermute | solution.py:60
  91.1 3.9 %collective-permute-start.22 = (f32[3,256]{1,0:T(4,128)}, f32[3,256]{1,0:T(4,128)S(1)}, u32[]{:S(2)}, u32[]{:S(2)}) collective-permute-start(f32[3,256]{1,0:T(4,128)} %get-tuple-element.10), channel_id=1, source_target_pairs={{0,3},{1,0},{2,1},{3,2},{16,17},{17,18},{18,19},{19,16},{4,7},{5,4... | collective-permute-start | bytes 9224 | tf_op jit(solution)/shard_map/ppermute | solution.py:52
  92.1 5.0 %collective-permute-start.23 = (f32[3,256]{1,0:T(4,128)}, f32[3,256]{1,0:T(4,128)S(1)}, u32[]{:S(2)}, u32[]{:S(2)}) collective-permute-start(f32[3,256]{1,0:T(4,128)} %get-tuple-element.11), channel_id=1, source_target_pairs={{0,1},{1,2},{2,3},{3,0},{16,19},{17,16},{18,17},{19,18},{4,5},{5,6... | collective-permute-start | bytes 9224 | tf_op jit(solution)/shard_map/ppermute | solution.py:52
  108.5 5.4 %collective-permute-start.25 = (f32[3,256]{1,0:T(4,128)}, f32[3,256]{1,0:T(4,128)S(1)}, u32[]{:S(2)}, u32[]{:S(2)}) collective-permute-start(f32[3,256]{1,0:T(4,128)} %get-tuple-element.14), channel_id=1, source_target_pairs={{0,2},{1,3},{2,0},{3,1},{16,18},{17,19},{18,16},{19,17},{4,6},{5,7... | collective-permute-start | bytes 9224 | tf_op jit(solution)/shard_map/ppermute | solution.py:52
  (13 other events, 27.1 us)

commit v3 on v2

v3 whole, which is shorter than its diff:
```python
import functools

import jax
import jax.numpy as jnp
from jax import lax
from jax.experimental import pallas as pl
from jax.experimental.pallas import tpu as pltpu
from jax.sharding import Mesh
from jax.sharding import PartitionSpec as P

QROWS = 128
PBLK = 256
LISTED = 8
SOURCES = 4
PIECES = 5
RING = 4
PACE_F = 2
PACE_M, PACE_A, PACE_B = 3, 2, 8
AXES = ("z", "core", "y", "x")
VMEM = 60 * 1024 * 1024
REL = (0, -1, 1, 2)


def ring(axis, step):
    return [(i, (i + step) % RING) for i in range(RING)]


def shift(array, axis, step):
    return lax.ppermute(array, axis, ring(axis, step))


def device(z, core, y, x):
    return ((z * 2 + core) * RING + y) * RING + x


def shift_zy(array, first, step):
    pairs = []
    for z in range(RING):
        for core in range(2):
            for y in range(RING):
                for x in range(RING):
                    along_z = (core == 0) == first
                    to_z = (z + step) % RING if along_z else z
                    to_y = y if along_z else (y + step) % RING
                    pairs.append((device(z, core, y, x), device(to_z, core, to_y, x)))
    return lax.ppermute(array, AXES, pairs)


def shift_x(array, step):
    pairs = []
    for core in range(2):
        for x in range(RING):
            pairs.append((core * RING + x, core * RING + (x + (1 - 2 * core) * step) % RING))
    return lax.ppermute(array, ("core", "x"), pairs)


def both(array):
    return array, swap(array)


def swap(array):
    return lax.ppermute(array, "core", [(0, 1), (1, 0)])


def token(arrays, us):
    def kernel(*refs):
        refs[-1][...] = jnp.zeros_like(refs[-1])

    return pl.pallas_call(
        kernel,
        out_shape=jax.ShapeDtypeStruct((8, 128), jnp.float32),
        in_specs=[pl.BlockSpec(memory_space=pl.ANY)] * len(arrays),
        out_specs=pl.BlockSpec(memory_space=pltpu.VMEM),
        compiler_params=pltpu.CompilerParams(vmem_limit_bytes=VMEM),
        cost_estimate=pl.CostEstimate(
            flops=int(us * 1.15e9), bytes_accessed=0, transcendentals=0
        ),
    )(*arrays)


def after(array, tokens):
    def kernel(*refs):
        pass

    anywhere = pl.BlockSpec(memory_space=pl.ANY)
    return pl.pallas_call(
        kernel,
        out_shape=jax.ShapeDtypeStruct(array.shape, array.dtype),
        in_specs=[anywhere] * (1 + len(tokens)),
        out_specs=anywhere,
        input_output_aliases={0: 0},
        compiler_params=pltpu.CompilerParams(vmem_limit_bytes=VMEM),
        cost_estimate=pl.CostEstimate(flops=1000, bytes_accessed=0, transcendentals=0),
    )(array, *tokens)


def take(array, start, tokens):
    def kernel(ref, *refs):
        out, buf, sems = refs[-3:]
        loads, stores = [], []
        for n in range(2):
            loads.append(pltpu.make_async_copy(ref.at[start + n], buf.at[n], sems.at[n]))
            stores.append(pltpu.make_async_copy(buf.at[n], out.at[n], sems.at[2 + n]))
            loads[n].start()
        for n in range(2):
            loads[n].wait()
            stores[n].start()
        for n in range(2):
            stores[n].wait()

    anywhere = pl.BlockSpec(memory_space=pl.ANY)
    return pl.pallas_call(
        kernel,
        out_shape=jax.ShapeDtypeStruct((2, *array.shape[1:]), array.dtype),
        in_specs=[anywhere] * (1 + len(tokens)),
        out_specs=anywhere,
        scratch_shapes=[pltpu.VMEM((2, *array.shape[1:]), array.dtype), pltpu.SemaphoreType.DMA((4,))],
        compiler_params=pltpu.CompilerParams(vmem_limit_bytes=VMEM),
        cost_estimate=pl.CostEstimate(flops=1000, bytes_accessed=0, transcendentals=0),
    )(array, *tokens)


def score_kernel(extra, scale, info, lists, positive, *refs):
    refs = list(refs)
    queries = [refs.pop(0) for _ in range(SOURCES)]
    pieces = [[refs.pop(0) for _ in range(PIECES)] for _ in range(2)]
    del refs[:extra]
    outs, q_all, p_buf, a_sem, p_sem = refs
    me_z, me_core, me_y, me_x = (info[k] for k in range(4))
    feats = p_buf.shape[2] // 8

    def turn(value, step):
        return lax.rem(value + step + RING, RING)

    def any_of(s, block, test):
        found = test(lists[s, block * LISTED])
        for n in range(1, LISTED):
            found = jnp.logical_or(found, test(lists[s, block * LISTED + n]))
        return found

    def load_passages(k, source):
        g = lax.rem(me_core + source, 2)
        for which in range(2):
            @pl.when(g == which)
            def _():
                for m in range(RING):
                    i, j = (k, m) if source == 0 else (m, k)
                    column = pl.multiple_of((turn(me_z, REL[m]) * 2 + source) * feats, feats)
                    n, at = (i, j) if i < 3 else (3 + j // 2, j % 2)
                    pltpu.make_async_copy(
                        pieces[which][n].at[at], p_buf.at[k, :, pl.ds(column, feats)], p_sem.at[k]
                    ).start()

    def load_slot(k):
        for source in range(2):
            load_passages(k, source)

    def load_pair(pair):
        for s in pair:
            pltpu.make_async_copy(queries[s], q_all.at[s], a_sem.at[s]).start()

    load_slot(0)
    load_pair((0, 1))
    load_pair((2, 3))
    load_slot(1)

    def owner_of(k):
        return turn(me_y, jnp.where(k == 3, 2, jnp.where(k == 2, 1, -k))) * RING + me_x

    def choose(k, s):
        owner = owner_of(k)
        block = any_of(s, 1, lambda b: lax.shift_right_arithmetic(b, 1) == owner)
        block = block.astype(jnp.int32)
        return block, pl.ds(pl.multiple_of(block * QROWS, QROWS), QROWS)

    rows = lax.broadcasted_iota(jnp.int32, outs.shape, 1)
    outs[...] = jnp.where(rows == 0, -1e30, 0.0).astype(jnp.float32)
    def multiply(k, pair):
        index = lax.broadcasted_iota(jnp.int32, (PBLK, 2 * QROWS), 0)
        left = lax.broadcasted_iota(jnp.int32, (1, 2 * QROWS), 1) < QROWS
        owner = owner_of(k)
        chosen, lanes = zip(*[choose(k, s) for s in pair])
        listed = []
        for b in range(2):
            sides = [
                any_of(s, block, lambda v: v == owner * 2 + b).astype(jnp.int32)
                for s, block in zip(pair, chosen)
            ]
            listed.append(jnp.where(left, sides[0], sides[1]) > 0)
        rows = jnp.concatenate([q_all[s, part, :] for s, part in zip(pair, lanes)], axis=0)
        scores = lax.dot_general(
            p_buf[k], rows, (((1,), (1,)), ((), ())), preferred_element_type=jnp.float32
        ) * scale

        def get(row):
            found = [outs[s, row : row + 1, part] for s, part in zip(pair, lanes)]
            return jnp.concatenate(found, axis=1)

        wanted = jnp.concatenate(
            [positive[s, :, part] for s, part in zip(pair, lanes)], axis=1
        )
        old = get(0)
        halves = [scores[:PBLK], scores[PBLK:]]
        top = old
        for b in range(2):
            peak = jnp.max(halves[b], axis=0, keepdims=True)
            top = jnp.where(listed[b], jnp.maximum(top, peak), top)
        total = get(1) * jnp.exp(old - top)
        hits = get(2)
        for b in range(2):
            here = jnp.sum(jnp.exp(halves[b] - top), axis=0, keepdims=True)
            total = total + jnp.where(listed[b], here, 0.0)
            place = wanted - (owner * 2 + b) * PBLK
            hits = hits + jnp.sum(jnp.where(index == place, halves[b], 0.0), axis=0, keepdims=True)
        for n, (s, part) in enumerate(zip(pair, lanes)):
            side = slice(n * QROWS, (n + 1) * QROWS)
            outs[s, 0:1, part] = top[:, side]
            outs[s, 1:2, part] = total[:, side]
            outs[s, 2:3, part] = hits[:, side]

    @pl.loop(0, 2 * RING)
    def _(step):
        k, second = step // 2, lax.rem(step, 2)
        pair = (second * 2, second * 2 + 1)

        @pl.when(second == 0)
        def _():
            pltpu.make_async_copy(p_buf.at[k], p_buf.at[k], p_sem.at[k]).wait()
            for later in range(2, RING):
                @pl.when(k + 2 == later)
                def _():
                    load_slot(later)

        @pl.when(k == 0)
        def _():
            for s in pair:
                pltpu.make_async_copy(q_all.at[s], q_all.at[s], a_sem.at[s]).wait()

        multiply(k, pair)


def score(info, lists, positive, queries, pieces, extra=()):
    rows, features = queries[0].shape
    flat = list(queries) + [a for arrays in pieces for a in arrays]
    flat += list(extra)
    smem, vmem = pl.BlockSpec(memory_space=pltpu.SMEM), pl.BlockSpec(memory_space=pltpu.VMEM)
    anywhere = pl.BlockSpec(memory_space=pl.ANY)
    stats = jax.ShapeDtypeStruct((SOURCES, 3, rows), jnp.float32)
    return pl.pallas_call(
        functools.partial(score_kernel, len(extra), float(features) ** -0.5),
        out_shape=stats,
        in_specs=[smem, smem, vmem] + [anywhere] * len(flat),
        out_specs=vmem,
        scratch_shapes=[
            pltpu.VMEM((SOURCES, rows, features), jnp.bfloat16),
            pltpu.VMEM((RING, 2 * PBLK, features), jnp.bfloat16),
            pltpu.SemaphoreType.DMA((SOURCES,)),
            pltpu.SemaphoreType.DMA((RING,)),
        ],
        compiler_params=pltpu.CompilerParams(vmem_limit_bytes=VMEM),
        cost_estimate=pl.CostEstimate(flops=1000000, bytes_accessed=0, transcendentals=0),
    )(info, lists, positive, *flat)


def finish(stats):
    top, total, chosen = stats[:, 0], stats[:, 1], stats[:, 2]
    peak = jnp.max(top, axis=0)
    summed = jnp.sum(total * jnp.exp(top - peak[None, :]), axis=0)
    return peak + jnp.log(summed) - jnp.sum(chosen, axis=0)


def body(queries, passages, lists, positive):
    info = jnp.stack([lax.axis_index(a) for a in AXES]).astype(jnp.int32)

    size, slots = positive.shape[0], lists.size
    meta = jnp.pad(positive, (0, slots)) + jnp.pad(lists.reshape(-1), (size, 0))
    ahead, behind = shift_x(queries, 1), shift_x(queries, -1)
    ahead = after(ahead, [token([behind], PACE_B)])
    far = shift_x(ahead, 1)
    meta_a = shift_x(meta, 1)
    meta_f = shift_x(meta_a, 1)
    meta_b = shift_x(meta_f, 1)

    s = jnp.stack([passages] + [shift_zy(passages, True, step) for step in (1, -1, 2)])
    s = after(s, [token([meta_b, meta_f, meta_a], PACE_M)])
    pr, pl_ = shift_zy(s, False, 1), shift_zy(s, False, -1)
    sides = [both(s)]
    gate = token([sides[0][1]], PACE_A)
    fr = shift_zy(take(pr, 0, [gate]), False, 1)
    fl = shift_zy(take(pl_, 2, [gate]), False, -1)
    sides += [both(a) for a in (pr, pl_, fr, fl)]
    pieces = [[a for a, _ in sides], [b for _, b in sides]]

    metas = [meta, meta_a, meta_b, meta_f]
    wanted = jnp.stack([m[None, :size] for m in metas])
    ids = jnp.stack([m[size:] for m in metas])
    info = after(info, [token([far], PACE_F)])
    stats = score(info, ids, wanted, [queries, ahead, behind, far], pieces)
    back = [shift_x(a, step) for a, step in zip(stats[1:], (-1, 1, 2))]
    return finish(jnp.stack([stats[0]] + back))


def solution(mesh):
    fine = Mesh(mesh.devices.reshape(RING, 2, RING, RING), AXES)
    everywhere = ("z", "core", "y", "x")
    return jax.shard_map(
        body,
        mesh=fine,
        in_specs=(
            P(everywhere, None),
            P(("y", "x"), ("z", "core")),
            P(everywhere, None),
            P(everywhere),
        ),
        out_specs=P(everywhere),
        check_vma=False,
    )
```

time: 116 us -> 111 us (0.957)
  starting transfers between devices: 34.3 us -> 20.1 us
  waiting for transfers between devices: 43.3 us -> 54.9 us
  Pallas kernels: 28.4 us -> 24.2 us
  local copies, waits for them, and re-layouts: 3.43 us -> 4.71 us
    ppermute x9, waiting for transfers between devices: 16 us -> 38.5 us  [shift_x(): return lax.ppermute(array, ('core', 'x'), pairs)]
    ppermute x9, starting transfers between devices: 15.6 us -> 6.16 us  [shift_x(): return lax.ppermute(array, ('core', 'x'), pairs)]
    ppermute x9 -> x7, waiting for transfers between devices: 23.5 us -> 16.4 us  [shift_zy(): return lax.ppermute(array, AXES, pairs)]
    pallas_call x2 -> x3, Pallas kernels: 26.7 us -> 21.8 us  [the longest x1 17.7 us: score(): pl.pallas_call(functools.partial(score_kernel, len(extra), float(features...]
    ppermute x9 -> x7, starting transfers between devices: 17.2 us -> 13.4 us  [shift_zy(): return lax.ppermute(array, AXES, pairs)]
    ppermute x8 -> x5, waiting for transfers between devices: 3.8 us -> 0.01 us  [swap(): return lax.ppermute(array, 'core', [(0, 1), (1, 0)])]
    pallas_call x3 -> x4, Pallas kernels: 1.77 us -> 2.37 us  [token(): pl.pallas_call(kernel, out_shape=jax.ShapeDtypeStruct((8, 128), jnp.float...]
    another operation x6 -> x3, other arithmetic: 3.59 us -> 3.8 us  [the longest x1 2.61 us: body(): jnp.stack([passages] + [shift_zy(passages, True, step) for step in (1, -1...]
  transfers between devices with their start and end apart: 26 -> 21, of which waited for: 15 -> 10; matrix products, arithmetic and copies ran while one was open for 5% -> 5% of each run, Pallas kernels for 15% -> 6%
where the time goes in v3:
time: 111 us; the launch traced here: 110 us
  waiting for transfers between devices  54.9 us (49%)
  Pallas kernels  24.2 us (22%)
  starting transfers between devices  20.1 us (18%)
  other arithmetic  5.71 us (5%)
  local copies, waits for them, and re-layouts  4.71 us (4%)
    ppermute x9, waiting for transfers between devices, shift_x(): return lax.ppermute(array, ('core', 'x'), pairs)  38.5 us
    pallas_call x1, Pallas kernels, score(): pl.pallas_call(functools.partial(score_kernel, len(extra), float(features...  17.7 us
    ppermute x7, waiting for transfers between devices, shift_zy(): return lax.ppermute(array, AXES, pairs)  16.4 us
    ppermute x7, starting transfers between devices, shift_zy(): return lax.ppermute(array, AXES, pairs)  13.4 us
    ppermute x9, starting transfers between devices, shift_x(): return lax.ppermute(array, ('core', 'x'), pairs)  6.16 us
    pallas_call x2, Pallas kernels, take(): pl.pallas_call(kernel, out_shape=jax.ShapeDtypeStruct((2, *array.shape[1:...  4.16 us
    unnamed x20, local copies, waits for them, and re-layouts  3.23 us
    another operation x1, other arithmetic, body(): jnp.stack([passages] + [shift_zy(passages, True, step) for step in (1, -1...  2.61 us
  transfers between devices with their start and end apart: 21, of which 10 were waited for; matrix products, arithmetic and copies ran while one was open for 5% of the time, Pallas kernels for 6%

profile of v3, /device:TPU:0, one launch (start us, length us, event | category | flops | bytes accessed | tf_op | source)
XLA Modules:
  0.0 109.8 jit_solution(17295823221462967123)
XLA Ops:
  0.0 2.8 %collective-permute-start.1 = (bf16[256,4096]{1,0:T(8,128)(2,1)}, bf16[256,4096]{1,0:T(8,128)(2,1)}, u32[]{:S(2)}, u32[]{:S(2)}) collective-permute-start(bf16[256,4096]{1,0:T(8,128)(2,1)} %refs_0_.1), channel_id=1, source_target_pairs={{0,3},{1,0},{2,1},{3,2},{16,17},{17,18},{18,19},{19,16},{4,7},{5,4... | collective-permute-start | bytes 6291464 | tf_op jit(solution)/shard_map/ppermute | solution.py:54
  2.8 1.9 %collective-permute-start.6 = (bf16[512,512]{1,0:T(8,128)(2,1)}, bf16[512,512]{1,0:T(8,128)(2,1)S(1)}, u32[]{:S(2)}, u32[]{:S(2)}) collective-permute-start(bf16[512,512]{1,0:T(8,128)(2,1)} %param.5), channel_id=1, source_target_pairs={{0,32},{1,33},{2,34},{3,35},{4,36},{5,37},{6,38},{7,39},{8,40},{9,... | collective-permute-start | bytes 1572872 | tf_op jit(solution)/shard_map/ppermute | solution.py:46
  4.8 3.6 %collective-permute-start.8 = (bf16[512,512]{1,0:T(8,128)(2,1)}, bf16[512,512]{1,0:T(8,128)(2,1)S(1)}, u32[]{:S(2)}, u32[]{:S(2)}) collective-permute-start(bf16[512,512]{1,0:T(8,128)(2,1)} %param.5), channel_id=1, source_target_pairs={{0,64},{1,65},{2,66},{3,67},{4,68},{5,69},{6,70},{7,71},{8,72},{9,... | collective-permute-start | bytes 1572872 | tf_op jit(solution)/shard_map/ppermute | solution.py:46
  8.3 1.0 collective-permute-start.7
  9.4 0.8 reshape.4
  10.1 0.7 pad_add_fusion.2
  10.8 4.9 %collective-permute-done.3.refs_2_ = s32[272]{0:T(512)S(1)} collective-permute-done((s32[272]{0:T(512)S(1)}, s32[272]{0:T(512)S(1)}, u32[]{:S(2)}, u32[]{:S(2)}) %collective-permute-start.3) | collective-permute-done | bytes 1120 | tf_op jit(solution)/shard_map/ppermute | solution.py:54
  15.7 4.9 %collective-permute-done.4.refs_1_ = s32[272]{0:T(512)S(1)} collective-permute-done((s32[272]{0:T(512)S(1)}, s32[272]{0:T(512)S(1)}, u32[]{:S(2)}, u32[]{:S(2)}) %collective-permute-start.4) | collective-permute-done | bytes 1120 | tf_op jit(solution)/shard_map/ppermute | solution.py:54
  20.6 4.9 %collective-permute-done.5.refs_0_ = s32[272]{0:T(512)S(1)} collective-permute-done((s32[272]{0:T(512)S(1)}, s32[272]{0:T(512)S(1)}, u32[]{:S(2)}, u32[]{:S(2)}) %collective-permute-start.5) | collective-permute-done | bytes 1120 | tf_op jit(solution)/shard_map/ppermute | solution.py:54
  26.0 0.6 shard_map.50.refs_1_
  26.7 2.6 %pad_maximum_fusion.refs_0_ = bf16[4,512,512]{2,1,0:T(8,128)(2,1)} fusion(bf16[1,512,512]{2,1,0:T(8,128)(2,1)S(1)} %bitcast.43, bf16[1,512,512]{2,1,0:T(8,128)(2,1)} %bitcast.14, bf16[1,512,512]{2,1,0:T(8,128)(2,1)S(1)} %bitcast.42, bf16[1,512,512]{2,1,0:T(8,128)(2,1)S(1)} %bitcast.41), kind=kLoop, calls=%fused_computation | loop fusion | flops 3145728 | bytes 4194304 | tf_op jit(solution)/shard_map/stack | solution.py:284
  29.3 3.0 %collective-permute-start.10 = (bf16[4,512,512]{2,1,0:T(8,128)(2,1)}, bf16[4,512,512]{2,1,0:T(8,128)(2,1)}, u32[]{:S(2)}, u32[]{:S(2)}) collective-permute-start(bf16[4,512,512]{2,1,0:T(8,128)(2,1)} %shard_map.51.refs_4_), channel_id=1, source_target_pairs={{0,12},{1,13},{2,14},{3,15},{4,0},{5,1},{6,2},{7,3},{8,4},{9,5},{1... | collective-permute-start | bytes 6291464 | tf_op jit(solution)/shard_map/ppermute | solution.py:46
  32.3 0.6 shard_map.46.refs_1_
  32.9 20.0 %collective-permute-done.refs_0_ = bf16[256,4096]{1,0:T(8,128)(2,1)S(1)} collective-permute-done((bf16[256,4096]{1,0:T(8,128)(2,1)}, bf16[256,4096]{1,0:T(8,128)(2,1)S(1)}, u32[]{:S(2)}, u32[]{:S(2)}) %collective-permute-start) | collective-permute-done | bytes 2097184 | tf_op jit(solution)/shard_map/ppermute | solution.py:54
  52.9 1.3 %copy-done = bf16[256,4096]{1,0:T(8,128)(2,1)} copy-done((bf16[256,4096]{1,0:T(8,128)(2,1)}, bf16[256,4096]{1,0:T(8,128)(2,1)S(1)}, u32[]{:S(2)}) %copy-start) | copy-done | bytes 2097176
  54.2 0.6 shard_map.52.refs_0_
  54.8 1.3 %collective-permute-done.10.ref.refs_6_ = bf16[4,512,512]{2,1,0:T(8,128)(2,1)} collective-permute-done((bf16[4,512,512]{2,1,0:T(8,128)(2,1)}, bf16[4,512,512]{2,1,0:T(8,128)(2,1)}, u32[]{:S(2)}, u32[]{:S(2)}) %collective-permute-start.10) | collective-permute-done | bytes 2097184 | tf_op jit(solution)/shard_map/ppermute | solution.py:46
  56.2 2.1 %shard_map.54 = bf16[2,512,512]{2,1,0:T(8,128)(2,1)} custom-call(bf16[4,512,512]{2,1,0:T(8,128)(2,1)} %collective-permute-done.10.ref.refs_6_, f32[8,128]{1,0:T(8,128)} %shard_map.52.refs_0_), custom_call_target="tpu_custom_call" | custom-call | flops 1000 | tf_op jit(solution)/shard_map/pallas_call | solution.py:112
  58.3 3.8 %collective-permute-start.13 = (bf16[2,512,512]{2,1,0:T(8,128)(2,1)}, bf16[2,512,512]{2,1,0:T(8,128)(2,1)S(1)}, u32[]{:S(2)}, u32[]{:S(2)}) collective-permute-start(bf16[2,512,512]{2,1,0:T(8,128)(2,1)} %shard_map.54), channel_id=1, source_target_pairs={{0,12},{1,13},{2,14},{3,15},{4,0},{5,1},{6,2},{7,3},{8,4},{9,5},{1... | collective-permute-start | bytes 3145736 | tf_op jit(solution)/shard_map/ppermute | solution.py:46
  62.0 2.1 %shard_map.53 = bf16[2,512,512]{2,1,0:T(8,128)(2,1)} custom-call(bf16[4,512,512]{2,1,0:T(8,128)(2,1)} %collective-permute-done.9.ref.refs_5_, f32[8,128]{1,0:T(8,128)} %shard_map.52.refs_0_), custom_call_target="tpu_custom_call" | custom-call | flops 1000 | tf_op jit(solution)/shard_map/pallas_call | solution.py:112
  64.8 0.6 pad_add_fusion.3.refs_0_
  65.4 9.2 %collective-permute-done.13.refs_8_ = bf16[2,512,512]{2,1,0:T(8,128)(2,1)S(1)} collective-permute-done((bf16[2,512,512]{2,1,0:T(8,128)(2,1)}, bf16[2,512,512]{2,1,0:T(8,128)(2,1)S(1)}, u32[]{:S(2)}, u32[]{:S(2)}) %collective-permute-start.13) | collective-permute-done | bytes 1048608 | tf_op jit(solution)/shard_map/ppermute | solution.py:46
  74.7 5.9 %collective-permute-done.12.refs_7_ = bf16[2,512,512]{2,1,0:T(8,128)(2,1)} collective-permute-done((bf16[2,512,512]{2,1,0:T(8,128)(2,1)}, bf16[2,512,512]{2,1,0:T(8,128)(2,1)}, u32[]{:S(2)}, u32[]{:S(2)}) %collective-permute-start.12) | collective-permute-done | bytes 1048608 | tf_op jit(solution)/shard_map/ppermute | solution.py:46
  80.6 0.6 pad_add_fusion.positive
  81.7 1.3 %copy-done.1 = bf16[256,4096]{1,0:T(8,128)(2,1)} copy-done((bf16[256,4096]{1,0:T(8,128)(2,1)}, bf16[256,4096]{1,0:T(8,128)(2,1)S(1)}, u32[]{:S(2)}) %copy-start.1) | copy-done | bytes 2097176
  83.0 0.6 shard_map.48.refs_1_
  83.6 0.6 pad_add_fusion.1.lists
  84.2 17.7 %shard_map.55 = f32[4,3,256]{2,1,0:T(4,128)} custom-call(s32[4]{0:T(128)} %shard_map.49.info, s32[4,16]{1,0:T(4,128)} %pad_add_fusion.1.lists, s32[4,1,256]{2,1,0:T(1,128)} %pad_add_fusion.positive, bf16[256,4096]{1,0:T(8,128)(2,1)} %refs_0_.1, bf16[256,4096]{1,0:T(8,128)(2,1)} %shard_map.47.refs_1_, ...), custom_call_target="tpu_custom_call" | custom-call | flops 1000000 | tf_op jit(solution)/shard_map/pallas_call | solution.py:249
  101.9 0.7 fusion.6
  102.6 3.0 %collective-permute-start.19 = (f32[3,256]{1,0:T(4,128)S(1)}, f32[3,256]{1,0:T(4,128)S(1)}, u32[]{:S(2)}, u32[]{:S(2)}) collective-permute-start(f32[3,256]{1,0:T(4,128)S(1)} %get-tuple-element.11), channel_id=1, source_target_pairs={{0,1},{1,2},{2,3},{3,0},{16,19},{17,16},{18,17},{19,18},{4,5},{5,6... | collective-permute-start | bytes 9224 | tf_op jit(solution)/shard_map/ppermute | solution.py:54
  105.9 1.8 %collective-permute-done.20 = f32[3,256]{1,0:T(4,128)S(1)} collective-permute-done((f32[3,256]{1,0:T(4,128)S(1)}, f32[3,256]{1,0:T(4,128)S(1)}, u32[]{:S(2)}, u32[]{:S(2)}) %collective-permute-start.20) | collective-permute-done | bytes 3104 | tf_op jit(solution)/shard_map/ppermute | solution.py:54
  107.7 1.5 %collective-permute-done.18 = f32[3,256]{1,0:T(4,128)S(1)} collective-permute-done((f32[3,256]{1,0:T(4,128)S(1)}, f32[3,256]{1,0:T(4,128)S(1)}, u32[]{:S(2)}, u32[]{:S(2)}) %collective-permute-start.18) | collective-permute-done | bytes 3104 | tf_op jit(solution)/shard_map/ppermute | solution.py:54
  (59 shorter events, 2.8 us)
Async XLA Ops:
  0.0 32.3 %collective-permute-start.1 = (bf16[256,4096]{1,0:T(8,128)(2,1)}, bf16[256,4096]{1,0:T(8,128)(2,1)}, u32[]{:S(2)}, u32[]{:S(2)}) collective-permute-start(bf16[256,4096]{1,0:T(8,128)(2,1)} %refs_0_.1), channel_id=1, source_target_pairs={{0,3},{1,0},{2,1},{3,2},{16,17},{17,18},{18,19},{19,16},{4,7},{5,4... | collective-permute-start | bytes 6291464 | tf_op jit(solution)/shard_map/ppermute | solution.py:54
  2.8 23.8 %collective-permute-start.6 = (bf16[512,512]{1,0:T(8,128)(2,1)}, bf16[512,512]{1,0:T(8,128)(2,1)S(1)}, u32[]{:S(2)}, u32[]{:S(2)}) collective-permute-start(bf16[512,512]{1,0:T(8,128)(2,1)} %param.5), channel_id=1, source_target_pairs={{0,32},{1,33},{2,34},{3,35},{4,36},{5,37},{6,38},{7,39},{8,40},{9,... | collective-permute-start | bytes 1572872 | tf_op jit(solution)/shard_map/ppermute | solution.py:46
  4.8 21.9 %collective-permute-start.8 = (bf16[512,512]{1,0:T(8,128)(2,1)}, bf16[512,512]{1,0:T(8,128)(2,1)S(1)}, u32[]{:S(2)}, u32[]{:S(2)}) collective-permute-start(bf16[512,512]{1,0:T(8,128)(2,1)} %param.5), channel_id=1, source_target_pairs={{0,64},{1,65},{2,66},{3,67},{4,68},{5,69},{6,70},{7,71},{8,72},{9,... | collective-permute-start | bytes 1572872 | tf_op jit(solution)/shard_map/ppermute | solution.py:46
  8.3 18.3 %collective-permute-start.7 = (bf16[512,512]{1,0:T(8,128)(2,1)}, bf16[512,512]{1,0:T(8,128)(2,1)}, u32[]{:S(2)}, u32[]{:S(2)}) collective-permute-start(bf16[512,512]{1,0:T(8,128)(2,1)} %param.5), channel_id=1, source_target_pairs={{0,96},{1,97},{2,98},{3,99},{4,100},{5,101},{6,102},{7,103},{8,104... | collective-permute-start | bytes 1572872 | tf_op jit(solution)/shard_map/ppermute | solution.py:46
  10.8 15.8 %copy-start.3 = (bf16[512,512]{1,0:T(8,128)(2,1)S(1)}, bf16[512,512]{1,0:T(8,128)(2,1)}, u32[]{:S(2)}) copy-start(bf16[512,512]{1,0:T(8,128)(2,1)} %param.5) | copy-start | bytes 1572868
  10.8 4.9 %collective-permute-start.3 = (s32[272]{0:T(512)S(1)}, s32[272]{0:T(512)S(1)}, u32[]{:S(2)}, u32[]{:S(2)}) collective-permute-start(s32[272]{0:T(512)S(1)} %pad_add_fusion.2), channel_id=1, source_target_pairs={{0,1},{1,2},{2,3},{3,0},{16,19},{17,16},{18,17},{19,18},{4,5},{5,6... | collective-permute-start | bytes 3272 | tf_op jit(solution)/shard_map/ppermute | solution.py:54
  15.7 9.8 %copy-start.6 = (s32[272]{0:T(512)}, s32[272]{0:T(512)S(1)}, u32[]{:S(2)}) copy-start(s32[272]{0:T(512)S(1)} %collective-permute-done.3.refs_2_) | copy-start | bytes 3268
  15.7 4.9 %collective-permute-start.4 = (s32[272]{0:T(512)S(1)}, s32[272]{0:T(512)S(1)}, u32[]{:S(2)}, u32[]{:S(2)}) collective-permute-start(s32[272]{0:T(512)S(1)} %collective-permute-done.3.refs_2_), channel_id=1, source_target_pairs={{0,1},{1,2},{2,3},{3,0},{16,19},{17,16},{18,17},{19,18},{4,5},{5,6... | collective-permute-start | bytes 3272 | tf_op jit(solution)/shard_map/ppermute | solution.py:54
  20.6 4.9 %copy-start.8 = (s32[272]{0:T(512)}, s32[272]{0:T(512)S(1)}, u32[]{:S(2)}) copy-start(s32[272]{0:T(512)S(1)} %collective-permute-done.4.refs_1_) | copy-start | bytes 3268
  20.6 4.9 %collective-permute-start.5 = (s32[272]{0:T(512)S(1)}, s32[272]{0:T(512)S(1)}, u32[]{:S(2)}, u32[]{:S(2)}) collective-permute-start(s32[272]{0:T(512)S(1)} %collective-permute-done.4.refs_1_), channel_id=1, source_target_pairs={{0,1},{1,2},{2,3},{3,0},{16,19},{17,16},{18,17},{19,18},{4,5},{5,6... | collective-permute-start | bytes 3272 | tf_op jit(solution)/shard_map/ppermute | solution.py:54
  25.4 0.6 copy-start.4
  25.4 27.5 %collective-permute-start = (bf16[256,4096]{1,0:T(8,128)(2,1)}, bf16[256,4096]{1,0:T(8,128)(2,1)S(1)}, u32[]{:S(2)}, u32[]{:S(2)}) collective-permute-start(bf16[256,4096]{1,0:T(8,128)(2,1)} %refs_0_.1), channel_id=1, source_target_pairs={{0,1},{1,2},{2,3},{3,0},{16,19},{17,16},{18,17},{19,18},{4,5},{5,6... | collective-permute-start | bytes 6291464 | tf_op jit(solution)/shard_map/ppermute | solution.py:54
  29.3 25.0 %collective-permute-start.11 = (bf16[4,512,512]{2,1,0:T(8,128)(2,1)}, bf16[4,512,512]{2,1,0:T(8,128)(2,1)}, u32[]{:S(2)}, u32[]{:S(2)}) collective-permute-start(bf16[4,512,512]{2,1,0:T(8,128)(2,1)} %shard_map.51.refs_4_), channel_id=1, source_target_pairs={{0,16},{16,0},{1,17},{17,1},{2,18},{18,2},{3,19},{19,3},{4,20},{20... | collective-permute-start | bytes 6291464 | tf_op jit(solution)/shard_map/ppermute | solution.py:62
  29.3 26.9 %collective-permute-start.10 = (bf16[4,512,512]{2,1,0:T(8,128)(2,1)}, bf16[4,512,512]{2,1,0:T(8,128)(2,1)}, u32[]{:S(2)}, u32[]{:S(2)}) collective-permute-start(bf16[4,512,512]{2,1,0:T(8,128)(2,1)} %shard_map.51.refs_4_), channel_id=1, source_target_pairs={{0,12},{1,13},{2,14},{3,15},{4,0},{5,1},{6,2},{7,3},{8,4},{9,5},{1... | collective-permute-start | bytes 6291464 | tf_op jit(solution)/shard_map/ppermute | solution.py:46
  32.3 29.7 %collective-permute-start.9 = (bf16[4,512,512]{2,1,0:T(8,128)(2,1)}, bf16[4,512,512]{2,1,0:T(8,128)(2,1)}, u32[]{:S(2)}, u32[]{:S(2)}) collective-permute-start(bf16[4,512,512]{2,1,0:T(8,128)(2,1)} %shard_map.51.refs_4_), channel_id=1, source_target_pairs={{0,4},{1,5},{2,6},{3,7},{4,8},{5,9},{6,10},{7,11},{8,12},{9,13},{1... | collective-permute-start | bytes 6291464 | tf_op jit(solution)/shard_map/ppermute | solution.py:46
  52.9 1.3 %copy-start = (bf16[256,4096]{1,0:T(8,128)(2,1)}, bf16[256,4096]{1,0:T(8,128)(2,1)S(1)}, u32[]{:S(2)}) copy-start(bf16[256,4096]{1,0:T(8,128)(2,1)S(1)} %collective-permute-done.refs_0_) | copy-start | bytes 6291460
  54.2 27.5 %collective-permute-start.2 = (bf16[256,4096]{1,0:T(8,128)(2,1)}, bf16[256,4096]{1,0:T(8,128)(2,1)S(1)}, u32[]{:S(2)}, u32[]{:S(2)}) collective-permute-start(bf16[256,4096]{1,0:T(8,128)(2,1)} %shard_map.47.refs_1_), channel_id=1, source_target_pairs={{0,1},{1,2},{2,3},{3,0},{16,19},{17,16},{18,17},{19,18},{4,5},{5,6... | collective-permute-start | bytes 6291464 | tf_op jit(solution)/shard_map/ppermute | solution.py:54
  58.2 7.2 %copy-start.7 = (s32[272]{0:T(512)S(1)}, s32[272]{0:T(512)}, u32[]{:S(2)}) copy-start(s32[272]{0:T(512)} %copy-done.6) | copy-start | bytes 3268
  58.2 22.3 %copy-start.9 = (s32[272]{0:T(512)S(1)}, s32[272]{0:T(512)}, u32[]{:S(2)}) copy-start(s32[272]{0:T(512)} %copy-done.8) | copy-start | bytes 3268
  58.2 22.3 %slice-start = ((s32[272]{0:T(512)}), s32[256]{0:T(256)S(1)}, s32[]{:S(2)}) async-start(s32[272]{0:T(512)} %copy-done.4), calls=%async_computation | async-start | bytes 2048 | tf_op jit(solution)/shard_map/slice | solution.py:295
  58.2 22.9 %copy-start.5 = (s32[272]{0:T(512)S(1)}, s32[272]{0:T(512)}, u32[]{:S(2)}) copy-start(s32[272]{0:T(512)} %copy-done.4) | copy-start | bytes 3268
  58.3 16.4 %collective-permute-start.13 = (bf16[2,512,512]{2,1,0:T(8,128)(2,1)}, bf16[2,512,512]{2,1,0:T(8,128)(2,1)S(1)}, u32[]{:S(2)}, u32[]{:S(2)}) collective-permute-start(bf16[2,512,512]{2,1,0:T(8,128)(2,1)} %shard_map.54), channel_id=1, source_target_pairs={{0,12},{1,13},{2,14},{3,15},{4,0},{5,1},{6,2},{7,3},{8,4},{9,5},{1... | collective-permute-start | bytes 3145736 | tf_op jit(solution)/shard_map/ppermute | solution.py:46
  64.1 16.4 %collective-permute-start.12 = (bf16[2,512,512]{2,1,0:T(8,128)(2,1)}, bf16[2,512,512]{2,1,0:T(8,128)(2,1)}, u32[]{:S(2)}, u32[]{:S(2)}) collective-permute-start(bf16[2,512,512]{2,1,0:T(8,128)(2,1)} %shard_map.53), channel_id=1, source_target_pairs={{0,4},{1,5},{2,6},{3,7},{4,8},{5,9},{6,10},{7,11},{8,12},{9,13},{1... | collective-permute-start | bytes 3145736 | tf_op jit(solution)/shard_map/ppermute | solution.py:46
  64.2 20.0 %collective-permute-start.15 = (bf16[4,512,512]{2,1,0:T(8,128)(2,1)}, bf16[4,512,512]{2,1,0:T(8,128)(2,1)}, u32[]{:S(2)}, u32[]{:S(2)}) collective-permute-start(bf16[4,512,512]{2,1,0:T(8,128)(2,1)} %collective-permute-done.10.ref.refs_6_), channel_id=1, source_target_pairs={{0,16},{16,0},{1,17},{17,1},{2,18},{18,2},{3,19},{19,3},{4,20},{20... | collective-permute-start | bytes 6291464 | tf_op jit(solution)/shard_map/ppermute | solution.py:62
  64.3 19.9 %collective-permute-start.14 = (bf16[4,512,512]{2,1,0:T(8,128)(2,1)}, bf16[4,512,512]{2,1,0:T(8,128)(2,1)}, u32[]{:S(2)}, u32[]{:S(2)}) collective-permute-start(bf16[4,512,512]{2,1,0:T(8,128)(2,1)} %collective-permute-done.9.ref.refs_5_), channel_id=1, source_target_pairs={{0,16},{16,0},{1,17},{17,1},{2,18},{18,2},{3,19},{19,3},{4,20},{20... | collective-permute-start | bytes 6291464 | tf_op jit(solution)/shard_map/ppermute | solution.py:62
  74.6 9.6 %copy-start.2 = (bf16[2,512,512]{2,1,0:T(8,128)(2,1)}, bf16[2,512,512]{2,1,0:T(8,128)(2,1)S(1)}, u32[]{:S(2)}) copy-start(bf16[2,512,512]{2,1,0:T(8,128)(2,1)S(1)} %collective-permute-done.13.refs_8_) | copy-start | bytes 3145732
  74.7 9.5 %collective-permute-start.17 = (bf16[2,512,512]{2,1,0:T(8,128)(2,1)S(1)}, bf16[2,512,512]{2,1,0:T(8,128)(2,1)}, u32[]{:S(2)}, u32[]{:S(2)}) collective-permute-start(bf16[2,512,512]{2,1,0:T(8,128)(2,1)S(1)} %collective-permute-done.13.refs_8_), channel_id=1, source_target_pairs={{0,16},{16,0},{1,17},{17,1},{2,18},{18,2},{3,19},{19,3},{4,20},{20... | collective-permute-start | bytes 3145736 | tf_op jit(solution)/shard_map/ppermute | solution.py:62
  80.5 3.7 %collective-permute-start.16 = (bf16[2,512,512]{2,1,0:T(8,128)(2,1)}, bf16[2,512,512]{2,1,0:T(8,128)(2,1)}, u32[]{:S(2)}, u32[]{:S(2)}) collective-permute-start(bf16[2,512,512]{2,1,0:T(8,128)(2,1)} %collective-permute-done.12.refs_7_), channel_id=1, source_target_pairs={{0,16},{16,0},{1,17},{17,1},{2,18},{18,2},{3,19},{19,3},{4,20},{20... | collective-permute-start | bytes 3145736 | tf_op jit(solution)/shard_map/ppermute | solution.py:62
  81.7 1.3 %copy-start.1 = (bf16[256,4096]{1,0:T(8,128)(2,1)}, bf16[256,4096]{1,0:T(8,128)(2,1)S(1)}, u32[]{:S(2)}) copy-start(bf16[256,4096]{1,0:T(8,128)(2,1)S(1)} %collective-permute-done.2.refs_0_.refs_3_) | copy-start | bytes 6291460
  102.6 5.1 %collective-permute-start.20 = (f32[3,256]{1,0:T(4,128)S(1)}, f32[3,256]{1,0:T(4,128)S(1)}, u32[]{:S(2)}, u32[]{:S(2)}) collective-permute-start(f32[3,256]{1,0:T(4,128)S(1)} %get-tuple-element.10), channel_id=1, source_target_pairs={{0,2},{1,3},{2,0},{3,1},{16,18},{17,19},{18,16},{19,17},{4,6},{5,7... | collective-permute-start | bytes 9224 | tf_op jit(solution)/shard_map/ppermute | solution.py:54
  102.6 5.1 %collective-permute-start.19 = (f32[3,256]{1,0:T(4,128)S(1)}, f32[3,256]{1,0:T(4,128)S(1)}, u32[]{:S(2)}, u32[]{:S(2)}) collective-permute-start(f32[3,256]{1,0:T(4,128)S(1)} %get-tuple-element.11), channel_id=1, source_target_pairs={{0,1},{1,2},{2,3},{3,0},{16,19},{17,16},{18,17},{19,18},{4,5},{5,6... | collective-permute-start | bytes 9224 | tf_op jit(solution)/shard_map/ppermute | solution.py:54
  105.6 3.6 %collective-permute-start.18 = (f32[3,256]{1,0:T(4,128)S(1)}, f32[3,256]{1,0:T(4,128)S(1)}, u32[]{:S(2)}, u32[]{:S(2)}) collective-permute-start(f32[3,256]{1,0:T(4,128)S(1)} %get-tuple-element.12), channel_id=1, source_target_pairs={{0,3},{1,0},{2,1},{3,2},{16,17},{17,18},{18,19},{19,16},{4,7},{5,4... | collective-permute-start | bytes 9224 | tf_op jit(solution)/shard_map/ppermute | solution.py:54

commit v4 on v3

--- a/solution.py
+++ b/solution.py
@@ -15,7 +15,7 @@
 PIECES = 5
 RING = 4
 PACE_F = 2
-PACE_M, PACE_A, PACE_B = 3, 2, 8
+PACE_M, PACE_A, PACE_B = 3, 5, 8
 AXES = ("z", "core", "y", "x")
 VMEM = 60 * 1024 * 1024
 REL = (0, -1, 1, 2)
@@ -125,6 +125,7 @@
     queries = [refs.pop(0) for _ in range(SOURCES)]
     pieces = [[refs.pop(0) for _ in range(PIECES)] for _ in range(2)]
     del refs[:extra]
+    results = [refs.pop(0) for _ in range(SOURCES)]
     outs, q_all, p_buf, a_sem, p_sem = refs
     me_z, me_core, me_y, me_x = (info[k] for k in range(4))
     feats = p_buf.shape[2] // 8
@@ -161,8 +162,6 @@
 
     load_slot(0)
     load_pair((0, 1))
-    load_pair((2, 3))
-    load_slot(1)
 
     def owner_of(k):
         return turn(me_y, jnp.where(k == 3, 2, jnp.where(k == 2, 1, -k))) * RING + me_x
@@ -226,17 +225,25 @@
         @pl.when(second == 0)
         def _():
             pltpu.make_async_copy(p_buf.at[k], p_buf.at[k], p_sem.at[k]).wait()
-            for later in range(2, RING):
-                @pl.when(k + 2 == later)
-                def _():
-                    load_slot(later)
 
         @pl.when(k == 0)
         def _():
             for s in pair:
                 pltpu.make_async_copy(q_all.at[s], q_all.at[s], a_sem.at[s]).wait()
 
+        @pl.when(step == 0)
+        def _():
+            load_pair((2, 3))
+
+        for later in range(1, RING):
+            @pl.when(step == 2 * later - 2)
+            def _():
+                load_slot(later)
+
         multiply(k, pair)
+
+    for s in range(SOURCES):
+        results[s][...] = outs[s]
 
 
 def score(info, lists, positive, queries, pieces, extra=()):
@@ -245,19 +252,20 @@
     flat += list(extra)
     smem, vmem = pl.BlockSpec(memory_space=pltpu.SMEM), pl.BlockSpec(memory_space=pltpu.VMEM)
     anywhere = pl.BlockSpec(memory_space=pl.ANY)
-    stats = jax.ShapeDtypeStruct((SOURCES, 3, rows), jnp.float32)
+    stats = [jax.ShapeDtypeStruct((3, rows), jnp.float32)] * SOURCES
     return pl.pallas_call(
         functools.partial(score_kernel, len(extra), float(features) ** -0.5),
         out_shape=stats,
         in_specs=[smem, smem, vmem] + [anywhere] * len(flat),
-        out_specs=vmem,
+        out_specs=[vmem] * SOURCES,
         scratch_shapes=[
+            pltpu.VMEM((SOURCES, 3, rows), jnp.float32),
             pltpu.VMEM((SOURCES, rows, features), jnp.bfloat16),
             pltpu.VMEM((RING, 2 * PBLK, features), jnp.bfloat16),
             pltpu.SemaphoreType.DMA((SOURCES,)),
             pltpu.SemaphoreType.DMA((RING,)),
         ],
-        compiler_params=pltpu.CompilerParams(vmem_limit_bytes=VMEM),
+        compiler_params=pltpu.CompilerParams(vmem_limit_bytes=48 * 1024 * 1024),
         cost_estimate=pl.CostEstimate(flops=1000000, bytes_accessed=0, transcendentals=0),
     )(info, lists, positive, *flat)
 
@@ -282,10 +290,10 @@
     meta_b = shift_x(meta_f, 1)
 
     s = jnp.stack([passages] + [shift_zy(passages, True, step) for step in (1, -1, 2)])
-    s = after(s, [token([meta_b, meta_f, meta_a], PACE_M)])
+    s = after(s, [token([meta_f], PACE_M)])
     pr, pl_ = shift_zy(s, False, 1), shift_zy(s, False, -1)
     sides = [both(s)]
-    gate = token([sides[0][1]], PACE_A)
+    gate = token([sides[0][1], meta_b], PACE_A)
     fr = shift_zy(take(pr, 0, [gate]), False, 1)
     fl = shift_zy(take(pl_, 2, [gate]), False, -1)
     sides += [both(a) for a in (pr, pl_, fr, fl)]

time: 111 us -> 108 us (0.973)
  waiting for transfers between devices: 54.9 us -> 43.1 us
  starting transfers between devices: 20.1 us -> 31.1 us
  other arithmetic: 5.71 us -> 4.51 us
    ppermute x5, starting transfers between devices: 0.59 us -> 10.6 us  [swap(): return lax.ppermute(array, 'core', [(0, 1), (1, 0)])]
    ppermute x7, waiting for transfers between devices: 16.4 us -> 7.95 us  [shift_zy(): return lax.ppermute(array, AXES, pairs)]
    ppermute x9, waiting for transfers between devices: 38.5 us -> 33.4 us  [shift_x(): return lax.ppermute(array, ('core', 'x'), pairs)]
    ppermute x5, waiting for transfers between devices: 0.01 us -> 1.72 us  [swap(): return lax.ppermute(array, 'core', [(0, 1), (1, 0)])]
    ppermute x9, starting transfers between devices: 6.16 us -> 7.57 us  [shift_x(): return lax.ppermute(array, ('core', 'x'), pairs)]
    unnamed x20 -> x14, local copies, waits for them, and re-layouts: 3.23 us -> 3.07 us
  transfers between devices with their start and end apart: 21 -> 21, of which waited for: 10 -> 10; matrix products, arithmetic and copies ran while one was open for 5% -> 4% of each run, Pallas kernels for 6% -> 6%
where the time goes in v4:
time: 108 us; the launch traced here: 107 us
  waiting for transfers between devices  43.1 us (40%)
  starting transfers between devices  31.1 us (29%)
  Pallas kernels  24.3 us (22%)
  other arithmetic  4.51 us (4%)
  local copies, waits for them, and re-layouts  3.86 us (4%)
    ppermute x9, waiting for transfers between devices, shift_x(): return lax.ppermute(array, ('core', 'x'), pairs)  33.4 us
    pallas_call x1, Pallas kernels, score(): pl.pallas_call(functools.partial(score_kernel, len(extra), float(features...  17.8 us
    ppermute x7, starting transfers between devices, shift_zy(): return lax.ppermute(array, AXES, pairs)  12.9 us
    ppermute x5, starting transfers between devices, swap(): return lax.ppermute(array, 'core', [(0, 1), (1, 0)])  10.6 us
    ppermute x7, waiting for transfers between devices, shift_zy(): return lax.ppermute(array, AXES, pairs)  7.95 us
    ppermute x9, starting transfers between devices, shift_x(): return lax.ppermute(array, ('core', 'x'), pairs)  7.57 us
    pallas_call x2, Pallas kernels, take(): pl.pallas_call(kernel, out_shape=jax.ShapeDtypeStruct((2, *array.shape[1:...  4.1 us
    unnamed x14, local copies, waits for them, and re-layouts  3.07 us
  transfers between devices with their start and end apart: 21, of which 10 were waited for; matrix products, arithmetic and copies ran while one was open for 4% of the time, Pallas kernels for 6%

profile of v4, /device:TPU:0, one launch (start us, length us, event | category | flops | bytes accessed | tf_op | source)
XLA Modules:
  0.0 107.0 jit_solution(780112569877485895)
XLA Ops:
  0.0 2.8 %collective-permute-start.1 = (bf16[256,4096]{1,0:T(8,128)(2,1)}, bf16[256,4096]{1,0:T(8,128)(2,1)}, u32[]{:S(2)}, u32[]{:S(2)}) collective-permute-start(bf16[256,4096]{1,0:T(8,128)(2,1)} %refs_0_.1), channel_id=1, source_target_pairs={{0,3},{1,0},{2,1},{3,2},{16,17},{17,18},{18,19},{19,16},{4,7},{5,4... | collective-permute-start | bytes 6291464 | tf_op jit(solution)/shard_map/ppermute | solution.py:54
  2.8 1.9 %collective-permute-start.6 = (bf16[512,512]{1,0:T(8,128)(2,1)}, bf16[512,512]{1,0:T(8,128)(2,1)S(1)}, u32[]{:S(2)}, u32[]{:S(2)}) collective-permute-start(bf16[512,512]{1,0:T(8,128)(2,1)} %param.5), channel_id=1, source_target_pairs={{0,32},{1,33},{2,34},{3,35},{4,36},{5,37},{6,38},{7,39},{8,40},{9,... | collective-permute-start | bytes 1572872 | tf_op jit(solution)/shard_map/ppermute | solution.py:46
  4.8 3.6 %collective-permute-start.8 = (bf16[512,512]{1,0:T(8,128)(2,1)}, bf16[512,512]{1,0:T(8,128)(2,1)S(1)}, u32[]{:S(2)}, u32[]{:S(2)}) collective-permute-start(bf16[512,512]{1,0:T(8,128)(2,1)} %param.5), channel_id=1, source_target_pairs={{0,64},{1,65},{2,66},{3,67},{4,68},{5,69},{6,70},{7,71},{8,72},{9,... | collective-permute-start | bytes 1572872 | tf_op jit(solution)/shard_map/ppermute | solution.py:46
  8.3 1.0 collective-permute-start.7
  9.4 0.8 reshape.4
  10.1 0.7 pad_add_fusion.2
  10.8 4.9 %collective-permute-done.3 = s32[272]{0:T(512)S(1)} collective-permute-done((s32[272]{0:T(512)S(1)}, s32[272]{0:T(512)S(1)}, u32[]{:S(2)}, u32[]{:S(2)}) %collective-permute-start.3) | collective-permute-done | bytes 1120 | tf_op jit(solution)/shard_map/ppermute | solution.py:54
  15.7 4.9 %collective-permute-done.4.refs_0_ = s32[272]{0:T(512)S(1)} collective-permute-done((s32[272]{0:T(512)S(1)}, s32[272]{0:T(512)S(1)}, u32[]{:S(2)}, u32[]{:S(2)}) %collective-permute-start.4) | collective-permute-done | bytes 1120 | tf_op jit(solution)/shard_map/ppermute | solution.py:54
  20.6 0.6 copy-done.5
  21.8 2.6 %pad_maximum_fusion.refs_0_ = bf16[4,512,512]{2,1,0:T(8,128)(2,1)} fusion(bf16[1,512,512]{2,1,0:T(8,128)(2,1)S(1)} %bitcast.39, bf16[1,512,512]{2,1,0:T(8,128)(2,1)} %bitcast.14, bf16[1,512,512]{2,1,0:T(8,128)(2,1)S(1)} %bitcast.38, bf16[1,512,512]{2,1,0:T(8,128)(2,1)S(1)} %bitcast.37), kind=kLoop, calls=%fused_computation | loop fusion | flops 3145728 | bytes 4194304 | tf_op jit(solution)/shard_map/stack | solution.py:292
  24.4 3.0 %collective-permute-start.10 = (bf16[4,512,512]{2,1,0:T(8,128)(2,1)}, bf16[4,512,512]{2,1,0:T(8,128)(2,1)}, u32[]{:S(2)}, u32[]{:S(2)}) collective-permute-start(bf16[4,512,512]{2,1,0:T(8,128)(2,1)} %shard_map.51.refs_4_), channel_id=1, source_target_pairs={{0,12},{1,13},{2,14},{3,15},{4,0},{5,1},{6,2},{7,3},{8,4},{9,5},{1... | collective-permute-start | bytes 6291464 | tf_op jit(solution)/shard_map/ppermute | solution.py:46
  27.4 8.5 %collective-permute-done.1.refs_0_.refs_2_ = bf16[256,4096]{1,0:T(8,128)(2,1)} collective-permute-done((bf16[256,4096]{1,0:T(8,128)(2,1)}, bf16[256,4096]{1,0:T(8,128)(2,1)}, u32[]{:S(2)}, u32[]{:S(2)}) %collective-permute-start.1) | collective-permute-done | bytes 2097184 | tf_op jit(solution)/shard_map/ppermute | solution.py:54
  35.9 2.1 %collective-permute-start.5 = (s32[272]{0:T(512)S(1)}, s32[272]{0:T(512)S(1)}, u32[]{:S(2)}, u32[]{:S(2)}) collective-permute-start(s32[272]{0:T(512)S(1)} %copy-done.6), channel_id=1, source_target_pairs={{0,1},{1,2},{2,3},{3,0},{16,19},{17,16},{18,17},{19,18},{4,5},{5,6... | collective-permute-start | bytes 3272 | tf_op jit(solution)/shard_map/ppermute | solution.py:54
  38.1 0.6 shard_map.46.refs_1_
  38.7 10.1 %collective-permute-done.refs_0_ = bf16[256,4096]{1,0:T(8,128)(2,1)S(1)} collective-permute-done((bf16[256,4096]{1,0:T(8,128)(2,1)}, bf16[256,4096]{1,0:T(8,128)(2,1)S(1)}, u32[]{:S(2)}, u32[]{:S(2)}) %collective-permute-start) | collective-permute-done | bytes 2097184 | tf_op jit(solution)/shard_map/ppermute | solution.py:54
  48.7 1.3 %copy-done.1 = bf16[256,4096]{1,0:T(8,128)(2,1)} copy-done((bf16[256,4096]{1,0:T(8,128)(2,1)}, bf16[256,4096]{1,0:T(8,128)(2,1)S(1)}, u32[]{:S(2)}) %copy-start.1) | copy-done | bytes 2097176
  51.1 0.6 shard_map.52.refs_0_
  51.7 2.0 %shard_map.54 = bf16[2,512,512]{2,1,0:T(8,128)(2,1)} custom-call(bf16[4,512,512]{2,1,0:T(8,128)(2,1)} %collective-permute-done.10.ref.refs_6_, f32[8,128]{1,0:T(8,128)} %shard_map.52.refs_0_), custom_call_target="tpu_custom_call" | custom-call | flops 1000 | tf_op jit(solution)/shard_map/pallas_call | solution.py:112
  53.8 3.3 %collective-permute-start.13 = (bf16[2,512,512]{2,1,0:T(8,128)(2,1)}, bf16[2,512,512]{2,1,0:T(8,128)(2,1)S(1)}, u32[]{:S(2)}, u32[]{:S(2)}) collective-permute-start(bf16[2,512,512]{2,1,0:T(8,128)(2,1)} %shard_map.54), channel_id=1, source_target_pairs={{0,12},{1,13},{2,14},{3,15},{4,0},{5,1},{6,2},{7,3},{8,4},{9,5},{1... | collective-permute-start | bytes 3145736 | tf_op jit(solution)/shard_map/ppermute | solution.py:46
  57.1 2.1 %shard_map.53 = bf16[2,512,512]{2,1,0:T(8,128)(2,1)} custom-call(bf16[4,512,512]{2,1,0:T(8,128)(2,1)} %collective-permute-done.9.ref.refs_5_, f32[8,128]{1,0:T(8,128)} %shard_map.52.refs_0_), custom_call_target="tpu_custom_call" | custom-call | flops 1000 | tf_op jit(solution)/shard_map/pallas_call | solution.py:112
  59.3 4.1 %collective-permute-start.15 = (bf16[4,512,512]{2,1,0:T(8,128)(2,1)}, bf16[4,512,512]{2,1,0:T(8,128)(2,1)}, u32[]{:S(2)}, u32[]{:S(2)}) collective-permute-start(bf16[4,512,512]{2,1,0:T(8,128)(2,1)} %collective-permute-done.10.ref.refs_6_), channel_id=1, source_target_pairs={{0,16},{16,0},{1,17},{17,1},{2,18},{18,2},{3,19},{19,3},{4,20},{20... | collective-permute-start | bytes 6291464 | tf_op jit(solution)/shard_map/ppermute | solution.py:62
  64.0 5.7 %collective-permute-done.13.refs_8_ = bf16[2,512,512]{2,1,0:T(8,128)(2,1)S(1)} collective-permute-done((bf16[2,512,512]{2,1,0:T(8,128)(2,1)}, bf16[2,512,512]{2,1,0:T(8,128)(2,1)S(1)}, u32[]{:S(2)}, u32[]{:S(2)}) %collective-permute-start.13) | collective-permute-done | bytes 1048608 | tf_op jit(solution)/shard_map/ppermute | solution.py:46
  69.7 3.5 %collective-permute-start.17 = (bf16[2,512,512]{2,1,0:T(8,128)(2,1)S(1)}, bf16[2,512,512]{2,1,0:T(8,128)(2,1)S(1)}, u32[]{:S(2)}, u32[]{:S(2)}) collective-permute-start(bf16[2,512,512]{2,1,0:T(8,128)(2,1)S(1)} %collective-permute-done.13.refs_8_), channel_id=1, source_target_pairs={{0,16},{16,0},{1,17},{17,1},{2,18},{18,2},{3,19},{19,3},{4,20},{20... | collective-permute-start | bytes 3145736 | tf_op jit(solution)/shard_map/ppermute | solution.py:62
  73.2 2.3 %collective-permute-done.12.refs_7_ = bf16[2,512,512]{2,1,0:T(8,128)(2,1)S(1)} collective-permute-done((bf16[2,512,512]{2,1,0:T(8,128)(2,1)}, bf16[2,512,512]{2,1,0:T(8,128)(2,1)S(1)}, u32[]{:S(2)}, u32[]{:S(2)}) %collective-permute-start.12) | collective-permute-done | bytes 1048608 | tf_op jit(solution)/shard_map/ppermute | solution.py:46
  75.5 2.9 %collective-permute-start.16 = (bf16[2,512,512]{2,1,0:T(8,128)(2,1)S(1)}, bf16[2,512,512]{2,1,0:T(8,128)(2,1)}, u32[]{:S(2)}, u32[]{:S(2)}) collective-permute-start(bf16[2,512,512]{2,1,0:T(8,128)(2,1)S(1)} %collective-permute-done.12.refs_7_), channel_id=1, source_target_pairs={{0,16},{16,0},{1,17},{17,1},{2,18},{18,2},{3,19},{19,3},{4,20},{20... | collective-permute-start | bytes 3145736 | tf_op jit(solution)/shard_map/ppermute | solution.py:62
  78.4 0.6 shard_map.48.refs_1_
  79.1 1.7 %collective-permute-done.16.refs_12_ = bf16[2,512,512]{2,1,0:T(8,128)(2,1)} collective-permute-done((bf16[2,512,512]{2,1,0:T(8,128)(2,1)S(1)}, bf16[2,512,512]{2,1,0:T(8,128)(2,1)}, u32[]{:S(2)}, u32[]{:S(2)}) %collective-permute-start.16) | collective-permute-done | bytes 1048608 | tf_op jit(solution)/shard_map/ppermute | solution.py:62
  81.4 17.8 %shard_map.55 = (f32[3,256]{1,0:T(4,128)S(1)}, f32[3,256]{1,0:T(4,128)S(1)}, f32[3,256]{1,0:T(4,128)S(1)}, f32[3,256]{1,0:T(4,128)S(1)}) custom-call(s32[4]{0:T(128)S(1)} %copy-done, s32[4,16]{1,0:T(4,128)S(1)} %pad_add_fusion.1.lists, s32[4,1,256]{2,1,0:T(1,128)S(1)} %pad_add_fusion.positive, bf16[256,4096]{1,0:T(8,128)(2,1)} %refs_0_.1, ...), custom_call_target="tpu_custom_call" | custom-call | flops 1000000 | tf_op jit(solution)/shard_map/pallas_call | solution.py:256
  99.6 1.7 %collective-permute-start.19 = (f32[3,256]{1,0:T(4,128)S(1)}, f32[3,256]{1,0:T(4,128)S(1)}, u32[]{:S(2)}, u32[]{:S(2)}) collective-permute-start(f32[3,256]{1,0:T(4,128)S(1)} %get-tuple-element.11), channel_id=1, source_target_pairs={{0,1},{1,2},{2,3},{3,0},{16,19},{17,16},{18,17},{19,18},{4,5},{5,6... | collective-permute-start | bytes 9224 | tf_op jit(solution)/shard_map/ppermute | solution.py:54
  101.3 1.6 %collective-permute-done.18 = f32[3,256]{1,0:T(4,128)S(1)} collective-permute-done((f32[3,256]{1,0:T(4,128)S(1)}, f32[3,256]{1,0:T(4,128)S(1)}, u32[]{:S(2)}, u32[]{:S(2)}) %collective-permute-start.18) | collective-permute-done | bytes 3104 | tf_op jit(solution)/shard_map/ppermute | solution.py:54
  102.9 1.5 %collective-permute-done.19 = f32[3,256]{1,0:T(4,128)S(1)} collective-permute-done((f32[3,256]{1,0:T(4,128)S(1)}, f32[3,256]{1,0:T(4,128)S(1)}, u32[]{:S(2)}, u32[]{:S(2)}) %collective-permute-start.19) | collective-permute-done | bytes 3104 | tf_op jit(solution)/shard_map/ppermute | solution.py:54
  104.4 2.0 %collective-permute-done.20 = f32[3,256]{1,0:T(4,128)S(1)} collective-permute-done((f32[3,256]{1,0:T(4,128)S(1)}, f32[3,256]{1,0:T(4,128)S(1)}, u32[]{:S(2)}, u32[]{:S(2)}) %collective-permute-start.20) | collective-permute-done | bytes 3104 | tf_op jit(solution)/shard_map/ppermute | solution.py:54
  (52 shorter events, 4.0 us)
Async XLA Ops:
  0.0 35.9 %collective-permute-start.1 = (bf16[256,4096]{1,0:T(8,128)(2,1)}, bf16[256,4096]{1,0:T(8,128)(2,1)}, u32[]{:S(2)}, u32[]{:S(2)}) collective-permute-start(bf16[256,4096]{1,0:T(8,128)(2,1)} %refs_0_.1), channel_id=1, source_target_pairs={{0,3},{1,0},{2,1},{3,2},{16,17},{17,18},{18,19},{19,16},{4,7},{5,4... | collective-permute-start | bytes 6291464 | tf_op jit(solution)/shard_map/ppermute | solution.py:54
  2.8 18.9 %collective-permute-start.6 = (bf16[512,512]{1,0:T(8,128)(2,1)}, bf16[512,512]{1,0:T(8,128)(2,1)S(1)}, u32[]{:S(2)}, u32[]{:S(2)}) collective-permute-start(bf16[512,512]{1,0:T(8,128)(2,1)} %param.5), channel_id=1, source_target_pairs={{0,32},{1,33},{2,34},{3,35},{4,36},{5,37},{6,38},{7,39},{8,40},{9,... | collective-permute-start | bytes 1572872 | tf_op jit(solution)/shard_map/ppermute | solution.py:46
  4.8 17.0 %collective-permute-start.8 = (bf16[512,512]{1,0:T(8,128)(2,1)}, bf16[512,512]{1,0:T(8,128)(2,1)S(1)}, u32[]{:S(2)}, u32[]{:S(2)}) collective-permute-start(bf16[512,512]{1,0:T(8,128)(2,1)} %param.5), channel_id=1, source_target_pairs={{0,64},{1,65},{2,66},{3,67},{4,68},{5,69},{6,70},{7,71},{8,72},{9,... | collective-permute-start | bytes 1572872 | tf_op jit(solution)/shard_map/ppermute | solution.py:46
  8.3 13.4 %collective-permute-start.7 = (bf16[512,512]{1,0:T(8,128)(2,1)}, bf16[512,512]{1,0:T(8,128)(2,1)}, u32[]{:S(2)}, u32[]{:S(2)}) collective-permute-start(bf16[512,512]{1,0:T(8,128)(2,1)} %param.5), channel_id=1, source_target_pairs={{0,96},{1,97},{2,98},{3,99},{4,100},{5,101},{6,102},{7,103},{8,104... | collective-permute-start | bytes 1572872 | tf_op jit(solution)/shard_map/ppermute | solution.py:46
  10.8 11.0 %copy-start.2 = (bf16[512,512]{1,0:T(8,128)(2,1)S(1)}, bf16[512,512]{1,0:T(8,128)(2,1)}, u32[]{:S(2)}) copy-start(bf16[512,512]{1,0:T(8,128)(2,1)} %param.5) | copy-start | bytes 1572868
  10.8 4.9 %collective-permute-start.3 = (s32[272]{0:T(512)S(1)}, s32[272]{0:T(512)S(1)}, u32[]{:S(2)}, u32[]{:S(2)}) collective-permute-start(s32[272]{0:T(512)S(1)} %pad_add_fusion.2), channel_id=1, source_target_pairs={{0,1},{1,2},{2,3},{3,0},{16,19},{17,16},{18,17},{19,18},{4,5},{5,6... | collective-permute-start | bytes 3272 | tf_op jit(solution)/shard_map/ppermute | solution.py:54
  15.7 4.9 %collective-permute-start.4 = (s32[272]{0:T(512)S(1)}, s32[272]{0:T(512)S(1)}, u32[]{:S(2)}, u32[]{:S(2)}) collective-permute-start(s32[272]{0:T(512)S(1)} %collective-permute-done.3), channel_id=1, source_target_pairs={{0,1},{1,2},{2,3},{3,0},{16,19},{17,16},{18,17},{19,18},{4,5},{5,6... | collective-permute-start | bytes 3272 | tf_op jit(solution)/shard_map/ppermute | solution.py:54
  20.6 0.6 copy-start.5
  20.6 28.2 %collective-permute-start = (bf16[256,4096]{1,0:T(8,128)(2,1)}, bf16[256,4096]{1,0:T(8,128)(2,1)S(1)}, u32[]{:S(2)}, u32[]{:S(2)}) collective-permute-start(bf16[256,4096]{1,0:T(8,128)(2,1)} %refs_0_.1), channel_id=1, source_target_pairs={{0,1},{1,2},{2,3},{3,0},{16,19},{17,16},{18,17},{19,18},{4,5},{5,6... | collective-permute-start | bytes 6291464 | tf_op jit(solution)/shard_map/ppermute | solution.py:54
  24.4 11.5 %copy-start.6 = (s32[272]{0:T(512)S(1)}, s32[272]{0:T(512)}, u32[]{:S(2)}) copy-start(s32[272]{0:T(512)} %copy-done.5) | copy-start | bytes 3268
  24.4 26.1 %collective-permute-start.11 = (bf16[4,512,512]{2,1,0:T(8,128)(2,1)}, bf16[4,512,512]{2,1,0:T(8,128)(2,1)}, u32[]{:S(2)}, u32[]{:S(2)}) collective-permute-start(bf16[4,512,512]{2,1,0:T(8,128)(2,1)} %shard_map.51.refs_4_), channel_id=1, source_target_pairs={{0,16},{16,0},{1,17},{17,1},{2,18},{18,2},{3,19},{19,3},{4,20},{20... | collective-permute-start | bytes 6291464 | tf_op jit(solution)/shard_map/ppermute | solution.py:62
  24.4 27.3 %collective-permute-start.10 = (bf16[4,512,512]{2,1,0:T(8,128)(2,1)}, bf16[4,512,512]{2,1,0:T(8,128)(2,1)}, u32[]{:S(2)}, u32[]{:S(2)}) collective-permute-start(bf16[4,512,512]{2,1,0:T(8,128)(2,1)} %shard_map.51.refs_4_), channel_id=1, source_target_pairs={{0,12},{1,13},{2,14},{3,15},{4,0},{5,1},{6,2},{7,3},{8,4},{9,5},{1... | collective-permute-start | bytes 6291464 | tf_op jit(solution)/shard_map/ppermute | solution.py:46
  27.4 29.7 %collective-permute-start.9 = (bf16[4,512,512]{2,1,0:T(8,128)(2,1)}, bf16[4,512,512]{2,1,0:T(8,128)(2,1)}, u32[]{:S(2)}, u32[]{:S(2)}) collective-permute-start(bf16[4,512,512]{2,1,0:T(8,128)(2,1)} %shard_map.51.refs_4_), channel_id=1, source_target_pairs={{0,4},{1,5},{2,6},{3,7},{4,8},{5,9},{6,10},{7,11},{8,12},{9,13},{1... | collective-permute-start | bytes 6291464 | tf_op jit(solution)/shard_map/ppermute | solution.py:46
  35.9 14.6 %collective-permute-start.5 = (s32[272]{0:T(512)S(1)}, s32[272]{0:T(512)S(1)}, u32[]{:S(2)}, u32[]{:S(2)}) collective-permute-start(s32[272]{0:T(512)S(1)} %copy-done.6), channel_id=1, source_target_pairs={{0,1},{1,2},{2,3},{3,0},{16,19},{17,16},{18,17},{19,18},{4,5},{5,6... | collective-permute-start | bytes 3272 | tf_op jit(solution)/shard_map/ppermute | solution.py:54
  48.7 1.3 %copy-start.1 = (bf16[256,4096]{1,0:T(8,128)(2,1)}, bf16[256,4096]{1,0:T(8,128)(2,1)S(1)}, u32[]{:S(2)}) copy-start(bf16[256,4096]{1,0:T(8,128)(2,1)S(1)} %collective-permute-done.refs_0_) | copy-start | bytes 6291460
  50.0 28.4 %collective-permute-start.2 = (bf16[256,4096]{1,0:T(8,128)(2,1)}, bf16[256,4096]{1,0:T(8,128)(2,1)}, u32[]{:S(2)}, u32[]{:S(2)}) collective-permute-start(bf16[256,4096]{1,0:T(8,128)(2,1)} %shard_map.47.refs_1_), channel_id=1, source_target_pairs={{0,1},{1,2},{2,3},{3,0},{16,19},{17,16},{18,17},{19,18},{4,5},{5,6... | collective-permute-start | bytes 6291464 | tf_op jit(solution)/shard_map/ppermute | solution.py:54
  50.5 0.6 copy-start.3
  53.8 24.6 %slice-start = ((s32[272]{0:T(512)}), s32[256]{0:T(256)S(1)}, s32[]{:S(2)}) async-start(s32[272]{0:T(512)} %copy-done.3), calls=%async_computation | async-start | bytes 2048 | tf_op jit(solution)/shard_map/slice | solution.py:303
  53.8 24.6 %copy-start.4 = (s32[272]{0:T(512)S(1)}, s32[272]{0:T(512)}, u32[]{:S(2)}) copy-start(s32[272]{0:T(512)} %copy-done.3) | copy-start | bytes 3268
  53.8 16.0 %collective-permute-start.13 = (bf16[2,512,512]{2,1,0:T(8,128)(2,1)}, bf16[2,512,512]{2,1,0:T(8,128)(2,1)S(1)}, u32[]{:S(2)}, u32[]{:S(2)}) collective-permute-start(bf16[2,512,512]{2,1,0:T(8,128)(2,1)} %shard_map.54), channel_id=1, source_target_pairs={{0,12},{1,13},{2,14},{3,15},{4,0},{5,1},{6,2},{7,3},{8,4},{9,5},{1... | collective-permute-start | bytes 3145736 | tf_op jit(solution)/shard_map/ppermute | solution.py:46
  59.2 16.3 %collective-permute-start.12 = (bf16[2,512,512]{2,1,0:T(8,128)(2,1)}, bf16[2,512,512]{2,1,0:T(8,128)(2,1)S(1)}, u32[]{:S(2)}, u32[]{:S(2)}) collective-permute-start(bf16[2,512,512]{2,1,0:T(8,128)(2,1)} %shard_map.53), channel_id=1, source_target_pairs={{0,4},{1,5},{2,6},{3,7},{4,8},{5,9},{6,10},{7,11},{8,12},{9,13},{1... | collective-permute-start | bytes 3145736 | tf_op jit(solution)/shard_map/ppermute | solution.py:46
  59.3 19.8 %collective-permute-start.15 = (bf16[4,512,512]{2,1,0:T(8,128)(2,1)}, bf16[4,512,512]{2,1,0:T(8,128)(2,1)}, u32[]{:S(2)}, u32[]{:S(2)}) collective-permute-start(bf16[4,512,512]{2,1,0:T(8,128)(2,1)} %collective-permute-done.10.ref.refs_6_), channel_id=1, source_target_pairs={{0,16},{16,0},{1,17},{17,1},{2,18},{18,2},{3,19},{19,3},{4,20},{20... | collective-permute-start | bytes 6291464 | tf_op jit(solution)/shard_map/ppermute | solution.py:62
  63.4 15.7 %collective-permute-start.14 = (bf16[4,512,512]{2,1,0:T(8,128)(2,1)}, bf16[4,512,512]{2,1,0:T(8,128)(2,1)}, u32[]{:S(2)}, u32[]{:S(2)}) collective-permute-start(bf16[4,512,512]{2,1,0:T(8,128)(2,1)} %collective-permute-done.9.ref.refs_5_), channel_id=1, source_target_pairs={{0,16},{16,0},{1,17},{17,1},{2,18},{18,2},{3,19},{19,3},{4,20},{20... | collective-permute-start | bytes 6291464 | tf_op jit(solution)/shard_map/ppermute | solution.py:62
  69.7 9.3 %collective-permute-start.17 = (bf16[2,512,512]{2,1,0:T(8,128)(2,1)S(1)}, bf16[2,512,512]{2,1,0:T(8,128)(2,1)S(1)}, u32[]{:S(2)}, u32[]{:S(2)}) collective-permute-start(bf16[2,512,512]{2,1,0:T(8,128)(2,1)S(1)} %collective-permute-done.13.refs_8_), channel_id=1, source_target_pairs={{0,16},{16,0},{1,17},{17,1},{2,18},{18,2},{3,19},{19,3},{4,20},{20... | collective-permute-start | bytes 3145736 | tf_op jit(solution)/shard_map/ppermute | solution.py:62
  75.5 5.3 %collective-permute-start.16 = (bf16[2,512,512]{2,1,0:T(8,128)(2,1)S(1)}, bf16[2,512,512]{2,1,0:T(8,128)(2,1)}, u32[]{:S(2)}, u32[]{:S(2)}) collective-permute-start(bf16[2,512,512]{2,1,0:T(8,128)(2,1)S(1)} %collective-permute-done.12.refs_7_), channel_id=1, source_target_pairs={{0,16},{16,0},{1,17},{17,1},{2,18},{18,2},{3,19},{19,3},{4,20},{20... | collective-permute-start | bytes 3145736 | tf_op jit(solution)/shard_map/ppermute | solution.py:62
  80.8 0.6 copy-start
  99.2 3.7 %collective-permute-start.18 = (f32[3,256]{1,0:T(4,128)S(1)}, f32[3,256]{1,0:T(4,128)S(1)}, u32[]{:S(2)}, u32[]{:S(2)}) collective-permute-start(f32[3,256]{1,0:T(4,128)S(1)} %get-tuple-element.10), channel_id=1, source_target_pairs={{0,3},{1,0},{2,1},{3,2},{16,17},{17,18},{18,19},{19,16},{4,7},{5,4... | collective-permute-start | bytes 9224 | tf_op jit(solution)/shard_map/ppermute | solution.py:54
  99.6 4.8 %collective-permute-start.19 = (f32[3,256]{1,0:T(4,128)S(1)}, f32[3,256]{1,0:T(4,128)S(1)}, u32[]{:S(2)}, u32[]{:S(2)}) collective-permute-start(f32[3,256]{1,0:T(4,128)S(1)} %get-tuple-element.11), channel_id=1, source_target_pairs={{0,1},{1,2},{2,3},{3,0},{16,19},{17,16},{18,17},{19,18},{4,5},{5,6... | collective-permute-start | bytes 9224 | tf_op jit(solution)/shard_map/ppermute | solution.py:54
  101.3 5.1 %collective-permute-start.20 = (f32[3,256]{1,0:T(4,128)S(1)}, f32[3,256]{1,0:T(4,128)S(1)}, u32[]{:S(2)}, u32[]{:S(2)}) collective-permute-start(f32[3,256]{1,0:T(4,128)S(1)} %get-tuple-element.12), channel_id=1, source_target_pairs={{0,2},{1,3},{2,0},{3,1},{16,18},{17,19},{18,16},{19,17},{4,6},{5,7... | collective-permute-start | bytes 9224 | tf_op jit(solution)/shard_map/ppermute | solution.py:54

commit v5 on v4

--- a/solution.py
+++ b/solution.py
@@ -17,7 +17,7 @@
 PACE_F = 2
 PACE_M, PACE_A, PACE_B = 3, 5, 8
 AXES = ("z", "core", "y", "x")
-VMEM = 60 * 1024 * 1024
+VMEM = 8 * 1024 * 1024
 REL = (0, -1, 1, 2)
 
 

time: 108 us -> 106 us (0.981)
  waiting for transfers between devices: 43.1 us -> 48.1 us
  other arithmetic: 4.51 us -> 1.67 us
  Pallas kernels: 24.3 us -> 21.7 us
  local copies, waits for them, and re-layouts: 3.86 us -> 2.11 us
    ppermute x9, waiting for transfers between devices: 33.4 us -> 36.4 us  [shift_x(): return lax.ppermute(array, ('core', 'x'), pairs)]
    another operation x1, other arithmetic: 2.63 us -> 0.26 us  [body(): jnp.stack([passages] + [shift_zy(passages, True, step) for step in (1, -1...]
    pallas_call x4, Pallas kernels: 2.34 us -> 0.01 us  [token(): pl.pallas_call(kernel, out_shape=jax.ShapeDtypeStruct((8, 128), jnp.float...]
    unnamed x14 -> x6, local copies, waits for them, and re-layouts: 3.07 us -> 1.33 us
    ppermute x7, waiting for transfers between devices: 7.95 us -> 9.49 us  [shift_zy(): return lax.ppermute(array, AXES, pairs)]
  transfers between devices with their start and end apart: 21 -> 21, of which waited for: 10 -> 11; matrix products, arithmetic and copies ran while one was open for 4% -> 2% of each run, Pallas kernels for 6% -> 4%
where the time goes in v5:
time: 106 us; the launch traced here: 105 us
  waiting for transfers between devices  48.1 us (45%)
  starting transfers between devices  30.9 us (29%)
  Pallas kernels  21.7 us (20%)
  local copies, waits for them, and re-layouts  2.11 us (2%)
  other arithmetic  1.67 us (2%)
    ppermute x9, waiting for transfers between devices, shift_x(): return lax.ppermute(array, ('core', 'x'), pairs)  36.4 us
    pallas_call x1, Pallas kernels, score(): pl.pallas_call(functools.partial(score_kernel, len(extra), float(features...  17.6 us
    ppermute x7, starting transfers between devices, shift_zy(): return lax.ppermute(array, AXES, pairs)  12.8 us
    ppermute x5, starting transfers between devices, swap(): return lax.ppermute(array, 'core', [(0, 1), (1, 0)])  10.2 us
    ppermute x7, waiting for transfers between devices, shift_zy(): return lax.ppermute(array, AXES, pairs)  9.49 us
    ppermute x9, starting transfers between devices, shift_x(): return lax.ppermute(array, ('core', 'x'), pairs)  7.92 us
    pallas_call x2, Pallas kernels, take(): pl.pallas_call(kernel, out_shape=jax.ShapeDtypeStruct((2, *array.shape[1:...  4.13 us
    ppermute x5, waiting for transfers between devices, swap(): return lax.ppermute(array, 'core', [(0, 1), (1, 0)])  2.17 us
  transfers between devices with their start and end apart: 21, of which 11 were waited for; matrix products, arithmetic and copies ran while one was open for 2% of the time, Pallas kernels for 4%

profile of v5, /device:TPU:0, one launch (start us, length us, event | category | flops | bytes accessed | tf_op | source)
XLA Modules:
  0.0 104.6 jit_solution(2721959024942133431)
XLA Ops:
  0.0 2.8 %collective-permute-start.1 = (bf16[256,4096]{1,0:T(8,128)(2,1)}, bf16[256,4096]{1,0:T(8,128)(2,1)}, u32[]{:S(2)}, u32[]{:S(2)}) collective-permute-start(bf16[256,4096]{1,0:T(8,128)(2,1)} %refs_0_.1), channel_id=1, source_target_pairs={{0,3},{1,0},{2,1},{3,2},{16,17},{17,18},{18,19},{19,16},{4,7},{5,4... | collective-permute-start | bytes 6291464 | tf_op jit(solution)/shard_map/ppermute | solution.py:54
  2.8 1.9 %collective-permute-start.6 = (bf16[512,512]{1,0:T(8,128)(2,1)}, bf16[512,512]{1,0:T(8,128)(2,1)S(1)}, u32[]{:S(2)}, u32[]{:S(2)}) collective-permute-start(bf16[512,512]{1,0:T(8,128)(2,1)} %param.5), channel_id=1, source_target_pairs={{0,32},{1,33},{2,34},{3,35},{4,36},{5,37},{6,38},{7,39},{8,40},{9,... | collective-permute-start | bytes 1572872 | tf_op jit(solution)/shard_map/ppermute | solution.py:46
  4.8 3.6 %collective-permute-start.8 = (bf16[512,512]{1,0:T(8,128)(2,1)}, bf16[512,512]{1,0:T(8,128)(2,1)S(1)}, u32[]{:S(2)}, u32[]{:S(2)}) collective-permute-start(bf16[512,512]{1,0:T(8,128)(2,1)} %param.5), channel_id=1, source_target_pairs={{0,64},{1,65},{2,66},{3,67},{4,68},{5,69},{6,70},{7,71},{8,72},{9,... | collective-permute-start | bytes 1572872 | tf_op jit(solution)/shard_map/ppermute | solution.py:46
  8.3 1.0 collective-permute-start.7
  9.4 0.8 reshape.4
  10.1 0.7 pad_add_fusion.2
  10.8 4.9 %collective-permute-done.3 = s32[272]{0:T(512)S(1)} collective-permute-done((s32[272]{0:T(512)S(1)}, s32[272]{0:T(512)S(1)}, u32[]{:S(2)}, u32[]{:S(2)}) %collective-permute-start.3) | collective-permute-done | bytes 1120 | tf_op jit(solution)/shard_map/ppermute | solution.py:54
  15.7 4.9 %collective-permute-done.4.refs_0_ = s32[272]{0:T(512)S(1)} collective-permute-done((s32[272]{0:T(512)S(1)}, s32[272]{0:T(512)S(1)}, u32[]{:S(2)}, u32[]{:S(2)}) %collective-permute-start.4) | collective-permute-done | bytes 1120 | tf_op jit(solution)/shard_map/ppermute | solution.py:54
  20.6 0.8 collective-permute-done.8
  21.7 3.1 %collective-permute-start.10 = (bf16[4,512,512]{2,1,0:T(8,128)(2,1)S(1)}, bf16[4,512,512]{2,1,0:T(8,128)(2,1)}, u32[]{:S(2)}, u32[]{:S(2)}) collective-permute-start(bf16[4,512,512]{2,1,0:T(8,128)(2,1)S(1)} %shard_map.51.refs_4_), channel_id=1, source_target_pairs={{0,12},{1,13},{2,14},{3,15},{4,0},{5,1},{6,2},{7,3},{8,4},{9,5},{1... | collective-permute-start | bytes 6291464 | tf_op jit(solution)/shard_map/ppermute | solution.py:46
  24.8 11.1 %collective-permute-done.1.refs_0_.refs_2_ = bf16[256,4096]{1,0:T(8,128)(2,1)} collective-permute-done((bf16[256,4096]{1,0:T(8,128)(2,1)}, bf16[256,4096]{1,0:T(8,128)(2,1)}, u32[]{:S(2)}, u32[]{:S(2)}) %collective-permute-start.1) | collective-permute-done | bytes 2097184 | tf_op jit(solution)/shard_map/ppermute | solution.py:54
  35.9 2.1 %collective-permute-start.5 = (s32[272]{0:T(512)S(1)}, s32[272]{0:T(512)S(1)}, u32[]{:S(2)}, u32[]{:S(2)}) collective-permute-start(s32[272]{0:T(512)S(1)} %collective-permute-done.4.refs_0_), channel_id=1, source_target_pairs={{0,1},{1,2},{2,3},{3,0},{16,19},{17,16},{18,17},{19,18},{4,5},{5,6... | collective-permute-start | bytes 3272 | tf_op jit(solution)/shard_map/ppermute | solution.py:54
  38.1 10.8 %collective-permute-done.refs_0_ = bf16[256,4096]{1,0:T(8,128)(2,1)} collective-permute-done((bf16[256,4096]{1,0:T(8,128)(2,1)}, bf16[256,4096]{1,0:T(8,128)(2,1)}, u32[]{:S(2)}, u32[]{:S(2)}) %collective-permute-start) | collective-permute-done | bytes 2097184 | tf_op jit(solution)/shard_map/ppermute | solution.py:54
  48.8 0.5 collective-permute-start.2
  49.3 1.3 %copy-done.1 = bf16[4,512,512]{2,1,0:T(8,128)(2,1)} copy-done((bf16[4,512,512]{2,1,0:T(8,128)(2,1)}, bf16[4,512,512]{2,1,0:T(8,128)(2,1)S(1)}, u32[]{:S(2)}) %copy-start.1) | copy-done | bytes 2097176
  50.6 2.1 %shard_map.54 = bf16[2,512,512]{2,1,0:T(8,128)(2,1)} custom-call(bf16[4,512,512]{2,1,0:T(8,128)(2,1)} %collective-permute-done.10.ref.refs_6_, f32[8,128]{1,0:T(8,128)S(1)} %shard_map.52.refs_0_), custom_call_target="tpu_custom_call" | custom-call | flops 1000 | tf_op jit(solution)/shard_map/pallas_call | solution.py:112
  52.7 3.1 %collective-permute-start.13 = (bf16[2,512,512]{2,1,0:T(8,128)(2,1)}, bf16[2,512,512]{2,1,0:T(8,128)(2,1)S(1)}, u32[]{:S(2)}, u32[]{:S(2)}) collective-permute-start(bf16[2,512,512]{2,1,0:T(8,128)(2,1)} %shard_map.54), channel_id=1, source_target_pairs={{0,12},{1,13},{2,14},{3,15},{4,0},{5,1},{6,2},{7,3},{8,4},{9,5},{1... | collective-permute-start | bytes 3145736 | tf_op jit(solution)/shard_map/ppermute | solution.py:46
  55.8 2.0 %shard_map.53 = bf16[2,512,512]{2,1,0:T(8,128)(2,1)} custom-call(bf16[4,512,512]{2,1,0:T(8,128)(2,1)} %collective-permute-done.9.ref.refs_5_, f32[8,128]{1,0:T(8,128)S(1)} %shard_map.52.refs_0_), custom_call_target="tpu_custom_call" | custom-call | flops 1000 | tf_op jit(solution)/shard_map/pallas_call | solution.py:112
  58.0 4.0 %collective-permute-start.15 = (bf16[4,512,512]{2,1,0:T(8,128)(2,1)}, bf16[4,512,512]{2,1,0:T(8,128)(2,1)}, u32[]{:S(2)}, u32[]{:S(2)}) collective-permute-start(bf16[4,512,512]{2,1,0:T(8,128)(2,1)} %collective-permute-done.10.ref.refs_6_), channel_id=1, source_target_pairs={{0,16},{16,0},{1,17},{17,1},{2,18},{18,2},{3,19},{19,3},{4,20},{20... | collective-permute-start | bytes 6291464 | tf_op jit(solution)/shard_map/ppermute | solution.py:62
  62.1 6.3 %collective-permute-done.13.refs_8_ = bf16[2,512,512]{2,1,0:T(8,128)(2,1)S(1)} collective-permute-done((bf16[2,512,512]{2,1,0:T(8,128)(2,1)}, bf16[2,512,512]{2,1,0:T(8,128)(2,1)S(1)}, u32[]{:S(2)}, u32[]{:S(2)}) %collective-permute-start.13) | collective-permute-done | bytes 1048608 | tf_op jit(solution)/shard_map/ppermute | solution.py:46
  68.5 3.3 %collective-permute-start.17 = (bf16[2,512,512]{2,1,0:T(8,128)(2,1)S(1)}, bf16[2,512,512]{2,1,0:T(8,128)(2,1)S(1)}, u32[]{:S(2)}, u32[]{:S(2)}) collective-permute-start(bf16[2,512,512]{2,1,0:T(8,128)(2,1)S(1)} %collective-permute-done.13.refs_8_), channel_id=1, source_target_pairs={{0,16},{16,0},{1,17},{17,1},{2,18},{18,2},{3,19},{19,3},{4,20},{20... | collective-permute-start | bytes 3145736 | tf_op jit(solution)/shard_map/ppermute | solution.py:62
  71.8 2.4 %collective-permute-done.12.refs_7_ = bf16[2,512,512]{2,1,0:T(8,128)(2,1)S(1)} collective-permute-done((bf16[2,512,512]{2,1,0:T(8,128)(2,1)}, bf16[2,512,512]{2,1,0:T(8,128)(2,1)S(1)}, u32[]{:S(2)}, u32[]{:S(2)}) %collective-permute-start.12) | collective-permute-done | bytes 1048608 | tf_op jit(solution)/shard_map/ppermute | solution.py:46
  74.2 2.7 %collective-permute-start.16 = (bf16[2,512,512]{2,1,0:T(8,128)(2,1)S(1)}, bf16[2,512,512]{2,1,0:T(8,128)(2,1)S(1)}, u32[]{:S(2)}, u32[]{:S(2)}) collective-permute-start(bf16[2,512,512]{2,1,0:T(8,128)(2,1)S(1)} %collective-permute-done.12.refs_7_), channel_id=1, source_target_pairs={{0,16},{16,0},{1,17},{17,1},{2,18},{18,2},{3,19},{19,3},{4,20},{20... | collective-permute-start | bytes 3145736 | tf_op jit(solution)/shard_map/ppermute | solution.py:62
  77.0 2.2 %collective-permute-done.16.refs_12_ = bf16[2,512,512]{2,1,0:T(8,128)(2,1)S(1)} collective-permute-done((bf16[2,512,512]{2,1,0:T(8,128)(2,1)S(1)}, bf16[2,512,512]{2,1,0:T(8,128)(2,1)S(1)}, u32[]{:S(2)}, u32[]{:S(2)}) %collective-permute-start.16) | collective-permute-done | bytes 1048608 | tf_op jit(solution)/shard_map/ppermute | solution.py:62
  79.2 17.6 %shard_map.55 = (f32[3,256]{1,0:T(4,128)S(1)}, f32[3,256]{1,0:T(4,128)S(1)}, f32[3,256]{1,0:T(4,128)S(1)}, f32[3,256]{1,0:T(4,128)S(1)}) custom-call(s32[4]{0:T(128)S(1)} %shard_map.49.info, s32[4,16]{1,0:T(4,128)S(1)} %pad_add_fusion.1.lists, s32[4,1,256]{2,1,0:T(1,128)S(1)} %pad_add_fusion.positive, bf16[256,4096]{1,0:T(8,128)(2,1)} %refs_0_.1, ...), custom_call_target="tpu_custom_call" | custom-call | flops 1000000 | tf_op jit(solution)/shard_map/pallas_call | solution.py:256
  96.8 0.6 collective-permute-start.18
  97.5 1.4 %collective-permute-start.19 = (f32[3,256]{1,0:T(4,128)S(1)}, f32[3,256]{1,0:T(4,128)S(1)}, u32[]{:S(2)}, u32[]{:S(2)}) collective-permute-start(f32[3,256]{1,0:T(4,128)S(1)} %get-tuple-element.11), channel_id=1, source_target_pairs={{0,1},{1,2},{2,3},{3,0},{16,19},{17,16},{18,17},{19,18},{4,5},{5,6... | collective-permute-start | bytes 9224 | tf_op jit(solution)/shard_map/ppermute | solution.py:54
  98.9 0.4 collective-permute-start.20
  99.3 1.2 %collective-permute-done.18 = f32[3,256]{1,0:T(4,128)S(1)} collective-permute-done((f32[3,256]{1,0:T(4,128)S(1)}, f32[3,256]{1,0:T(4,128)S(1)}, u32[]{:S(2)}, u32[]{:S(2)}) %collective-permute-start.18) | collective-permute-done | bytes 3104 | tf_op jit(solution)/shard_map/ppermute | solution.py:54
  100.5 1.8 %collective-permute-done.19 = f32[3,256]{1,0:T(4,128)S(1)} collective-permute-done((f32[3,256]{1,0:T(4,128)S(1)}, f32[3,256]{1,0:T(4,128)S(1)}, u32[]{:S(2)}, u32[]{:S(2)}) %collective-permute-start.19) | collective-permute-done | bytes 3104 | tf_op jit(solution)/shard_map/ppermute | solution.py:54
  102.3 1.7 %collective-permute-done.20 = f32[3,256]{1,0:T(4,128)S(1)} collective-permute-done((f32[3,256]{1,0:T(4,128)S(1)}, f32[3,256]{1,0:T(4,128)S(1)}, u32[]{:S(2)}, u32[]{:S(2)}) %collective-permute-start.20) | collective-permute-done | bytes 3104 | tf_op jit(solution)/shard_map/ppermute | solution.py:54
  104.1 0.6 add_subtract_fusion
  (43 shorter events, 0.7 us)
Async XLA Ops:
  0.0 35.9 %collective-permute-start.1 = (bf16[256,4096]{1,0:T(8,128)(2,1)}, bf16[256,4096]{1,0:T(8,128)(2,1)}, u32[]{:S(2)}, u32[]{:S(2)}) collective-permute-start(bf16[256,4096]{1,0:T(8,128)(2,1)} %refs_0_.1), channel_id=1, source_target_pairs={{0,3},{1,0},{2,1},{3,2},{16,17},{17,18},{18,19},{19,16},{4,7},{5,4... | collective-permute-start | bytes 6291464 | tf_op jit(solution)/shard_map/ppermute | solution.py:54
  2.8 17.7 %collective-permute-start.6 = (bf16[512,512]{1,0:T(8,128)(2,1)}, bf16[512,512]{1,0:T(8,128)(2,1)S(1)}, u32[]{:S(2)}, u32[]{:S(2)}) collective-permute-start(bf16[512,512]{1,0:T(8,128)(2,1)} %param.5), channel_id=1, source_target_pairs={{0,32},{1,33},{2,34},{3,35},{4,36},{5,37},{6,38},{7,39},{8,40},{9,... | collective-permute-start | bytes 1572872 | tf_op jit(solution)/shard_map/ppermute | solution.py:46
  4.8 16.6 %collective-permute-start.8 = (bf16[512,512]{1,0:T(8,128)(2,1)}, bf16[512,512]{1,0:T(8,128)(2,1)S(1)}, u32[]{:S(2)}, u32[]{:S(2)}) collective-permute-start(bf16[512,512]{1,0:T(8,128)(2,1)} %param.5), channel_id=1, source_target_pairs={{0,64},{1,65},{2,66},{3,67},{4,68},{5,69},{6,70},{7,71},{8,72},{9,... | collective-permute-start | bytes 1572872 | tf_op jit(solution)/shard_map/ppermute | solution.py:46
  8.3 13.0 %collective-permute-start.7 = (bf16[512,512]{1,0:T(8,128)(2,1)}, bf16[512,512]{1,0:T(8,128)(2,1)S(1)}, u32[]{:S(2)}, u32[]{:S(2)}) collective-permute-start(bf16[512,512]{1,0:T(8,128)(2,1)} %param.5), channel_id=1, source_target_pairs={{0,96},{1,97},{2,98},{3,99},{4,100},{5,101},{6,102},{7,103},{8,104... | collective-permute-start | bytes 1572872 | tf_op jit(solution)/shard_map/ppermute | solution.py:46
  10.8 10.5 %copy-start.2 = (bf16[512,512]{1,0:T(8,128)(2,1)S(1)}, bf16[512,512]{1,0:T(8,128)(2,1)}, u32[]{:S(2)}) copy-start(bf16[512,512]{1,0:T(8,128)(2,1)} %param.5) | copy-start | bytes 1572868
  10.8 4.9 %collective-permute-start.3 = (s32[272]{0:T(512)S(1)}, s32[272]{0:T(512)S(1)}, u32[]{:S(2)}, u32[]{:S(2)}) collective-permute-start(s32[272]{0:T(512)S(1)} %pad_add_fusion.2), channel_id=1, source_target_pairs={{0,1},{1,2},{2,3},{3,0},{16,19},{17,16},{18,17},{19,18},{4,5},{5,6... | collective-permute-start | bytes 3272 | tf_op jit(solution)/shard_map/ppermute | solution.py:54
  15.7 4.9 %collective-permute-start.4 = (s32[272]{0:T(512)S(1)}, s32[272]{0:T(512)S(1)}, u32[]{:S(2)}, u32[]{:S(2)}) collective-permute-start(s32[272]{0:T(512)S(1)} %collective-permute-done.3), channel_id=1, source_target_pairs={{0,1},{1,2},{2,3},{3,0},{16,19},{17,16},{18,17},{19,18},{4,5},{5,6... | collective-permute-start | bytes 3272 | tf_op jit(solution)/shard_map/ppermute | solution.py:54
  20.6 28.3 %collective-permute-start = (bf16[256,4096]{1,0:T(8,128)(2,1)}, bf16[256,4096]{1,0:T(8,128)(2,1)}, u32[]{:S(2)}, u32[]{:S(2)}) collective-permute-start(bf16[256,4096]{1,0:T(8,128)(2,1)} %refs_0_.1), channel_id=1, source_target_pairs={{0,1},{1,2},{2,3},{3,0},{16,19},{17,16},{18,17},{19,18},{4,5},{5,6... | collective-permute-start | bytes 6291464 | tf_op jit(solution)/shard_map/ppermute | solution.py:54
  21.6 16.5 %copy-start = (bf16[4,512,512]{2,1,0:T(8,128)(2,1)}, bf16[4,512,512]{2,1,0:T(8,128)(2,1)S(1)}, u32[]{:S(2)}) copy-start(bf16[4,512,512]{2,1,0:T(8,128)(2,1)S(1)} %shard_map.51.refs_4_) | copy-start | bytes 6291460
  21.6 27.7 %collective-permute-start.11 = (bf16[4,512,512]{2,1,0:T(8,128)(2,1)S(1)}, bf16[4,512,512]{2,1,0:T(8,128)(2,1)S(1)}, u32[]{:S(2)}, u32[]{:S(2)}) collective-permute-start(bf16[4,512,512]{2,1,0:T(8,128)(2,1)S(1)} %shard_map.51.refs_4_), channel_id=1, source_target_pairs={{0,16},{16,0},{1,17},{17,1},{2,18},{18,2},{3,19},{19,3},{4,20},{20... | collective-permute-start | bytes 6291464 | tf_op jit(solution)/shard_map/ppermute | solution.py:62
  21.7 28.9 %collective-permute-start.10 = (bf16[4,512,512]{2,1,0:T(8,128)(2,1)S(1)}, bf16[4,512,512]{2,1,0:T(8,128)(2,1)}, u32[]{:S(2)}, u32[]{:S(2)}) collective-permute-start(bf16[4,512,512]{2,1,0:T(8,128)(2,1)S(1)} %shard_map.51.refs_4_), channel_id=1, source_target_pairs={{0,12},{1,13},{2,14},{3,15},{4,0},{5,1},{6,2},{7,3},{8,4},{9,5},{1... | collective-permute-start | bytes 6291464 | tf_op jit(solution)/shard_map/ppermute | solution.py:46
  24.8 31.0 %collective-permute-start.9 = (bf16[4,512,512]{2,1,0:T(8,128)(2,1)S(1)}, bf16[4,512,512]{2,1,0:T(8,128)(2,1)}, u32[]{:S(2)}, u32[]{:S(2)}) collective-permute-start(bf16[4,512,512]{2,1,0:T(8,128)(2,1)S(1)} %shard_map.51.refs_4_), channel_id=1, source_target_pairs={{0,4},{1,5},{2,6},{3,7},{4,8},{5,9},{6,10},{7,11},{8,12},{9,13},{1... | collective-permute-start | bytes 6291464 | tf_op jit(solution)/shard_map/ppermute | solution.py:46
  35.9 13.4 %collective-permute-start.5 = (s32[272]{0:T(512)S(1)}, s32[272]{0:T(512)S(1)}, u32[]{:S(2)}, u32[]{:S(2)}) collective-permute-start(s32[272]{0:T(512)S(1)} %collective-permute-done.4.refs_0_), channel_id=1, source_target_pairs={{0,1},{1,2},{2,3},{3,0},{16,19},{17,16},{18,17},{19,18},{4,5},{5,6... | collective-permute-start | bytes 3272 | tf_op jit(solution)/shard_map/ppermute | solution.py:54
  48.8 28.1 %collective-permute-start.2 = (bf16[256,4096]{1,0:T(8,128)(2,1)}, bf16[256,4096]{1,0:T(8,128)(2,1)}, u32[]{:S(2)}, u32[]{:S(2)}) collective-permute-start(bf16[256,4096]{1,0:T(8,128)(2,1)} %shard_map.47.refs_1_), channel_id=1, source_target_pairs={{0,1},{1,2},{2,3},{3,0},{16,19},{17,16},{18,17},{19,18},{4,5},{5,6... | collective-permute-start | bytes 6291464 | tf_op jit(solution)/shard_map/ppermute | solution.py:54
  49.3 1.3 %copy-start.1 = (bf16[4,512,512]{2,1,0:T(8,128)(2,1)}, bf16[4,512,512]{2,1,0:T(8,128)(2,1)S(1)}, u32[]{:S(2)}) copy-start(bf16[4,512,512]{2,1,0:T(8,128)(2,1)S(1)} %collective-permute-done.11.refs_0_.refs_9_) | copy-start | bytes 6291460
  52.7 15.7 %collective-permute-start.13 = (bf16[2,512,512]{2,1,0:T(8,128)(2,1)}, bf16[2,512,512]{2,1,0:T(8,128)(2,1)S(1)}, u32[]{:S(2)}, u32[]{:S(2)}) collective-permute-start(bf16[2,512,512]{2,1,0:T(8,128)(2,1)} %shard_map.54), channel_id=1, source_target_pairs={{0,12},{1,13},{2,14},{3,15},{4,0},{5,1},{6,2},{7,3},{8,4},{9,5},{1... | collective-permute-start | bytes 3145736 | tf_op jit(solution)/shard_map/ppermute | solution.py:46
  57.9 16.3 %collective-permute-start.12 = (bf16[2,512,512]{2,1,0:T(8,128)(2,1)}, bf16[2,512,512]{2,1,0:T(8,128)(2,1)S(1)}, u32[]{:S(2)}, u32[]{:S(2)}) collective-permute-start(bf16[2,512,512]{2,1,0:T(8,128)(2,1)} %shard_map.53), channel_id=1, source_target_pairs={{0,4},{1,5},{2,6},{3,7},{4,8},{5,9},{6,10},{7,11},{8,12},{9,13},{1... | collective-permute-start | bytes 3145736 | tf_op jit(solution)/shard_map/ppermute | solution.py:46
  58.0 19.1 %collective-permute-start.15 = (bf16[4,512,512]{2,1,0:T(8,128)(2,1)}, bf16[4,512,512]{2,1,0:T(8,128)(2,1)}, u32[]{:S(2)}, u32[]{:S(2)}) collective-permute-start(bf16[4,512,512]{2,1,0:T(8,128)(2,1)} %collective-permute-done.10.ref.refs_6_), channel_id=1, source_target_pairs={{0,16},{16,0},{1,17},{17,1},{2,18},{18,2},{3,19},{19,3},{4,20},{20... | collective-permute-start | bytes 6291464 | tf_op jit(solution)/shard_map/ppermute | solution.py:62
  61.9 15.1 %collective-permute-start.14 = (bf16[4,512,512]{2,1,0:T(8,128)(2,1)}, bf16[4,512,512]{2,1,0:T(8,128)(2,1)}, u32[]{:S(2)}, u32[]{:S(2)}) collective-permute-start(bf16[4,512,512]{2,1,0:T(8,128)(2,1)} %collective-permute-done.9.ref.refs_5_), channel_id=1, source_target_pairs={{0,16},{16,0},{1,17},{17,1},{2,18},{18,2},{3,19},{19,3},{4,20},{20... | collective-permute-start | bytes 6291464 | tf_op jit(solution)/shard_map/ppermute | solution.py:62
  68.5 8.6 %collective-permute-start.17 = (bf16[2,512,512]{2,1,0:T(8,128)(2,1)S(1)}, bf16[2,512,512]{2,1,0:T(8,128)(2,1)S(1)}, u32[]{:S(2)}, u32[]{:S(2)}) collective-permute-start(bf16[2,512,512]{2,1,0:T(8,128)(2,1)S(1)} %collective-permute-done.13.refs_8_), channel_id=1, source_target_pairs={{0,16},{16,0},{1,17},{17,1},{2,18},{18,2},{3,19},{19,3},{4,20},{20... | collective-permute-start | bytes 3145736 | tf_op jit(solution)/shard_map/ppermute | solution.py:62
  74.2 5.0 %collective-permute-start.16 = (bf16[2,512,512]{2,1,0:T(8,128)(2,1)S(1)}, bf16[2,512,512]{2,1,0:T(8,128)(2,1)S(1)}, u32[]{:S(2)}, u32[]{:S(2)}) collective-permute-start(bf16[2,512,512]{2,1,0:T(8,128)(2,1)S(1)} %collective-permute-done.12.refs_7_), channel_id=1, source_target_pairs={{0,16},{16,0},{1,17},{17,1},{2,18},{18,2},{3,19},{19,3},{4,20},{20... | collective-permute-start | bytes 3145736 | tf_op jit(solution)/shard_map/ppermute | solution.py:62
  96.8 3.7 %collective-permute-start.18 = (f32[3,256]{1,0:T(4,128)S(1)}, f32[3,256]{1,0:T(4,128)S(1)}, u32[]{:S(2)}, u32[]{:S(2)}) collective-permute-start(f32[3,256]{1,0:T(4,128)S(1)} %get-tuple-element.10), channel_id=1, source_target_pairs={{0,3},{1,0},{2,1},{3,2},{16,17},{17,18},{18,19},{19,16},{4,7},{5,4... | collective-permute-start | bytes 9224 | tf_op jit(solution)/shard_map/ppermute | solution.py:54
  97.5 4.8 %collective-permute-start.19 = (f32[3,256]{1,0:T(4,128)S(1)}, f32[3,256]{1,0:T(4,128)S(1)}, u32[]{:S(2)}, u32[]{:S(2)}) collective-permute-start(f32[3,256]{1,0:T(4,128)S(1)} %get-tuple-element.11), channel_id=1, source_target_pairs={{0,1},{1,2},{2,3},{3,0},{16,19},{17,16},{18,17},{19,18},{4,5},{5,6... | collective-permute-start | bytes 9224 | tf_op jit(solution)/shard_map/ppermute | solution.py:54
  98.9 5.1 %collective-permute-start.20 = (f32[3,256]{1,0:T(4,128)S(1)}, f32[3,256]{1,0:T(4,128)S(1)}, u32[]{:S(2)}, u32[]{:S(2)}) collective-permute-start(f32[3,256]{1,0:T(4,128)S(1)} %get-tuple-element.12), channel_id=1, source_target_pairs={{0,2},{1,3},{2,0},{3,1},{16,18},{17,19},{18,16},{19,17},{4,6},{5,7... | collective-permute-start | bytes 9224 | tf_op jit(solution)/shard_map/ppermute | solution.py:54
